TPU v7x, 512 devices: a whole 4x4x16 slice. The times are simulated.
512 devices in a mesh: leaf: 512 (over x, z, y, core).
Axes of the slice: x: 4, y: 4, z: 16, core: 2. Of those that a mesh axis runs over, the one named last changes fastest.
Arguments:
- rhs: float32 [262144, 512], P('leaf'), may hold values from -6 to 6
- leaf_inverse: float32 [262144, 512], P('leaf'), may hold values from -0.25 to 0.25
- basis: float32 [262144, 576], P('leaf'), may hold values from -0.25 to 0.25
- caps: float32 [512, 9, 128, 128], P('leaf'), as said below
Outputs:
- solution: float32 [262144, 512], P('leaf')
Inputs may be any that keep to these rules, and one draw needn't show every extreme that they name: caps[d, l] is equal for all leaves d with the same d // 2 ** (l + 1).
All inputs are finite; a program needn't handle non-finite values.
Results may differ from a plain program's by a relative error of at most 0.00014.
Values sent between devices are 32-bit elements; how exact they have to be, the bound alone decides.
No kernel may reach another device: no remote copies, remote signals or barrier semaphores. Data moves between devices by JAX's collectives and lax.ppermute only.
A program may use at most 64 MiB of HBM per device.

v0:
```python
import functools

import jax
import jax.numpy as jnp
from jax import lax
from jax.experimental import pallas as pl
from jax.experimental.pallas import tpu as pltpu
from jax.sharding import PartitionSpec as P

HIGHEST = lax.Precision.HIGHEST
F32 = jnp.float32
BF16 = jnp.bfloat16
RANK = 64
LEVELS = 9
PARTNER = (1, 2, 6, 8, 16, 32, 96, 128, 384)
NN, NT = ((1,), (0,)), ((1,), (1,))


def bits():
    d = lax.axis_index("leaf")
    core, y_low, y_high = d & 1, d >> 1 & 1, d >> 2 & 1
    return d, core, y_low ^ y_high, y_high


def sent(array, mask):
    count = lax.axis_size("leaf")
    return lax.ppermute(array, "leaf", [(i, i ^ mask) for i in range(count)])


def call(body, outs, *args, tokens=(), flops=0, grant=6):
    vmem = pl.BlockSpec(memory_space=pltpu.VMEM)
    shapes = [jax.ShapeDtypeStruct(o[0], o[1]) if isinstance(o[0], tuple) else
              jax.ShapeDtypeStruct(o, F32) for o in outs]
    count, after = len(args), len(args) + len(tokens)

    def kernel(*refs):
        body(*refs[:count], *refs[after:])

    moved = sum(a.size * a.dtype.itemsize for a in args)
    return pl.pallas_call(
        kernel,
        out_shape=shapes,
        in_specs=[vmem] * after,
        out_specs=[vmem] * len(outs),
        compiler_params=pltpu.CompilerParams(vmem_limit_bytes=grant * 2**20),
        cost_estimate=pl.CostEstimate(flops=flops, bytes_accessed=moved, transcendentals=0),
    )(*args, *tokens)


def mm(a, b, dims):
    return lax.dot_general(a, b, (dims, ((), ())), preferred_element_type=F32)


def split(x):
    high = x.astype(BF16)
    return high, (x - high.astype(F32)).astype(BF16)


def mm3(a, b, dims):
    return mm(a[0], b[0], dims) + (mm(a[0], b[1], dims) + mm(a[1], b[0], dims))


def small(a, b, dims):
    return lax.dot_general(a, b, (dims, ((), ())), precision=HIGHEST, preferred_element_type=F32)


def side(*parts):
    return jnp.concatenate(parts, axis=1)


def stack(*parts):
    return jnp.concatenate(parts, axis=0)


def either(flag, if_zero, if_one):
    return jnp.where(flag == 0, if_zero, if_one)


def folded(x):
    full = x.shape[1] // 128
    parts = [x[:, 128 * i : 128 * (i + 1)] for i in range(full)]
    last = x[:, 128 * full :]
    return stack(*parts, side(last[:32], last[32:]))


def unfolded(x):
    full = x.shape[0] // 64
    parts = [x[64 * i : 64 * (i + 1)] for i in range(full)]
    last = x[64 * full :]
    return side(*parts, stack(last[:, :64], last[:, 64:]))


def gram_kernel(basis_ref, high_ref, low_ref, send_ref, keep_ref):
    _, core, _, _ = bits()
    for level in range(LEVELS):
        top = (LEVELS - 1 - level) * RANK
        high, low = split(basis_ref[level * RANK : (level + 1) * RANK, :])
        high_ref[top : top + RANK, :] = high
        low_ref[top : top + RANK, :] = low

    def rows(top, bottom):
        return high_ref[top:bottom, :], low_ref[top:bottom, :]

    a = mm3(rows(320, 576), rows(0, 512), NT)
    b = mm3(rows(64, 320), rows(0, 256), NT)
    row3, row4, row5, row6, row7 = a[:64], b[192:], b[128:192], b[64:128], b[:64]
    first = side(
        row4[:, :128], side(row5[:, :64], row6[:, :64]), side(row7[:, :64], row3[:, 256:320]),
        row3[:, :128],
    )
    second = side(
        row4[:, 128:], side(row5[:, 64:128], row6[:, 64:128]), row5[:, 128:256], row3[:, 128:256]
    )
    send_ref[:192, :] = a[64:]
    keep_ref[:192, :] = a[64:]
    send_ref[192:, :] = either(core, second, first)
    keep_ref[192:, :] = either(core, first, second)


def gram_core_kernel(keep_ref, got_ref, out_ref):
    out_ref[:, :512] = keep_ref[192:, :] + got_ref[192:, :]
    out_ref[:, 512:896] = keep_ref[:64, :384] + got_ref[:64, :384]
    out_ref[:, 896:] = keep_ref[64:128, :] + got_ref[64:128, :]


def gram_add_kernel(own_ref, got_ref, out_ref):
    lanes = out_ref.shape[1]
    out_ref[...] = own_ref[:, :lanes] + got_ref[:, :lanes]


def gram_level_kernel(level, own_ref, got_ref, swap_ref, next_ref=None, send_ref=None):
    _, core, _, _ = bits()
    own, other = own_ref[...], got_ref[...]
    if level > 3:
        other = unfolded(other)
    total = own + other
    if level == 3:
        swap_ref[:, :256] = side(own[:, 384:], other[:, 384:])
        swap_ref[:, 256:] = side(own[:, 320:384], other[:, 320:384])
        rest = total[:, :320]
    elif level == 4:
        swap_ref[...] = folded(side(own[:, :128], other[:, :128], total[:, 128:192]))
        rest = total[:, 128:]
    else:
        swap_ref[:, :128] = side(other[:, :64], either(core, total[:, 128:], other[:, 128:]))
        swap_ref[:, 128:] = side(total[:, 64:128], own[:, 128:])
    if level < 5:
        next_ref[...] = rest
        send_ref[...] = folded(rest)


GRAM_OUTS = {
    3: [(64, 384), (64, 320), (160, 128)],
    4: [(160, 128), (64, 192), (96, 128)],
    5: [(64, 256)],
}


def solve_kernel(theirs, rhs_ref, inverse_ref, high_ref, low_ref, iterate_ref, terms_ref):
    _, core, _, _ = bits()
    half = 1 - core if theirs else core
    columns = rhs_ref[:, pl.ds(pl.multiple_of(half * 256, 256), 256)]
    iterate = mm3(split(inverse_ref[...]), split(columns), NN)
    iterate_ref[...] = iterate
    terms_ref[:, :576] = mm3(split(iterate.T), (high_ref[...], low_ref[...]), NT)
    terms_ref[:, 576:] = jnp.zeros((256, 64), F32)


def caps_kernel(caps_ref, out_ref):
    d, _, _, _ = bits()
    for level in range(LEVELS):
        cap = caps_ref[level]
        turned = stack(cap[RANK:], cap[:RANK])
        turned = side(turned[:, RANK:], turned[:, :RANK])
        out_ref[level] = either(d >> level & 1, cap, turned)


def basis_kernel(basis_ref, high_ref, low_ref):
    high_ref[...], low_ref[...] = split(basis_ref[...].T)


def solved(own, other, cap):
    keep = own.shape[1] - RANK
    return small(side(own[:, keep:], other[:, keep:]), cap, NT)


def rest_of(own, other, both, gram_own, gram_other):
    keep = own.shape[1] - RANK
    return own[:, :keep] + other[:, :keep] - small(both, stack(gram_own, gram_other), NN)


def level0_kernel(own_ref, got_ref, keep_ref, gram_ref, caps_ref, both_ref, send_ref, next_ref):
    _, _, part, _ = bits()
    own, other = own_ref[:, :576], got_ref[:, :576]
    both = solved(own, other, caps_ref[0])
    both_ref[...] = both
    rest = rest_of(own, other, both, keep_ref[128:192, :], gram_ref[128:192, :])
    send_ref[...] = either(part, rest[128:], rest[:128])
    next_ref[...] = either(part, rest[:128], rest[128:])


def level1_kernel(own_ref, got_ref, low_ref, low_got_ref, caps_ref, both_ref, send_ref, next_ref):
    _, _, _, y_high = bits()
    own, other = own_ref[...], got_ref[...]
    both = solved(own, other, caps_ref[1])
    both_ref[...] = both
    rest = rest_of(own, other, both, low_ref[:, 896:1344], low_got_ref[:, 896:1344])
    send_ref[:, :448] = either(y_high, rest[64:], rest[:64])
    next_ref[:, :448] = either(y_high, rest[:64], rest[64:])
    send_ref[:, 448:] = jnp.zeros((64, 64), F32)
    next_ref[:, 448:] = jnp.zeros((64, 64), F32)


def level2_kernel(own_ref, got_ref, low_ref, low_got_ref, caps_ref, both_ref, next_ref):
    own, other = own_ref[:, :448], got_ref[:, :448]
    both = solved(own, other, caps_ref[2])
    both_ref[...] = both
    next_ref[...] = rest_of(own, other, both, low_ref[:, 512:896], low_got_ref[:, 512:896])


def level3_kernel(own_ref, got_ref, swap_ref, swap_got_ref, caps_ref, both_ref, next_ref,
                  send_ref):
    _, core, _, _ = bits()
    own, other = own_ref[...], got_ref[...]
    both = solved(own, other, caps_ref[3])
    both_ref[...] = both
    mine, got = swap_ref[...], swap_got_ref[...]
    a, b = either(core, mine, got), either(core, got, mine)
    row_own = side(a[:, :128], b[:, :128], a[:, 256:320])
    row_other = side(a[:, 128:256], b[:, 128:256], a[:, 320:384])
    rest = rest_of(own, other, both, row_own, row_other)
    next_ref[...] = rest
    send_ref[...] = folded(rest)


def level4_kernel(own_ref, got_ref, swap_ref, swap_got_ref, caps_ref, both_ref, next_ref):
    _, core, _, _ = bits()
    own, other = own_ref[...], unfolded(got_ref[...])
    both = solved(own, other, caps_ref[4])
    both_ref[...] = both
    mine, got = unfolded(swap_ref[...]), unfolded(swap_got_ref[...])
    a, b = either(core, mine, got), either(core, got, mine)
    row_own = side(a[:, :128], b[:, :128])
    row_other = side(a[:, 128:256], b[:, 128:256])
    next_ref[...] = rest_of(own, other, both, row_own, row_other)


def level5_kernel(own_ref, got_ref, swap4_ref, swap4_got_ref, swap_ref, swap_got_ref, caps_ref,
                  both2_ref, both3_ref, both4_ref, both_ref, next_ref, down_ref):
    down_ref[:, :128] = side(both2_ref[:, RANK:], both3_ref[:, :RANK])
    down_ref[:, 128:] = both4_ref[...]
    _, core, _, _ = bits()
    own, other = own_ref[...], got_ref[...]
    both = solved(own, other, caps_ref[5])
    both_ref[...] = both
    mine, got = unfolded(swap4_ref[...]), unfolded(swap4_got_ref[...])
    a4, b4 = either(core, mine, got), either(core, got, mine)
    mine, got = swap_ref[...], swap_got_ref[...]
    a, b = either(core, mine, got), either(core, got, mine)
    row_own = side(a4[:, 256:320], b4[:, 256:320], b[:, 192:])
    row_other = side(a[:, :64], b[:, :128])
    rest = rest_of(own, other, both, row_own, row_other)
    next_ref[...] = side(rest, a[:, 128:192], b[:, 128:192], a[:, 64:128])


def level6_kernel(own_ref, got_ref, caps_ref, down_mine_ref, down_got_ref, both2_ref, both1_ref,
                  both_ref, next_ref, down_ref):
    _, _, _, y_high = bits()
    mine = side(both2_ref[:, :RANK], down_mine_ref[:, RANK:192])
    theirs = down_got_ref[:, :192]
    rows = either(y_high, stack(mine, theirs), stack(theirs, mine))
    down_ref[...] = side(both1_ref[:, RANK:], rows)
    own, other = own_ref[:, :192], got_ref[:, :192]
    both = solved(own, other, caps_ref[6])
    both_ref[...] = both
    next_ref[:, :128] = rest_of(own, other, both, own_ref[:, 192:320], got_ref[:, 192:320])
    gram7 = own_ref[:, 320:] + got_ref[:, 320:]
    next_ref[:, 128:] = side(gram7, gram7)


def level7_kernel(own_ref, got_ref, caps_ref, both_ref, next_ref):
    own, other = own_ref[:, :128], got_ref[:, :128]
    both = solved(own, other, caps_ref[7])
    both_ref[...] = both
    rest = rest_of(own, other, both, own_ref[:, 128:192], got_ref[:, 128:192])
    next_ref[...] = side(rest, jnp.zeros((64, RANK), F32))


def level8_kernel(own_ref, got_ref, both5_ref, both6_ref, both7_ref, caps_ref, down_mine_ref,
                  down_got_ref, both1_ref, both0_ref, out_ref, down_send_ref, down_own_ref):
    _, _, part, _ = bits()
    both = solved(own_ref[:, :RANK], got_ref[:, :RANK], caps_ref[8])
    out_ref[:, :128] = side(both5_ref[:, :RANK], both6_ref[:, :RANK])
    out_ref[:, 128:] = side(both7_ref[:, :RANK], both[:, :RANK])
    mine = side(both1_ref[:, :RANK], down_mine_ref[:, RANK:])
    theirs = down_got_ref[...]
    rows = either(part, stack(mine, theirs), stack(theirs, mine))
    down_send_ref[:, :320] = side(both0_ref[:, RANK:], rows)
    down_own_ref[:, :320] = side(both0_ref[:, :RANK], rows)
    down_send_ref[:, 320:] = jnp.zeros((256, 64), F32)
    down_own_ref[:, 320:] = jnp.zeros((256, 64), F32)


def place(shard):
    core, part, y_high = shard >> 2, shard >> 1 & 1, shard & 1
    return y_high << 2 | (part ^ y_high) << 1 | core


def final_kernel(theirs_ref, mine_ref, got_ref, own_ref, all_ref, high_ref, low_ref, out_ref):
    _, core, _, _ = bits()
    factors = (high_ref[...], low_ref[...])
    last = [all_ref[place(shard)] for shard in range(8)]
    first, second = stack(*last[:4]), stack(*last[4:])
    own = side(own_ref[:, :320], either(core, first, second))
    other = side(got_ref[:, :320], either(core, second, first))
    own_out = mine_ref[...] - mm3(factors, split(own), NT)
    other_out = theirs_ref[...] - mm3(factors, split(other), NT)
    out_ref[:, :256] = either(core, own_out, other_out)
    out_ref[:, 256:] = either(core, other_out, own_out)


def local(rhs, leaf_inverse, basis, caps):
    partial = functools.partial
    high, low, gram_send, gram_keep = call(
        gram_kernel, [((576, 512), BF16), ((576, 512), BF16), (256, 512), (256, 512)],
        basis.T, flops=6 * 100_000_000, grant=12,
    )
    gram_got = sent(gram_send, PARTNER[0])
    iterate_theirs, terms_theirs = call(
        partial(solve_kernel, True), [(512, 256), (256, 640)],
        rhs, leaf_inverse, high, low, flops=6 * 142_000_000, grant=12,
    )
    terms_got = sent(terms_theirs, PARTNER[0])
    gram1, = call(gram_core_kernel, [(64, 1408)], gram_keep, gram_got, tokens=(terms_theirs,))
    gram1_got = sent(gram1, PARTNER[1])
    iterate_own, terms = call(
        partial(solve_kernel, False), [(512, 256), (256, 640)],
        rhs, leaf_inverse, high, low, tokens=(gram1,), flops=6 * 142_000_000, grant=12,
    )
    caps, = call(caps_kernel, [(9, 128, 128)], caps[0])
    both0, send1, state = call(
        level0_kernel, [(256, 128), (128, 512), (128, 512)],
        terms, terms_got, gram_keep, gram_got, caps,
    )
    got = sent(send1, PARTNER[1])
    gram2, = call(gram_add_kernel, [(64, 896)], gram1, gram1_got, tokens=(send1,))
    gram2_got = sent(gram2, PARTNER[2])
    both1, send2, state = call(
        level1_kernel, [(128, 128), (64, 512), (64, 512)], state, got, gram1, gram1_got, caps
    )
    got = sent(send2, PARTNER[2])
    gram, = call(gram_add_kernel, [(64, 512)], gram2, gram2_got, tokens=(send2,))
    grams = gram, sent(gram, PARTNER[3])
    both2, state = call(
        level2_kernel, [(64, 128), (64, 384)], state, got, gram2, gram2_got, caps
    )
    basis_high, basis_low = call(
        basis_kernel, [((512, 576), BF16), ((512, 576), BF16)], basis.T, tokens=(state,)
    )
    got = sent(state, PARTNER[3])
    swap, gram, going = call(
        partial(gram_level_kernel, 3), GRAM_OUTS[3], *grams, tokens=(state,)
    )
    swap_got = sent(swap, PARTNER[0])
    grams = gram, sent(going, PARTNER[4])
    both3, state, going = call(
        level3_kernel, [(64, 128), (64, 320), (160, 128)], state, got, swap, swap_got, caps
    )
    got = sent(going, PARTNER[4])
    swap4, gram, going = call(
        partial(gram_level_kernel, 4), GRAM_OUTS[4], *grams, tokens=(state,)
    )
    swap4_got = sent(swap4, PARTNER[0])
    grams = gram, sent(going, PARTNER[5])
    both4, state = call(
        level4_kernel, [(64, 128), (64, 256)], state, got, swap4, swap4_got, caps,
        tokens=(basis_low,),
    )
    got = sent(state, PARTNER[5])
    swap, = call(partial(gram_level_kernel, 5), GRAM_OUTS[5], *grams, tokens=(state,))
    swap_got = sent(swap, PARTNER[0])
    both5, state, down = call(
        level5_kernel, [(64, 128), (64, 384), (64, 256)],
        state, got, swap4, swap4_got, swap, swap_got, caps, both2, both3, both4,
    )
    got = sent(state, PARTNER[6])
    down_got = sent(down, PARTNER[2])
    both6, state, down = call(
        level6_kernel, [(64, 128), (64, 256), (128, 256)],
        state, got, caps, down, down_got, both2, both1,
    )
    got = sent(state, PARTNER[7])
    down_got = sent(down, PARTNER[1])
    both7, state = call(level7_kernel, [(64, 128), (64, 128)], state, got, caps)
    got = sent(state, PARTNER[8])
    last, down_send, down_own = call(
        level8_kernel, [(64, 256), (256, 384), (256, 384)],
        state, got, both5, both6, both7, caps, down, down_got, both1, both0,
    )
    down_got = sent(down_send, PARTNER[0])
    octets = [list(range(n, n + 8)) for n in range(0, 512, 8)]
    gathered = lax.all_gather(last, "leaf", axis_index_groups=octets)
    out, = call(
        final_kernel, [(512, 512)], iterate_theirs, iterate_own, down_got, down_own, gathered,
        basis_high, basis_low, flops=12 * 75_000_000, grant=16,
    )
    return out


def solution(mesh):
    return jax.shard_map(
        local,
        mesh=mesh,
        in_specs=(P("leaf", None), P("leaf", None), P("leaf", None), P("leaf", None, None, None)),
        out_specs=P("leaf", None),
        check_vma=False,
    )
```

profile of v0, /device:TPU:1, one launch (start us, length us, event | category | flops | bytes accessed | tf_op | source)
XLA Modules:
  0.0 127.2 jit_solution(107321940102365056)
XLA Ops:
  0.0 1.4 %copy-done.2 = f32[512,576]{0,1:T(8,128)S(1)} copy-done((f32[512,576]{0,1:T(8,128)S(1)}, f32[512,576]{0,1:T(8,128)}, u32[]{:S(2)}) %copy-start.2) | copy-done | bytes 1179672
  1.4 0.9 shard_map.46
  2.3 8.8 %collective-permute-start = (f32[256,512]{1,0:T(8,128)S(1)}, f32[256,512]{1,0:T(8,128)S(1)}, u32[]{:S(2)}, u32[]{:S(2)}) collective-permute-start(f32[256,512]{1,0:T(8,128)S(1)} %get-tuple-element.49), channel_id=1, source_target_pairs={{0,1},{1,0},{2,3},{3,2},{4,5},{5,4},{6,7},{7,6},{8,9},{9,8},{10,11... | collective-permute-start | bytes 1572872 | tf_op jit(solution)/shard_map/ppermute | solution.py:27
  11.1 2.1 %shard_map.47 = (f32[512,256]{1,0:T(8,128)S(1)}, f32[256,640]{1,0:T(8,128)S(1)}) custom-call(f32[512,512]{1,0:T(8,128)S(1)} %copy-done, f32[512,512]{1,0:T(8,128)S(1)} %copy-done.1, bf16[576,512]{1,0:T(8,128)(2,1)S(1)} %get-tuple-element.45.refs_2_, bf16[576,512]{1,0:T(8,128)(2,1)S(1)} %get-tuple-element.46.refs_3_), custom_call_target="tpu_custom_call" | custom-call | flops 852000000 | bytes 3276800 | tf_op jit(solution)/shard_map/pallas_call | solution.py:40
  13.3 0.0 copy-start.3
  13.3 2.1 %collective-permute-start.1 = (f32[256,640]{1,0:T(8,128)S(1)}, f32[256,640]{1,0:T(8,128)S(1)}, u32[]{:S(2)}, u32[]{:S(2)}) collective-permute-start(f32[256,640]{1,0:T(8,128)S(1)} %get-tuple-element.50.refs_2_), channel_id=1, source_target_pairs={{0,1},{1,0},{2,3},{3,2},{4,5},{5,4},{6,7},{7,6},{8,9},{9,8},{10,11... | collective-permute-start | bytes 1966088 | tf_op jit(solution)/shard_map/ppermute | solution.py:27
  15.4 0.0 collective-permute-done.refs_1_.refs_3_
  15.4 1.9 %collective-permute-start.3 = (f32[64,1408]{1,0:T(8,128)S(1)}, f32[64,1408]{1,0:T(8,128)S(1)}, u32[]{:S(2)}, u32[]{:S(2)}) collective-permute-start(f32[64,1408]{1,0:T(8,128)S(1)} %shard_map.48.refs_4_.refs_2_.refs_0_), channel_id=1, source_target_pairs={{0,2},{1,3},{2,0},{3,1},{4,6},{5,7},{6,4},{7,5},{8,10},{9,11},{10,... | collective-permute-start | bytes 1081352 | tf_op jit(solution)/shard_map/ppermute | solution.py:27
  17.3 0.0 copy-done.3
  17.4 0.2 shard_map.50.refs_4_.refs_6_.refs_2_.refs_5_
  17.6 2.2 %shard_map.49 = (f32[512,256]{1,0:T(8,128)S(1)}, f32[256,640]{1,0:T(8,128)S(1)}) custom-call(f32[512,512]{1,0:T(8,128)S(1)} %copy-done, f32[512,512]{1,0:T(8,128)S(1)} %copy-done.1, bf16[576,512]{1,0:T(8,128)(2,1)S(1)} %get-tuple-element.45.refs_2_, bf16[576,512]{1,0:T(8,128)(2,1)S(1)} %get-tuple-element.46.refs_3_, ...), custom_call_target="tpu_custom_call" | custom-call | flops 852000000 | bytes 3276800 | tf_op jit(solution)/shard_map/pallas_call | solution.py:40
  19.7 0.0 collective-permute-done.1.refs_1_
  19.8 1.0 shard_map.51
  20.8 3.4 %collective-permute-start.2 = (f32[128,512]{1,0:T(8,128)S(1)}, f32[128,512]{1,0:T(8,128)S(1)}, u32[]{:S(2)}, u32[]{:S(2)}) collective-permute-start(f32[128,512]{1,0:T(8,128)S(1)} %get-tuple-element.54.refs_2_), channel_id=1, source_target_pairs={{0,2},{1,3},{2,0},{3,1},{4,6},{5,7},{6,4},{7,5},{8,10},{9,11},{10,... | collective-permute-start | bytes 786440 | tf_op jit(solution)/shard_map/ppermute | solution.py:27
  24.1 2.7 %collective-permute-done.3.refs_3_.refs_1_ = f32[64,1408]{1,0:T(8,128)S(1)} collective-permute-done((f32[64,1408]{1,0:T(8,128)S(1)}, f32[64,1408]{1,0:T(8,128)S(1)}, u32[]{:S(2)}, u32[]{:S(2)}) %collective-permute-start.3) | collective-permute-done | bytes 360480 | tf_op jit(solution)/shard_map/ppermute | solution.py:27
  26.8 1.9 %collective-permute-start.5 = (f32[64,896]{1,0:T(8,128)S(1)}, f32[64,896]{1,0:T(8,128)S(1)}, u32[]{:S(2)}, u32[]{:S(2)}) collective-permute-start(f32[64,896]{1,0:T(8,128)S(1)} %shard_map.53.refs_2_.refs_0_), channel_id=1, source_target_pairs={{0,6},{1,7},{2,4},{3,5},{4,2},{5,3},{6,0},{7,1},{8,14},{9,15},{10,... | collective-permute-start | bytes 688136 | tf_op jit(solution)/shard_map/ppermute | solution.py:27
  28.8 3.7 %collective-permute-done.2.refs_1_ = f32[128,512]{1,0:T(8,128)S(1)} collective-permute-done((f32[128,512]{1,0:T(8,128)S(1)}, f32[128,512]{1,0:T(8,128)S(1)}, u32[]{:S(2)}, u32[]{:S(2)}) %collective-permute-start.2) | collective-permute-done | bytes 262176 | tf_op jit(solution)/shard_map/ppermute | solution.py:27
  32.4 0.6 shard_map.52
  33.1 1.9 %collective-permute-start.4 = (f32[64,512]{1,0:T(8,128)S(1)}, f32[64,512]{1,0:T(8,128)S(1)}, u32[]{:S(2)}, u32[]{:S(2)}) collective-permute-start(f32[64,512]{1,0:T(8,128)S(1)} %get-tuple-element.56.refs_2_), channel_id=1, source_target_pairs={{0,6},{1,7},{2,4},{3,5},{4,2},{5,3},{6,0},{7,1},{8,14},{9,15},{10,... | collective-permute-start | bytes 393224 | tf_op jit(solution)/shard_map/ppermute | solution.py:27
  35.0 0.0 collective-permute-done.5.refs_3_.refs_1_
  35.0 1.9 %collective-permute-start.7 = (f32[64,512]{1,0:T(8,128)S(1)}, f32[64,512]{1,0:T(8,128)S(1)}, u32[]{:S(2)}, u32[]{:S(2)}) collective-permute-start(f32[64,512]{1,0:T(8,128)S(1)} %shard_map.55.refs_0_), channel_id=1, source_target_pairs={{0,8},{1,9},{2,10},{3,11},{4,12},{5,13},{6,14},{7,15},{8,0},{9,1},... | collective-permute-start | bytes 393224 | tf_op jit(solution)/shard_map/ppermute | solution.py:27
  37.0 3.0 %collective-permute-done.4.refs_1_ = f32[64,512]{1,0:T(8,128)S(1)} collective-permute-done((f32[64,512]{1,0:T(8,128)S(1)}, f32[64,512]{1,0:T(8,128)S(1)}, u32[]{:S(2)}, u32[]{:S(2)}) %collective-permute-start.4) | collective-permute-done | bytes 131104 | tf_op jit(solution)/shard_map/ppermute | solution.py:27
  40.0 0.7 shard_map.54
  40.7 1.9 %collective-permute-start.6 = (f32[64,384]{1,0:T(8,128)S(1)}, f32[64,384]{1,0:T(8,128)S(1)}, u32[]{:S(2)}, u32[]{:S(2)}) collective-permute-start(f32[64,384]{1,0:T(8,128)S(1)} %get-tuple-element.57.refs_2_.refs_0_.refs_1_), channel_id=1, source_target_pairs={{0,8},{1,9},{2,10},{3,11},{4,12},{5,13},{6,14},{7,15},{8,0},{9,1},... | collective-permute-start | bytes 294920 | tf_op jit(solution)/shard_map/ppermute | solution.py:27
  42.6 0.0 collective-permute-done.7.refs_1_
  42.6 0.1 shard_map.56
  42.7 4.4 %collective-permute-start.8 = (f32[64,384]{1,0:T(8,128)S(1)}, f32[64,384]{1,0:T(8,128)S(1)}, u32[]{:S(2)}, u32[]{:S(2)}) collective-permute-start(f32[64,384]{1,0:T(8,128)S(1)} %get-tuple-element.58.refs_2_), channel_id=1, source_target_pairs={{0,1},{1,0},{2,3},{3,2},{4,5},{5,4},{6,7},{7,6},{8,9},{9,8},{10,11... | collective-permute-start | bytes 294920 | tf_op jit(solution)/shard_map/ppermute | solution.py:27
  47.1 1.9 %collective-permute-start.10 = (f32[160,128]{1,0:T(8,128)S(1)}, f32[160,128]{1,0:T(8,128)S(1)}, u32[]{:S(2)}, u32[]{:S(2)}) collective-permute-start(f32[160,128]{1,0:T(8,128)S(1)} %get-tuple-element.62), channel_id=1, source_target_pairs={{0,16},{1,17},{2,18},{3,19},{4,20},{5,21},{6,22},{7,23},{8,24},{9,... | collective-permute-start | bytes 245768 | tf_op jit(solution)/shard_map/ppermute | solution.py:27
  49.0 0.0 collective-permute-done.6.refs_1_
  49.0 0.0 collective-permute-done.8.refs_3_
  49.1 0.7 shard_map.57
  49.8 4.3 %collective-permute-start.9 = (f32[160,128]{1,0:T(8,128)S(1)}, f32[160,128]{1,0:T(8,128)S(1)}, u32[]{:S(2)}, u32[]{:S(2)}) collective-permute-start(f32[160,128]{1,0:T(8,128)S(1)} %get-tuple-element.60), channel_id=1, source_target_pairs={{0,16},{1,17},{2,18},{3,19},{4,20},{5,21},{6,22},{7,23},{8,24},{9,... | collective-permute-start | bytes 245768 | tf_op jit(solution)/shard_map/ppermute | solution.py:27
  54.1 0.0 collective-permute-done.10.refs_1_
  54.1 0.1 shard_map.58
  54.2 4.5 %collective-permute-start.11 = (f32[160,128]{1,0:T(8,128)S(1)}, f32[160,128]{1,0:T(8,128)S(1)}, u32[]{:S(2)}, u32[]{:S(2)}) collective-permute-start(f32[160,128]{1,0:T(8,128)S(1)} %get-tuple-element.63.refs_2_), channel_id=1, source_target_pairs={{0,1},{1,0},{2,3},{3,2},{4,5},{5,4},{6,7},{7,6},{8,9},{9,8},{10,11... | collective-permute-start | bytes 245768 | tf_op jit(solution)/shard_map/ppermute | solution.py:27
  58.7 6.1 %collective-permute-start.13 = (f32[96,128]{1,0:T(8,128)S(1)}, f32[96,128]{1,0:T(8,128)S(1)}, u32[]{:S(2)}, u32[]{:S(2)}) collective-permute-start(f32[96,128]{1,0:T(8,128)S(1)} %get-tuple-element.67), channel_id=1, source_target_pairs={{0,32},{1,33},{2,34},{3,35},{4,36},{5,37},{6,38},{7,39},{8,40},{9,... | collective-permute-start | bytes 147464 | tf_op jit(solution)/shard_map/ppermute | solution.py:27
  64.8 0.4 shard_map.59
  65.2 0.0 collective-permute-done.9.refs_1_
  65.3 0.0 collective-permute-done.11.refs_3_
  65.3 0.6 shard_map.60
  65.8 3.1 %collective-permute-start.12 = (f32[64,256]{1,0:T(8,128)S(1)}, f32[64,256]{1,0:T(8,128)S(1)}, u32[]{:S(2)}, u32[]{:S(2)}) collective-permute-start(f32[64,256]{1,0:T(8,128)S(1)} %get-tuple-element.65.refs_2_.refs_0_), channel_id=1, source_target_pairs={{0,32},{1,33},{2,34},{3,35},{4,36},{5,37},{6,38},{7,39},{8,40},{9,... | collective-permute-start | bytes 196616 | tf_op jit(solution)/shard_map/ppermute | solution.py:27
  69.0 0.5 collective-permute-done.13.refs_1_
  69.4 0.1 shard_map.61.refs_4_
  69.6 2.5 %collective-permute-start.14 = (f32[64,256]{1,0:T(8,128)S(1)}, f32[64,256]{1,0:T(8,128)S(1)}, u32[]{:S(2)}, u32[]{:S(2)}) collective-permute-start(f32[64,256]{1,0:T(8,128)S(1)} %shard_map.61.refs_4_), channel_id=1, source_target_pairs={{0,1},{1,0},{2,3},{3,2},{4,5},{5,4},{6,7},{7,6},{8,9},{9,8},{10,11... | collective-permute-start | bytes 196616 | tf_op jit(solution)/shard_map/ppermute | solution.py:27
  72.1 6.0 %collective-permute-done.12.refs_1_ = f32[64,256]{1,0:T(8,128)S(1)} collective-permute-done((f32[64,256]{1,0:T(8,128)S(1)}, f32[64,256]{1,0:T(8,128)S(1)}, u32[]{:S(2)}, u32[]{:S(2)}) %collective-permute-start.12) | collective-permute-done | bytes 65568 | tf_op jit(solution)/shard_map/ppermute | solution.py:27
  78.1 0.0 collective-permute-done.14.refs_5_
  78.1 0.5 shard_map.62
  78.6 4.2 %collective-permute-start.15 = (f32[64,384]{1,0:T(8,128)S(1)}, f32[64,384]{1,0:T(8,128)S(1)}, u32[]{:S(2)}, u32[]{:S(2)}) collective-permute-start(f32[64,384]{1,0:T(8,128)S(1)} %get-tuple-element.71.refs_0_), channel_id=1, source_target_pairs={{0,96},{1,97},{2,98},{3,99},{4,100},{5,101},{6,102},{7,103},{8,104... | collective-permute-start | bytes 294920 | tf_op jit(solution)/shard_map/ppermute | solution.py:27
  82.8 4.3 %collective-permute-start.16 = (f32[64,256]{1,0:T(8,128)S(1)}, f32[64,256]{1,0:T(8,128)S(1)}, u32[]{:S(2)}, u32[]{:S(2)}) collective-permute-start(f32[64,256]{1,0:T(8,128)S(1)} %get-tuple-element.72.refs_3_), channel_id=1, source_target_pairs={{0,6},{1,7},{2,4},{3,5},{4,2},{5,3},{6,0},{7,1},{8,14},{9,15},{10,... | collective-permute-start | bytes 196616 | tf_op jit(solution)/shard_map/ppermute | solution.py:27
  87.2 2.2 %collective-permute-done.16.refs_4_ = f32[64,256]{1,0:T(8,128)S(1)} collective-permute-done((f32[64,256]{1,0:T(8,128)S(1)}, f32[64,256]{1,0:T(8,128)S(1)}, u32[]{:S(2)}, u32[]{:S(2)}) %collective-permute-start.16) | collective-permute-done | bytes 65568 | tf_op jit(solution)/shard_map/ppermute | solution.py:27
  89.3 0.0 collective-permute-done.15.refs_1_
  89.3 0.5 shard_map.63
  89.9 1.9 %collective-permute-start.19 = (f32[128,256]{1,0:T(8,128)S(1)}, f32[128,256]{1,0:T(8,128)S(1)}, u32[]{:S(2)}, u32[]{:S(2)}) collective-permute-start(f32[128,256]{1,0:T(8,128)S(1)} %get-tuple-element.79.refs_6_), channel_id=1, source_target_pairs={{0,2},{1,3},{2,0},{3,1},{4,6},{5,7},{6,4},{7,5},{8,10},{9,11},{10,... | collective-permute-start | bytes 393224 | tf_op jit(solution)/shard_map/ppermute | solution.py:27
  91.8 3.1 %collective-permute-start.17 = (f32[64,256]{1,0:T(8,128)S(1)}, f32[64,256]{1,0:T(8,128)S(1)}, u32[]{:S(2)}, u32[]{:S(2)}) collective-permute-start(f32[64,256]{1,0:T(8,128)S(1)} %get-tuple-element.74.refs_0_), channel_id=1, source_target_pairs={{0,128},{1,129},{2,130},{3,131},{4,132},{5,133},{6,134},{7,135},{8... | collective-permute-start | bytes 196616 | tf_op jit(solution)/shard_map/ppermute | solution.py:27
  94.9 1.9 %collective-permute-done.17.refs_1_ = f32[64,256]{1,0:T(8,128)S(1)} collective-permute-done((f32[64,256]{1,0:T(8,128)S(1)}, f32[64,256]{1,0:T(8,128)S(1)}, u32[]{:S(2)}, u32[]{:S(2)}) %collective-permute-start.17) | collective-permute-done | bytes 65568 | tf_op jit(solution)/shard_map/ppermute | solution.py:27
  96.8 0.5 shard_map.64
  97.3 4.4 %collective-permute-start.18 = (f32[64,128]{1,0:T(8,128)S(1)}, f32[64,128]{1,0:T(8,128)S(1)}, u32[]{:S(2)}, u32[]{:S(2)}) collective-permute-start(f32[64,128]{1,0:T(8,128)S(1)} %get-tuple-element.75.refs_0_), channel_id=1, source_target_pairs={{0,384},{1,385},{2,386},{3,387},{4,388},{5,389},{6,390},{7,391},{8... | collective-permute-start | bytes 98312 | tf_op jit(solution)/shard_map/ppermute | solution.py:27
  101.7 1.5 %collective-permute-done.18.refs_1_ = f32[64,128]{1,0:T(8,128)S(1)} collective-permute-done((f32[64,128]{1,0:T(8,128)S(1)}, f32[64,128]{1,0:T(8,128)S(1)}, u32[]{:S(2)}, u32[]{:S(2)}) %collective-permute-start.18) | collective-permute-done | bytes 32800 | tf_op jit(solution)/shard_map/ppermute | solution.py:27
  103.2 0.0 collective-permute-done.19.refs_7_
  103.2 0.4 shard_map.65
  103.6 6.7 %collective-permute-start.20 = (f32[256,384]{1,0:T(8,128)S(1)}, f32[256,384]{1,0:T(8,128)S(1)}, u32[]{:S(2)}, u32[]{:S(2)}) collective-permute-start(f32[256,384]{1,0:T(8,128)S(1)} %get-tuple-element.81), channel_id=1, source_target_pairs={{0,1},{1,0},{2,3},{3,2},{4,5},{5,4},{6,7},{7,6},{8,9},{9,8},{10,11... | collective-permute-start | bytes 1179656 | tf_op jit(solution)/shard_map/ppermute | solution.py:27
  110.3 14.5 %all-gather = f32[512,256]{1,0:T(8,128)S(1)} all-gather(f32[64,256]{1,0:T(8,128)S(1)} %get-tuple-element.83), channel_id=2, replica_groups={{0,1,2,3,4,5,6,7},{8,9,10,11,12,13,14,15},{16,17,18,19,20,21,22,23},{24..., dimensions={0}, use_global_device_ids=true | all-gather | bytes 589824 | tf_op jit(solution)/shard_map/all_gather | solution.py:402
  124.8 0.0 collective-permute-done.20.refs_2_
  124.8 2.4 %shard_map.66 = f32[512,512]{1,0:T(8,128)} custom-call(f32[512,256]{1,0:T(8,128)S(1)} %get-tuple-element.47.refs_0_, f32[512,256]{1,0:T(8,128)S(1)} %get-tuple-element.51.refs_1_, f32[256,384]{1,0:T(8,128)S(1)} %collective-permute-done.20.refs_2_, f32[256,384]{1,0:T(8,128)S(1)} %get-tuple-element.82.refs_3_, f32[8,64,256]{2,1,0:T(8,128)S(1)} %bitcast.3, ...), custom_call_target="tpu_custom_call" | custom-call | flops 900000000 | bytes 3538944 | tf_op jit(solution)/shard_map/pallas_call | solution.py:40
  (8 shorter events, 0.1 us)
Async XLA Ops:
  0.0 11.1 %copy-start = (f32[512,512]{1,0:T(8,128)S(1)}, f32[512,512]{1,0:T(8,128)}, u32[]{:S(2)}) copy-start(f32[512,512]{1,0:T(8,128)} %refs_0_.3) | copy-start | bytes 3145732
  0.0 11.1 %copy-start.1 = (f32[512,512]{1,0:T(8,128)S(1)}, f32[512,512]{1,0:T(8,128)}, u32[]{:S(2)}) copy-start(f32[512,512]{1,0:T(8,128)} %refs_1_.3) | copy-start | bytes 3145732
  0.0 1.4 %copy-start.2 = (f32[512,576]{0,1:T(8,128)S(1)}, f32[512,576]{0,1:T(8,128)}, u32[]{:S(2)}) copy-start(f32[512,576]{0,1:T(8,128)} %param.6) | copy-start | bytes 3538948
  2.3 13.1 %collective-permute-start = (f32[256,512]{1,0:T(8,128)S(1)}, f32[256,512]{1,0:T(8,128)S(1)}, u32[]{:S(2)}, u32[]{:S(2)}) collective-permute-start(f32[256,512]{1,0:T(8,128)S(1)} %get-tuple-element.49), channel_id=1, source_target_pairs={{0,1},{1,0},{2,3},{3,2},{4,5},{5,4},{6,7},{7,6},{8,9},{9,8},{10,11... | collective-permute-start | bytes 1572872 | tf_op jit(solution)/shard_map/ppermute | solution.py:27
  13.3 4.1 %copy-start.3 = (f32[1,9,128,128]{3,2,1,0:T(8,128)S(1)}, f32[1,9,128,128]{3,2,1,0:T(8,128)}, u32[]{:S(2)}) copy-start(f32[1,9,128,128]{3,2,1,0:T(8,128)} %param.7) | copy-start | bytes 1769476
  13.3 6.5 %collective-permute-start.1 = (f32[256,640]{1,0:T(8,128)S(1)}, f32[256,640]{1,0:T(8,128)S(1)}, u32[]{:S(2)}, u32[]{:S(2)}) collective-permute-start(f32[256,640]{1,0:T(8,128)S(1)} %get-tuple-element.50.refs_2_), channel_id=1, source_target_pairs={{0,1},{1,0},{2,3},{3,2},{4,5},{5,4},{6,7},{7,6},{8,9},{9,8},{10,11... | collective-permute-start | bytes 1966088 | tf_op jit(solution)/shard_map/ppermute | solution.py:27
  15.4 11.4 %collective-permute-start.3 = (f32[64,1408]{1,0:T(8,128)S(1)}, f32[64,1408]{1,0:T(8,128)S(1)}, u32[]{:S(2)}, u32[]{:S(2)}) collective-permute-start(f32[64,1408]{1,0:T(8,128)S(1)} %shard_map.48.refs_4_.refs_2_.refs_0_), channel_id=1, source_target_pairs={{0,2},{1,3},{2,0},{3,1},{4,6},{5,7},{6,4},{7,5},{8,10},{9,11},{10,... | collective-permute-start | bytes 1081352 | tf_op jit(solution)/shard_map/ppermute | solution.py:27
  20.8 11.6 %collective-permute-start.2 = (f32[128,512]{1,0:T(8,128)S(1)}, f32[128,512]{1,0:T(8,128)S(1)}, u32[]{:S(2)}, u32[]{:S(2)}) collective-permute-start(f32[128,512]{1,0:T(8,128)S(1)} %get-tuple-element.54.refs_2_), channel_id=1, source_target_pairs={{0,2},{1,3},{2,0},{3,1},{4,6},{5,7},{6,4},{7,5},{8,10},{9,11},{10,... | collective-permute-start | bytes 786440 | tf_op jit(solution)/shard_map/ppermute | solution.py:27
  26.8 8.2 %collective-permute-start.5 = (f32[64,896]{1,0:T(8,128)S(1)}, f32[64,896]{1,0:T(8,128)S(1)}, u32[]{:S(2)}, u32[]{:S(2)}) collective-permute-start(f32[64,896]{1,0:T(8,128)S(1)} %shard_map.53.refs_2_.refs_0_), channel_id=1, source_target_pairs={{0,6},{1,7},{2,4},{3,5},{4,2},{5,3},{6,0},{7,1},{8,14},{9,15},{10,... | collective-permute-start | bytes 688136 | tf_op jit(solution)/shard_map/ppermute | solution.py:27
  33.1 6.9 %collective-permute-start.4 = (f32[64,512]{1,0:T(8,128)S(1)}, f32[64,512]{1,0:T(8,128)S(1)}, u32[]{:S(2)}, u32[]{:S(2)}) collective-permute-start(f32[64,512]{1,0:T(8,128)S(1)} %get-tuple-element.56.refs_2_), channel_id=1, source_target_pairs={{0,6},{1,7},{2,4},{3,5},{4,2},{5,3},{6,0},{7,1},{8,14},{9,15},{10,... | collective-permute-start | bytes 393224 | tf_op jit(solution)/shard_map/ppermute | solution.py:27
  35.0 7.6 %collective-permute-start.7 = (f32[64,512]{1,0:T(8,128)S(1)}, f32[64,512]{1,0:T(8,128)S(1)}, u32[]{:S(2)}, u32[]{:S(2)}) collective-permute-start(f32[64,512]{1,0:T(8,128)S(1)} %shard_map.55.refs_0_), channel_id=1, source_target_pairs={{0,8},{1,9},{2,10},{3,11},{4,12},{5,13},{6,14},{7,15},{8,0},{9,1},... | collective-permute-start | bytes 393224 | tf_op jit(solution)/shard_map/ppermute | solution.py:27
  40.7 8.4 %collective-permute-start.6 = (f32[64,384]{1,0:T(8,128)S(1)}, f32[64,384]{1,0:T(8,128)S(1)}, u32[]{:S(2)}, u32[]{:S(2)}) collective-permute-start(f32[64,384]{1,0:T(8,128)S(1)} %get-tuple-element.57.refs_2_.refs_0_.refs_1_), channel_id=1, source_target_pairs={{0,8},{1,9},{2,10},{3,11},{4,12},{5,13},{6,14},{7,15},{8,0},{9,1},... | collective-permute-start | bytes 294920 | tf_op jit(solution)/shard_map/ppermute | solution.py:27
  42.7 6.4 %collective-permute-start.8 = (f32[64,384]{1,0:T(8,128)S(1)}, f32[64,384]{1,0:T(8,128)S(1)}, u32[]{:S(2)}, u32[]{:S(2)}) collective-permute-start(f32[64,384]{1,0:T(8,128)S(1)} %get-tuple-element.58.refs_2_), channel_id=1, source_target_pairs={{0,1},{1,0},{2,3},{3,2},{4,5},{5,4},{6,7},{7,6},{8,9},{9,8},{10,11... | collective-permute-start | bytes 294920 | tf_op jit(solution)/shard_map/ppermute | solution.py:27
  47.1 7.0 %collective-permute-start.10 = (f32[160,128]{1,0:T(8,128)S(1)}, f32[160,128]{1,0:T(8,128)S(1)}, u32[]{:S(2)}, u32[]{:S(2)}) collective-permute-start(f32[160,128]{1,0:T(8,128)S(1)} %get-tuple-element.62), channel_id=1, source_target_pairs={{0,16},{1,17},{2,18},{3,19},{4,20},{5,21},{6,22},{7,23},{8,24},{9,... | collective-permute-start | bytes 245768 | tf_op jit(solution)/shard_map/ppermute | solution.py:27
  49.8 15.4 %collective-permute-start.9 = (f32[160,128]{1,0:T(8,128)S(1)}, f32[160,128]{1,0:T(8,128)S(1)}, u32[]{:S(2)}, u32[]{:S(2)}) collective-permute-start(f32[160,128]{1,0:T(8,128)S(1)} %get-tuple-element.60), channel_id=1, source_target_pairs={{0,16},{1,17},{2,18},{3,19},{4,20},{5,21},{6,22},{7,23},{8,24},{9,... | collective-permute-start | bytes 245768 | tf_op jit(solution)/shard_map/ppermute | solution.py:27
  54.2 11.0 %collective-permute-start.11 = (f32[160,128]{1,0:T(8,128)S(1)}, f32[160,128]{1,0:T(8,128)S(1)}, u32[]{:S(2)}, u32[]{:S(2)}) collective-permute-start(f32[160,128]{1,0:T(8,128)S(1)} %get-tuple-element.63.refs_2_), channel_id=1, source_target_pairs={{0,1},{1,0},{2,3},{3,2},{4,5},{5,4},{6,7},{7,6},{8,9},{9,8},{10,11... | collective-permute-start | bytes 245768 | tf_op jit(solution)/shard_map/ppermute | solution.py:27
  58.7 10.7 %collective-permute-start.13 = (f32[96,128]{1,0:T(8,128)S(1)}, f32[96,128]{1,0:T(8,128)S(1)}, u32[]{:S(2)}, u32[]{:S(2)}) collective-permute-start(f32[96,128]{1,0:T(8,128)S(1)} %get-tuple-element.67), channel_id=1, source_target_pairs={{0,32},{1,33},{2,34},{3,35},{4,36},{5,37},{6,38},{7,39},{8,40},{9,... | collective-permute-start | bytes 147464 | tf_op jit(solution)/shard_map/ppermute | solution.py:27
  65.8 12.2 %collective-permute-start.12 = (f32[64,256]{1,0:T(8,128)S(1)}, f32[64,256]{1,0:T(8,128)S(1)}, u32[]{:S(2)}, u32[]{:S(2)}) collective-permute-start(f32[64,256]{1,0:T(8,128)S(1)} %get-tuple-element.65.refs_2_.refs_0_), channel_id=1, source_target_pairs={{0,32},{1,33},{2,34},{3,35},{4,36},{5,37},{6,38},{7,39},{8,40},{9,... | collective-permute-start | bytes 196616 | tf_op jit(solution)/shard_map/ppermute | solution.py:27
  69.6 8.5 %collective-permute-start.14 = (f32[64,256]{1,0:T(8,128)S(1)}, f32[64,256]{1,0:T(8,128)S(1)}, u32[]{:S(2)}, u32[]{:S(2)}) collective-permute-start(f32[64,256]{1,0:T(8,128)S(1)} %shard_map.61.refs_4_), channel_id=1, source_target_pairs={{0,1},{1,0},{2,3},{3,2},{4,5},{5,4},{6,7},{7,6},{8,9},{9,8},{10,11... | collective-permute-start | bytes 196616 | tf_op jit(solution)/shard_map/ppermute | solution.py:27
  78.6 10.7 %collective-permute-start.15 = (f32[64,384]{1,0:T(8,128)S(1)}, f32[64,384]{1,0:T(8,128)S(1)}, u32[]{:S(2)}, u32[]{:S(2)}) collective-permute-start(f32[64,384]{1,0:T(8,128)S(1)} %get-tuple-element.71.refs_0_), channel_id=1, source_target_pairs={{0,96},{1,97},{2,98},{3,99},{4,100},{5,101},{6,102},{7,103},{8,104... | collective-permute-start | bytes 294920 | tf_op jit(solution)/shard_map/ppermute | solution.py:27
  82.8 6.5 %collective-permute-start.16 = (f32[64,256]{1,0:T(8,128)S(1)}, f32[64,256]{1,0:T(8,128)S(1)}, u32[]{:S(2)}, u32[]{:S(2)}) collective-permute-start(f32[64,256]{1,0:T(8,128)S(1)} %get-tuple-element.72.refs_3_), channel_id=1, source_target_pairs={{0,6},{1,7},{2,4},{3,5},{4,2},{5,3},{6,0},{7,1},{8,14},{9,15},{10,... | collective-permute-start | bytes 196616 | tf_op jit(solution)/shard_map/ppermute | solution.py:27
  89.9 13.3 %collective-permute-start.19 = (f32[128,256]{1,0:T(8,128)S(1)}, f32[128,256]{1,0:T(8,128)S(1)}, u32[]{:S(2)}, u32[]{:S(2)}) collective-permute-start(f32[128,256]{1,0:T(8,128)S(1)} %get-tuple-element.79.refs_6_), channel_id=1, source_target_pairs={{0,2},{1,3},{2,0},{3,1},{4,6},{5,7},{6,4},{7,5},{8,10},{9,11},{10,... | collective-permute-start | bytes 393224 | tf_op jit(solution)/shard_map/ppermute | solution.py:27
  91.8 5.0 %collective-permute-start.17 = (f32[64,256]{1,0:T(8,128)S(1)}, f32[64,256]{1,0:T(8,128)S(1)}, u32[]{:S(2)}, u32[]{:S(2)}) collective-permute-start(f32[64,256]{1,0:T(8,128)S(1)} %get-tuple-element.74.refs_0_), channel_id=1, source_target_pairs={{0,128},{1,129},{2,130},{3,131},{4,132},{5,133},{6,134},{7,135},{8... | collective-permute-start | bytes 196616 | tf_op jit(solution)/shard_map/ppermute | solution.py:27
  97.3 5.9 %collective-permute-start.18 = (f32[64,128]{1,0:T(8,128)S(1)}, f32[64,128]{1,0:T(8,128)S(1)}, u32[]{:S(2)}, u32[]{:S(2)}) collective-permute-start(f32[64,128]{1,0:T(8,128)S(1)} %get-tuple-element.75.refs_0_), channel_id=1, source_target_pairs={{0,384},{1,385},{2,386},{3,387},{4,388},{5,389},{6,390},{7,391},{8... | collective-permute-start | bytes 98312 | tf_op jit(solution)/shard_map/ppermute | solution.py:27
  103.6 21.2 %collective-permute-start.20 = (f32[256,384]{1,0:T(8,128)S(1)}, f32[256,384]{1,0:T(8,128)S(1)}, u32[]{:S(2)}, u32[]{:S(2)}) collective-permute-start(f32[256,384]{1,0:T(8,128)S(1)} %get-tuple-element.81), channel_id=1, source_target_pairs={{0,1},{1,0},{2,3},{3,2},{4,5},{5,4},{6,7},{7,6},{8,9},{9,8},{10,11... | collective-permute-start | bytes 1179656 | tf_op jit(solution)/shard_map/ppermute | solution.py:27
where the time goes:
time: 128 us; the launch traced here: 127 us
  starting transfers between devices  75.2 us (59%)
  waiting for transfers between devices  21.4 us (17%)
  blocking collectives  14.5 us (11%)
  Pallas kernels  14.3 us (11%)
  local copies, waits for them, and re-layouts  1.43 us (1%)
    ppermute x21, starting transfers between devices, sent(): return lax.ppermute(array, 'leaf', [(i, i ^ mask) for i in range(count)])  75.2 us
    ppermute x21, waiting for transfers between devices, sent(): return lax.ppermute(array, 'leaf', [(i, i ^ mask) for i in range(count)])  21.4 us
    all_gather x1, blocking collectives, local(): gathered = lax.all_gather(last, 'leaf', axis_index_groups=octets)  14.5 us
    pallas_call x21, Pallas kernels, call(): pl.pallas_call(kernel, out_shape=shapes, in_specs=[vmem] * after, out_spe...  14.3 us
  transfers between devices with their start and end apart: 21, of which 8 were waited for; matrix products, arithmetic and copies ran while one was open for 0% of the time, Pallas kernels for 7%

commit v1 on v0

--- a/solution.py
+++ b/solution.py
@@ -233,8 +233,10 @@
     send_ref[...] = folded(rest)
 
 
-def level4_kernel(own_ref, got_ref, swap_ref, swap_got_ref, caps_ref, both_ref, next_ref):
-    _, core, _, _ = bits()
+def level4_kernel(own_ref, got_ref, swap_ref, swap_got_ref, caps_ref, both2_ref, both_ref,
+                  next_ref, down_ref):
+    _, core, _, _ = bits()
+    down_ref[...] = folded(both2_ref[:, RANK:])
     own, other = own_ref[...], unfolded(got_ref[...])
     both = solved(own, other, caps_ref[4])
     both_ref[...] = both
@@ -246,10 +248,12 @@
 
 
 def level5_kernel(own_ref, got_ref, swap4_ref, swap4_got_ref, swap_ref, swap_got_ref, caps_ref,
-                  both2_ref, both3_ref, both4_ref, both_ref, next_ref, down_ref):
-    down_ref[:, :128] = side(both2_ref[:, RANK:], both3_ref[:, :RANK])
-    down_ref[:, 128:] = both4_ref[...]
-    _, core, _, _ = bits()
+                  both2_ref, both1_ref, down_got_ref, both_ref, next_ref, down_ref):
+    _, core, _, y_high = bits()
+    mine, got = both2_ref[:, :RANK], unfolded(down_got_ref[...])
+    down_ref[...] = side(
+        both1_ref[:, RANK:], either(y_high, stack(mine, got), stack(got, mine))
+    )
     own, other = own_ref[...], got_ref[...]
     both = solved(own, other, caps_ref[5])
     both_ref[...] = both
@@ -263,13 +267,15 @@
     next_ref[...] = side(rest, a[:, 128:192], b[:, 128:192], a[:, 64:128])
 
 
-def level6_kernel(own_ref, got_ref, caps_ref, down_mine_ref, down_got_ref, both2_ref, both1_ref,
-                  both_ref, next_ref, down_ref):
-    _, _, _, y_high = bits()
-    mine = side(both2_ref[:, :RANK], down_mine_ref[:, RANK:192])
-    theirs = down_got_ref[:, :192]
-    rows = either(y_high, stack(mine, theirs), stack(theirs, mine))
-    down_ref[...] = side(both1_ref[:, RANK:], rows)
+def level6_kernel(own_ref, got_ref, caps_ref, down_mine_ref, down_got_ref, both1_ref, both0_ref,
+                  both_ref, next_ref, down_send_ref, down_own_ref):
+    _, _, part, _ = bits()
+    mine = side(both1_ref[:, :RANK], down_mine_ref[:, RANK:])
+    theirs = down_got_ref[...]
+    rows = either(part, stack(mine, theirs), stack(theirs, mine))
+    fill = jnp.zeros((256, RANK), F32)
+    down_send_ref[...] = side(both0_ref[:, RANK:], rows, fill)
+    down_own_ref[...] = side(both0_ref[:, :RANK], rows, fill)
     own, other = own_ref[:, :192], got_ref[:, :192]
     both = solved(own, other, caps_ref[6])
     both_ref[...] = both
@@ -286,19 +292,12 @@
     next_ref[...] = side(rest, jnp.zeros((64, RANK), F32))
 
 
-def level8_kernel(own_ref, got_ref, both5_ref, both6_ref, both7_ref, caps_ref, down_mine_ref,
-                  down_got_ref, both1_ref, both0_ref, out_ref, down_send_ref, down_own_ref):
-    _, _, part, _ = bits()
+def level8_kernel(own_ref, got_ref, both3_ref, both4_ref, both5_ref, both6_ref, both7_ref,
+                  caps_ref, out_ref):
     both = solved(own_ref[:, :RANK], got_ref[:, :RANK], caps_ref[8])
-    out_ref[:, :128] = side(both5_ref[:, :RANK], both6_ref[:, :RANK])
-    out_ref[:, 128:] = side(both7_ref[:, :RANK], both[:, :RANK])
-    mine = side(both1_ref[:, :RANK], down_mine_ref[:, RANK:])
-    theirs = down_got_ref[...]
-    rows = either(part, stack(mine, theirs), stack(theirs, mine))
-    down_send_ref[:, :320] = side(both0_ref[:, RANK:], rows)
-    down_own_ref[:, :320] = side(both0_ref[:, :RANK], rows)
-    down_send_ref[:, 320:] = jnp.zeros((256, 64), F32)
-    down_own_ref[:, 320:] = jnp.zeros((256, 64), F32)
+    out_ref[:, :128] = side(both3_ref[:, :RANK], both4_ref[:, :RANK])
+    out_ref[:, 128:256] = side(both5_ref[:, :RANK], both6_ref[:, :RANK])
+    out_ref[:, 256:] = side(both7_ref[:, :RANK], both[:, :RANK])
 
 
 def place(shard):
@@ -311,8 +310,8 @@
     factors = (high_ref[...], low_ref[...])
     last = [all_ref[place(shard)] for shard in range(8)]
     first, second = stack(*last[:4]), stack(*last[4:])
-    own = side(own_ref[:, :320], either(core, first, second))
-    other = side(got_ref[:, :320], either(core, second, first))
+    own = side(own_ref[:, :192], either(core, first, second))
+    other = side(got_ref[:, :192], either(core, second, first))
     own_out = mine_ref[...] - mm3(factors, split(own), NT)
     other_out = theirs_ref[...] - mm3(factors, split(other), NT)
     out_ref[:, :256] = either(core, own_out, other_out)
@@ -372,32 +371,31 @@
     )
     swap4_got = sent(swap4, PARTNER[0])
     grams = gram, sent(going, PARTNER[5])
-    both4, state = call(
-        level4_kernel, [(64, 128), (64, 256)], state, got, swap4, swap4_got, caps,
-        tokens=(basis_low,),
-    )
+    both4, state, down = call(
+        level4_kernel, [(64, 128), (64, 256), (32, 128)],
+        state, got, swap4, swap4_got, caps, both2, tokens=(basis_low,),
+    )
+    down_got = sent(down, PARTNER[2])
     got = sent(state, PARTNER[5])
     swap, = call(partial(gram_level_kernel, 5), GRAM_OUTS[5], *grams, tokens=(state,))
     swap_got = sent(swap, PARTNER[0])
     both5, state, down = call(
-        level5_kernel, [(64, 128), (64, 384), (64, 256)],
-        state, got, swap4, swap4_got, swap, swap_got, caps, both2, both3, both4,
+        level5_kernel, [(64, 128), (64, 384), (128, 128)],
+        state, got, swap4, swap4_got, swap, swap_got, caps, both2, both1, down_got,
     )
     got = sent(state, PARTNER[6])
-    down_got = sent(down, PARTNER[2])
-    both6, state, down = call(
-        level6_kernel, [(64, 128), (64, 256), (128, 256)],
-        state, got, caps, down, down_got, both2, both1,
+    down_got = sent(down, PARTNER[1])
+    both6, state, down_send, down_own = call(
+        level6_kernel, [(64, 128), (64, 256), (256, 256), (256, 256)],
+        state, got, caps, down, down_got, both1, both0,
     )
     got = sent(state, PARTNER[7])
-    down_got = sent(down, PARTNER[1])
+    down_got = sent(down_send, PARTNER[0])
     both7, state = call(level7_kernel, [(64, 128), (64, 128)], state, got, caps)
     got = sent(state, PARTNER[8])
-    last, down_send, down_own = call(
-        level8_kernel, [(64, 256), (256, 384), (256, 384)],
-        state, got, both5, both6, both7, caps, down, down_got, both1, both0,
-    )
-    down_got = sent(down_send, PARTNER[0])
+    last, = call(
+        level8_kernel, [(64, 384)], state, got, both3, both4, both5, both6, both7, caps
+    )
     octets = [list(range(n, n + 8)) for n in range(0, 512, 8)]
     gathered = lax.all_gather(last, "leaf", axis_index_groups=octets)
     out, = call(

time: 128 us -> 125 us (0.977)
  waiting for transfers between devices: 21.4 us -> 18.8 us
    ppermute x21, waiting for transfers between devices: 21.4 us -> 18.8 us  [sent(): return lax.ppermute(array, 'leaf', [(i, i ^ mask) for i in range(count)])]
  transfers between devices with their start and end apart: 21 -> 21, of which waited for: 8 -> 8; matrix products, arithmetic and copies ran while one was open for 0% -> 0% of each run, Pallas kernels for 7% -> 8%
where the time goes in v1:
time: 125 us; the launch traced here: 124 us
  starting transfers between devices  75.8 us (61%)
  waiting for transfers between devices  18.8 us (15%)
  Pallas kernels  14.3 us (11%)
  blocking collectives  13.6 us (11%)
  local copies, waits for them, and re-layouts  1.43 us (1%)
    ppermute x21, starting transfers between devices, sent(): return lax.ppermute(array, 'leaf', [(i, i ^ mask) for i in range(count)])  75.8 us
    ppermute x21, waiting for transfers between devices, sent(): return lax.ppermute(array, 'leaf', [(i, i ^ mask) for i in range(count)])  18.8 us
    pallas_call x21, Pallas kernels, call(): pl.pallas_call(kernel, out_shape=shapes, in_specs=[vmem] * after, out_spe...  14.3 us
    all_gather x1, blocking collectives, local(): gathered = lax.all_gather(last, 'leaf', axis_index_groups=octets)  13.6 us
  transfers between devices with their start and end apart: 21, of which 8 were waited for; matrix products, arithmetic and copies ran while one was open for 0% of the time, Pallas kernels for 8%

profile of v1, /device:TPU:1, one launch (start us, length us, event | category | flops | bytes accessed | tf_op | source)
XLA Modules:
  0.0 124.4 jit_solution(10587320251348595904)
XLA Ops:
  0.0 1.4 %copy-done.2 = f32[512,576]{0,1:T(8,128)S(1)} copy-done((f32[512,576]{0,1:T(8,128)S(1)}, f32[512,576]{0,1:T(8,128)}, u32[]{:S(2)}) %copy-start.2) | copy-done | bytes 1179672
  1.4 0.9 shard_map.46
  2.3 8.8 %collective-permute-start = (f32[256,512]{1,0:T(8,128)S(1)}, f32[256,512]{1,0:T(8,128)S(1)}, u32[]{:S(2)}, u32[]{:S(2)}) collective-permute-start(f32[256,512]{1,0:T(8,128)S(1)} %get-tuple-element.48), channel_id=1, source_target_pairs={{0,1},{1,0},{2,3},{3,2},{4,5},{5,4},{6,7},{7,6},{8,9},{9,8},{10,11... | collective-permute-start | bytes 1572872 | tf_op jit(solution)/shard_map/ppermute | solution.py:27
  11.1 2.1 %shard_map.47 = (f32[512,256]{1,0:T(8,128)S(1)}, f32[256,640]{1,0:T(8,128)S(1)}) custom-call(f32[512,512]{1,0:T(8,128)S(1)} %copy-done, f32[512,512]{1,0:T(8,128)S(1)} %copy-done.1, bf16[576,512]{1,0:T(8,128)(2,1)S(1)} %get-tuple-element.44.refs_2_, bf16[576,512]{1,0:T(8,128)(2,1)S(1)} %get-tuple-element.45.refs_3_), custom_call_target="tpu_custom_call" | custom-call | flops 852000000 | bytes 3276800 | tf_op jit(solution)/shard_map/pallas_call | solution.py:40
  13.3 0.0 copy-start.3
  13.3 2.1 %collective-permute-start.1 = (f32[256,640]{1,0:T(8,128)S(1)}, f32[256,640]{1,0:T(8,128)S(1)}, u32[]{:S(2)}, u32[]{:S(2)}) collective-permute-start(f32[256,640]{1,0:T(8,128)S(1)} %get-tuple-element.49.refs_2_), channel_id=1, source_target_pairs={{0,1},{1,0},{2,3},{3,2},{4,5},{5,4},{6,7},{7,6},{8,9},{9,8},{10,11... | collective-permute-start | bytes 1966088 | tf_op jit(solution)/shard_map/ppermute | solution.py:27
  15.4 0.0 collective-permute-done.refs_1_.refs_3_
  15.4 1.9 %collective-permute-start.3 = (f32[64,1408]{1,0:T(8,128)S(1)}, f32[64,1408]{1,0:T(8,128)S(1)}, u32[]{:S(2)}, u32[]{:S(2)}) collective-permute-start(f32[64,1408]{1,0:T(8,128)S(1)} %shard_map.48.refs_4_.refs_2_.refs_0_), channel_id=1, source_target_pairs={{0,2},{1,3},{2,0},{3,1},{4,6},{5,7},{6,4},{7,5},{8,10},{9,11},{10,... | collective-permute-start | bytes 1081352 | tf_op jit(solution)/shard_map/ppermute | solution.py:27
  17.3 0.0 copy-done.3
  17.4 0.2 shard_map.50.refs_4_.refs_6_.refs_2_.refs_7_
  17.6 2.2 %shard_map.49 = (f32[512,256]{1,0:T(8,128)S(1)}, f32[256,640]{1,0:T(8,128)S(1)}) custom-call(f32[512,512]{1,0:T(8,128)S(1)} %copy-done, f32[512,512]{1,0:T(8,128)S(1)} %copy-done.1, bf16[576,512]{1,0:T(8,128)(2,1)S(1)} %get-tuple-element.44.refs_2_, bf16[576,512]{1,0:T(8,128)(2,1)S(1)} %get-tuple-element.45.refs_3_, ...), custom_call_target="tpu_custom_call" | custom-call | flops 852000000 | bytes 3276800 | tf_op jit(solution)/shard_map/pallas_call | solution.py:40
  19.7 0.0 collective-permute-done.1.refs_1_
  19.8 1.0 shard_map.51
  20.8 3.4 %collective-permute-start.2 = (f32[128,512]{1,0:T(8,128)S(1)}, f32[128,512]{1,0:T(8,128)S(1)}, u32[]{:S(2)}, u32[]{:S(2)}) collective-permute-start(f32[128,512]{1,0:T(8,128)S(1)} %get-tuple-element.53.refs_2_), channel_id=1, source_target_pairs={{0,2},{1,3},{2,0},{3,1},{4,6},{5,7},{6,4},{7,5},{8,10},{9,11},{10,... | collective-permute-start | bytes 786440 | tf_op jit(solution)/shard_map/ppermute | solution.py:27
  24.1 2.7 %collective-permute-done.3.refs_3_.refs_1_ = f32[64,1408]{1,0:T(8,128)S(1)} collective-permute-done((f32[64,1408]{1,0:T(8,128)S(1)}, f32[64,1408]{1,0:T(8,128)S(1)}, u32[]{:S(2)}, u32[]{:S(2)}) %collective-permute-start.3) | collective-permute-done | bytes 360480 | tf_op jit(solution)/shard_map/ppermute | solution.py:27
  26.8 1.9 %collective-permute-start.5 = (f32[64,896]{1,0:T(8,128)S(1)}, f32[64,896]{1,0:T(8,128)S(1)}, u32[]{:S(2)}, u32[]{:S(2)}) collective-permute-start(f32[64,896]{1,0:T(8,128)S(1)} %shard_map.53.refs_2_.refs_0_), channel_id=1, source_target_pairs={{0,6},{1,7},{2,4},{3,5},{4,2},{5,3},{6,0},{7,1},{8,14},{9,15},{10,... | collective-permute-start | bytes 688136 | tf_op jit(solution)/shard_map/ppermute | solution.py:27
  28.8 3.7 %collective-permute-done.2.refs_1_ = f32[128,512]{1,0:T(8,128)S(1)} collective-permute-done((f32[128,512]{1,0:T(8,128)S(1)}, f32[128,512]{1,0:T(8,128)S(1)}, u32[]{:S(2)}, u32[]{:S(2)}) %collective-permute-start.2) | collective-permute-done | bytes 262176 | tf_op jit(solution)/shard_map/ppermute | solution.py:27
  32.4 0.6 shard_map.52
  33.1 1.9 %collective-permute-start.4 = (f32[64,512]{1,0:T(8,128)S(1)}, f32[64,512]{1,0:T(8,128)S(1)}, u32[]{:S(2)}, u32[]{:S(2)}) collective-permute-start(f32[64,512]{1,0:T(8,128)S(1)} %get-tuple-element.55.refs_2_), channel_id=1, source_target_pairs={{0,6},{1,7},{2,4},{3,5},{4,2},{5,3},{6,0},{7,1},{8,14},{9,15},{10,... | collective-permute-start | bytes 393224 | tf_op jit(solution)/shard_map/ppermute | solution.py:27
  35.0 0.0 collective-permute-done.5.refs_3_.refs_1_
  35.0 1.9 %collective-permute-start.7 = (f32[64,512]{1,0:T(8,128)S(1)}, f32[64,512]{1,0:T(8,128)S(1)}, u32[]{:S(2)}, u32[]{:S(2)}) collective-permute-start(f32[64,512]{1,0:T(8,128)S(1)} %shard_map.55.refs_0_), channel_id=1, source_target_pairs={{0,8},{1,9},{2,10},{3,11},{4,12},{5,13},{6,14},{7,15},{8,0},{9,1},... | collective-permute-start | bytes 393224 | tf_op jit(solution)/shard_map/ppermute | solution.py:27
  37.0 3.0 %collective-permute-done.4.refs_1_ = f32[64,512]{1,0:T(8,128)S(1)} collective-permute-done((f32[64,512]{1,0:T(8,128)S(1)}, f32[64,512]{1,0:T(8,128)S(1)}, u32[]{:S(2)}, u32[]{:S(2)}) %collective-permute-start.4) | collective-permute-done | bytes 131104 | tf_op jit(solution)/shard_map/ppermute | solution.py:27
  40.0 0.7 shard_map.54
  40.7 1.9 %collective-permute-start.6 = (f32[64,384]{1,0:T(8,128)S(1)}, f32[64,384]{1,0:T(8,128)S(1)}, u32[]{:S(2)}, u32[]{:S(2)}) collective-permute-start(f32[64,384]{1,0:T(8,128)S(1)} %get-tuple-element.56.refs_2_.refs_0_.refs_1_), channel_id=1, source_target_pairs={{0,8},{1,9},{2,10},{3,11},{4,12},{5,13},{6,14},{7,15},{8,0},{9,1},... | collective-permute-start | bytes 294920 | tf_op jit(solution)/shard_map/ppermute | solution.py:27
  42.6 0.0 collective-permute-done.7.refs_1_
  42.6 0.1 shard_map.56
  42.7 4.4 %collective-permute-start.8 = (f32[64,384]{1,0:T(8,128)S(1)}, f32[64,384]{1,0:T(8,128)S(1)}, u32[]{:S(2)}, u32[]{:S(2)}) collective-permute-start(f32[64,384]{1,0:T(8,128)S(1)} %get-tuple-element.57.refs_2_), channel_id=1, source_target_pairs={{0,1},{1,0},{2,3},{3,2},{4,5},{5,4},{6,7},{7,6},{8,9},{9,8},{10,11... | collective-permute-start | bytes 294920 | tf_op jit(solution)/shard_map/ppermute | solution.py:27
  47.1 1.9 %collective-permute-start.10 = (f32[160,128]{1,0:T(8,128)S(1)}, f32[160,128]{1,0:T(8,128)S(1)}, u32[]{:S(2)}, u32[]{:S(2)}) collective-permute-start(f32[160,128]{1,0:T(8,128)S(1)} %get-tuple-element.61), channel_id=1, source_target_pairs={{0,16},{1,17},{2,18},{3,19},{4,20},{5,21},{6,22},{7,23},{8,24},{9,... | collective-permute-start | bytes 245768 | tf_op jit(solution)/shard_map/ppermute | solution.py:27
  49.0 0.0 collective-permute-done.6.refs_1_
  49.0 0.0 collective-permute-done.8.refs_3_
  49.1 0.7 shard_map.57
  49.8 4.3 %collective-permute-start.9 = (f32[160,128]{1,0:T(8,128)S(1)}, f32[160,128]{1,0:T(8,128)S(1)}, u32[]{:S(2)}, u32[]{:S(2)}) collective-permute-start(f32[160,128]{1,0:T(8,128)S(1)} %get-tuple-element.59), channel_id=1, source_target_pairs={{0,16},{1,17},{2,18},{3,19},{4,20},{5,21},{6,22},{7,23},{8,24},{9,... | collective-permute-start | bytes 245768 | tf_op jit(solution)/shard_map/ppermute | solution.py:27
  54.1 0.0 collective-permute-done.10.refs_1_
  54.1 0.1 shard_map.58
  54.2 4.5 %collective-permute-start.11 = (f32[160,128]{1,0:T(8,128)S(1)}, f32[160,128]{1,0:T(8,128)S(1)}, u32[]{:S(2)}, u32[]{:S(2)}) collective-permute-start(f32[160,128]{1,0:T(8,128)S(1)} %get-tuple-element.62.refs_2_), channel_id=1, source_target_pairs={{0,1},{1,0},{2,3},{3,2},{4,5},{5,4},{6,7},{7,6},{8,9},{9,8},{10,11... | collective-permute-start | bytes 245768 | tf_op jit(solution)/shard_map/ppermute | solution.py:27
  58.7 6.1 %collective-permute-start.13 = (f32[96,128]{1,0:T(8,128)S(1)}, f32[96,128]{1,0:T(8,128)S(1)}, u32[]{:S(2)}, u32[]{:S(2)}) collective-permute-start(f32[96,128]{1,0:T(8,128)S(1)} %get-tuple-element.67), channel_id=1, source_target_pairs={{0,32},{1,33},{2,34},{3,35},{4,36},{5,37},{6,38},{7,39},{8,40},{9,... | collective-permute-start | bytes 147464 | tf_op jit(solution)/shard_map/ppermute | solution.py:27
  64.8 0.4 shard_map.59
  65.2 0.0 collective-permute-done.9.refs_1_
  65.3 0.0 collective-permute-done.11.refs_3_
  65.3 0.6 shard_map.60
  65.9 3.1 %collective-permute-start.12 = (f32[64,256]{1,0:T(8,128)S(1)}, f32[64,256]{1,0:T(8,128)S(1)}, u32[]{:S(2)}, u32[]{:S(2)}) collective-permute-start(f32[64,256]{1,0:T(8,128)S(1)} %get-tuple-element.65.refs_2_.refs_0_), channel_id=1, source_target_pairs={{0,32},{1,33},{2,34},{3,35},{4,36},{5,37},{6,38},{7,39},{8,40},{9,... | collective-permute-start | bytes 196616 | tf_op jit(solution)/shard_map/ppermute | solution.py:27
  69.0 0.5 collective-permute-done.13.refs_1_
  69.4 0.1 shard_map.61.refs_4_
  69.6 2.5 %collective-permute-start.14 = (f32[64,256]{1,0:T(8,128)S(1)}, f32[64,256]{1,0:T(8,128)S(1)}, u32[]{:S(2)}, u32[]{:S(2)}) collective-permute-start(f32[64,256]{1,0:T(8,128)S(1)} %shard_map.61.refs_4_), channel_id=1, source_target_pairs={{0,1},{1,0},{2,3},{3,2},{4,5},{5,4},{6,7},{7,6},{8,9},{9,8},{10,11... | collective-permute-start | bytes 196616 | tf_op jit(solution)/shard_map/ppermute | solution.py:27
  72.1 4.9 %collective-permute-start.15 = (f32[32,128]{1,0:T(8,128)S(1)}, f32[32,128]{1,0:T(8,128)S(1)}, u32[]{:S(2)}, u32[]{:S(2)}) collective-permute-start(f32[32,128]{1,0:T(8,128)S(1)} %get-tuple-element.69), channel_id=1, source_target_pairs={{0,6},{1,7},{2,4},{3,5},{4,2},{5,3},{6,0},{7,1},{8,14},{9,15},{10,... | collective-permute-start | bytes 49160 | tf_op jit(solution)/shard_map/ppermute | solution.py:27
  77.0 1.4 %collective-permute-done.15.refs_9_ = f32[32,128]{1,0:T(8,128)S(1)} collective-permute-done((f32[32,128]{1,0:T(8,128)S(1)}, f32[32,128]{1,0:T(8,128)S(1)}, u32[]{:S(2)}, u32[]{:S(2)}) %collective-permute-start.15) | collective-permute-done | bytes 16416 | tf_op jit(solution)/shard_map/ppermute | solution.py:27
  78.4 0.0 collective-permute-done.12.refs_1_
  78.4 0.0 collective-permute-done.14.refs_5_
  78.4 0.5 shard_map.62
  78.9 7.1 %collective-permute-start.16 = (f32[64,384]{1,0:T(8,128)S(1)}, f32[64,384]{1,0:T(8,128)S(1)}, u32[]{:S(2)}, u32[]{:S(2)}) collective-permute-start(f32[64,384]{1,0:T(8,128)S(1)} %get-tuple-element.70.refs_0_), channel_id=1, source_target_pairs={{0,96},{1,97},{2,98},{3,99},{4,100},{5,101},{6,102},{7,103},{8,104... | collective-permute-start | bytes 294920 | tf_op jit(solution)/shard_map/ppermute | solution.py:27
  86.0 1.9 %collective-permute-start.17 = (f32[128,128]{1,0:T(8,128)S(1)}, f32[128,128]{1,0:T(8,128)S(1)}, u32[]{:S(2)}, u32[]{:S(2)}) collective-permute-start(f32[128,128]{1,0:T(8,128)S(1)} %get-tuple-element.71.refs_3_), channel_id=1, source_target_pairs={{0,2},{1,3},{2,0},{3,1},{4,6},{5,7},{6,4},{7,5},{8,10},{9,11},{10,... | collective-permute-start | bytes 196616 | tf_op jit(solution)/shard_map/ppermute | solution.py:27
  88.0 3.1 %collective-permute-done.17.refs_4_ = f32[128,128]{1,0:T(8,128)S(1)} collective-permute-done((f32[128,128]{1,0:T(8,128)S(1)}, f32[128,128]{1,0:T(8,128)S(1)}, u32[]{:S(2)}, u32[]{:S(2)}) %collective-permute-start.17) | collective-permute-done | bytes 65568 | tf_op jit(solution)/shard_map/ppermute | solution.py:27
  91.1 2.6 %collective-permute-done.16.refs_1_ = f32[64,384]{1,0:T(8,128)S(1)} collective-permute-done((f32[64,384]{1,0:T(8,128)S(1)}, f32[64,384]{1,0:T(8,128)S(1)}, u32[]{:S(2)}, u32[]{:S(2)}) %collective-permute-start.16) | collective-permute-done | bytes 98336 | tf_op jit(solution)/shard_map/ppermute | solution.py:27
  93.6 0.5 shard_map.63
  94.2 3.1 %collective-permute-start.19 = (f32[64,256]{1,0:T(8,128)S(1)}, f32[64,256]{1,0:T(8,128)S(1)}, u32[]{:S(2)}, u32[]{:S(2)}) collective-permute-start(f32[64,256]{1,0:T(8,128)S(1)} %get-tuple-element.75.refs_0_), channel_id=1, source_target_pairs={{0,128},{1,129},{2,130},{3,131},{4,132},{5,133},{6,134},{7,135},{8... | collective-permute-start | bytes 196616 | tf_op jit(solution)/shard_map/ppermute | solution.py:27
  97.3 1.9 %collective-permute-done.19.refs_1_ = f32[64,256]{1,0:T(8,128)S(1)} collective-permute-done((f32[64,256]{1,0:T(8,128)S(1)}, f32[64,256]{1,0:T(8,128)S(1)}, u32[]{:S(2)}, u32[]{:S(2)}) %collective-permute-start.19) | collective-permute-done | bytes 65568 | tf_op jit(solution)/shard_map/ppermute | solution.py:27
  99.2 0.5 shard_map.64
  99.7 4.4 %collective-permute-start.20 = (f32[64,128]{1,0:T(8,128)S(1)}, f32[64,128]{1,0:T(8,128)S(1)}, u32[]{:S(2)}, u32[]{:S(2)}) collective-permute-start(f32[64,128]{1,0:T(8,128)S(1)} %get-tuple-element.76.refs_0_), channel_id=1, source_target_pairs={{0,384},{1,385},{2,386},{3,387},{4,388},{5,389},{6,390},{7,391},{8... | collective-permute-start | bytes 98312 | tf_op jit(solution)/shard_map/ppermute | solution.py:27
  104.1 3.8 %collective-permute-start.18 = (f32[256,256]{1,0:T(8,128)S(1)}, f32[256,256]{1,0:T(8,128)S(1)}, u32[]{:S(2)}, u32[]{:S(2)}) collective-permute-start(f32[256,256]{1,0:T(8,128)S(1)} %get-tuple-element.73), channel_id=1, source_target_pairs={{0,1},{1,0},{2,3},{3,2},{4,5},{5,4},{6,7},{7,6},{8,9},{9,8},{10,11... | collective-permute-start | bytes 786440 | tf_op jit(solution)/shard_map/ppermute | solution.py:27
  107.9 0.0 collective-permute-done.20.refs_1_
  107.9 0.3 shard_map.65
  108.3 13.6 %all-gather = f32[512,384]{1,0:T(8,128)S(1)} all-gather(f32[64,384]{1,0:T(8,128)S(1)} %shard_map.65), channel_id=2, replica_groups={{0,1,2,3,4,5,6,7},{8,9,10,11,12,13,14,15},{16,17,18,19,20,21,22,23},{24..., dimensions={0}, use_global_device_ids=true | all-gather | bytes 884736 | tf_op jit(solution)/shard_map/all_gather | solution.py:400
  121.9 0.0 collective-permute-done.18.refs_2_
  121.9 2.5 %shard_map.66 = f32[512,512]{1,0:T(8,128)} custom-call(f32[512,256]{1,0:T(8,128)S(1)} %get-tuple-element.46.refs_0_, f32[512,256]{1,0:T(8,128)S(1)} %get-tuple-element.50.refs_1_, f32[256,256]{1,0:T(8,128)S(1)} %collective-permute-done.18.refs_2_, f32[256,256]{1,0:T(8,128)S(1)} %get-tuple-element.74.refs_3_, f32[8,64,384]{2,1,0:T(8,128)S(1)} %bitcast.3, ...), custom_call_target="tpu_custom_call" | custom-call | flops 900000000 | bytes 3538944 | tf_op jit(solution)/shard_map/pallas_call | solution.py:40
  (8 shorter events, 0.1 us)
Async XLA Ops:
  0.0 11.1 %copy-start = (f32[512,512]{1,0:T(8,128)S(1)}, f32[512,512]{1,0:T(8,128)}, u32[]{:S(2)}) copy-start(f32[512,512]{1,0:T(8,128)} %refs_0_.3) | copy-start | bytes 3145732
  0.0 11.1 %copy-start.1 = (f32[512,512]{1,0:T(8,128)S(1)}, f32[512,512]{1,0:T(8,128)}, u32[]{:S(2)}) copy-start(f32[512,512]{1,0:T(8,128)} %refs_1_.3) | copy-start | bytes 3145732
  0.0 1.4 %copy-start.2 = (f32[512,576]{0,1:T(8,128)S(1)}, f32[512,576]{0,1:T(8,128)}, u32[]{:S(2)}) copy-start(f32[512,576]{0,1:T(8,128)} %param.6) | copy-start | bytes 3538948
  2.3 13.1 %collective-permute-start = (f32[256,512]{1,0:T(8,128)S(1)}, f32[256,512]{1,0:T(8,128)S(1)}, u32[]{:S(2)}, u32[]{:S(2)}) collective-permute-start(f32[256,512]{1,0:T(8,128)S(1)} %get-tuple-element.48), channel_id=1, source_target_pairs={{0,1},{1,0},{2,3},{3,2},{4,5},{5,4},{6,7},{7,6},{8,9},{9,8},{10,11... | collective-permute-start | bytes 1572872 | tf_op jit(solution)/shard_map/ppermute | solution.py:27
  13.3 4.1 %copy-start.3 = (f32[1,9,128,128]{3,2,1,0:T(8,128)S(1)}, f32[1,9,128,128]{3,2,1,0:T(8,128)}, u32[]{:S(2)}) copy-start(f32[1,9,128,128]{3,2,1,0:T(8,128)} %param.7) | copy-start | bytes 1769476
  13.3 6.5 %collective-permute-start.1 = (f32[256,640]{1,0:T(8,128)S(1)}, f32[256,640]{1,0:T(8,128)S(1)}, u32[]{:S(2)}, u32[]{:S(2)}) collective-permute-start(f32[256,640]{1,0:T(8,128)S(1)} %get-tuple-element.49.refs_2_), channel_id=1, source_target_pairs={{0,1},{1,0},{2,3},{3,2},{4,5},{5,4},{6,7},{7,6},{8,9},{9,8},{10,11... | collective-permute-start | bytes 1966088 | tf_op jit(solution)/shard_map/ppermute | solution.py:27
  15.4 11.4 %collective-permute-start.3 = (f32[64,1408]{1,0:T(8,128)S(1)}, f32[64,1408]{1,0:T(8,128)S(1)}, u32[]{:S(2)}, u32[]{:S(2)}) collective-permute-start(f32[64,1408]{1,0:T(8,128)S(1)} %shard_map.48.refs_4_.refs_2_.refs_0_), channel_id=1, source_target_pairs={{0,2},{1,3},{2,0},{3,1},{4,6},{5,7},{6,4},{7,5},{8,10},{9,11},{10,... | collective-permute-start | bytes 1081352 | tf_op jit(solution)/shard_map/ppermute | solution.py:27
  20.8 11.6 %collective-permute-start.2 = (f32[128,512]{1,0:T(8,128)S(1)}, f32[128,512]{1,0:T(8,128)S(1)}, u32[]{:S(2)}, u32[]{:S(2)}) collective-permute-start(f32[128,512]{1,0:T(8,128)S(1)} %get-tuple-element.53.refs_2_), channel_id=1, source_target_pairs={{0,2},{1,3},{2,0},{3,1},{4,6},{5,7},{6,4},{7,5},{8,10},{9,11},{10,... | collective-permute-start | bytes 786440 | tf_op jit(solution)/shard_map/ppermute | solution.py:27
  26.8 8.2 %collective-permute-start.5 = (f32[64,896]{1,0:T(8,128)S(1)}, f32[64,896]{1,0:T(8,128)S(1)}, u32[]{:S(2)}, u32[]{:S(2)}) collective-permute-start(f32[64,896]{1,0:T(8,128)S(1)} %shard_map.53.refs_2_.refs_0_), channel_id=1, source_target_pairs={{0,6},{1,7},{2,4},{3,5},{4,2},{5,3},{6,0},{7,1},{8,14},{9,15},{10,... | collective-permute-start | bytes 688136 | tf_op jit(solution)/shard_map/ppermute | solution.py:27
  33.1 6.9 %collective-permute-start.4 = (f32[64,512]{1,0:T(8,128)S(1)}, f32[64,512]{1,0:T(8,128)S(1)}, u32[]{:S(2)}, u32[]{:S(2)}) collective-permute-start(f32[64,512]{1,0:T(8,128)S(1)} %get-tuple-element.55.refs_2_), channel_id=1, source_target_pairs={{0,6},{1,7},{2,4},{3,5},{4,2},{5,3},{6,0},{7,1},{8,14},{9,15},{10,... | collective-permute-start | bytes 393224 | tf_op jit(solution)/shard_map/ppermute | solution.py:27
  35.0 7.6 %collective-permute-start.7 = (f32[64,512]{1,0:T(8,128)S(1)}, f32[64,512]{1,0:T(8,128)S(1)}, u32[]{:S(2)}, u32[]{:S(2)}) collective-permute-start(f32[64,512]{1,0:T(8,128)S(1)} %shard_map.55.refs_0_), channel_id=1, source_target_pairs={{0,8},{1,9},{2,10},{3,11},{4,12},{5,13},{6,14},{7,15},{8,0},{9,1},... | collective-permute-start | bytes 393224 | tf_op jit(solution)/shard_map/ppermute | solution.py:27
  40.7 8.4 %collective-permute-start.6 = (f32[64,384]{1,0:T(8,128)S(1)}, f32[64,384]{1,0:T(8,128)S(1)}, u32[]{:S(2)}, u32[]{:S(2)}) collective-permute-start(f32[64,384]{1,0:T(8,128)S(1)} %get-tuple-element.56.refs_2_.refs_0_.refs_1_), channel_id=1, source_target_pairs={{0,8},{1,9},{2,10},{3,11},{4,12},{5,13},{6,14},{7,15},{8,0},{9,1},... | collective-permute-start | bytes 294920 | tf_op jit(solution)/shard_map/ppermute | solution.py:27
  42.7 6.4 %collective-permute-start.8 = (f32[64,384]{1,0:T(8,128)S(1)}, f32[64,384]{1,0:T(8,128)S(1)}, u32[]{:S(2)}, u32[]{:S(2)}) collective-permute-start(f32[64,384]{1,0:T(8,128)S(1)} %get-tuple-element.57.refs_2_), channel_id=1, source_target_pairs={{0,1},{1,0},{2,3},{3,2},{4,5},{5,4},{6,7},{7,6},{8,9},{9,8},{10,11... | collective-permute-start | bytes 294920 | tf_op jit(solution)/shard_map/ppermute | solution.py:27
  47.1 7.0 %collective-permute-start.10 = (f32[160,128]{1,0:T(8,128)S(1)}, f32[160,128]{1,0:T(8,128)S(1)}, u32[]{:S(2)}, u32[]{:S(2)}) collective-permute-start(f32[160,128]{1,0:T(8,128)S(1)} %get-tuple-element.61), channel_id=1, source_target_pairs={{0,16},{1,17},{2,18},{3,19},{4,20},{5,21},{6,22},{7,23},{8,24},{9,... | collective-permute-start | bytes 245768 | tf_op jit(solution)/shard_map/ppermute | solution.py:27
  49.8 15.4 %collective-permute-start.9 = (f32[160,128]{1,0:T(8,128)S(1)}, f32[160,128]{1,0:T(8,128)S(1)}, u32[]{:S(2)}, u32[]{:S(2)}) collective-permute-start(f32[160,128]{1,0:T(8,128)S(1)} %get-tuple-element.59), channel_id=1, source_target_pairs={{0,16},{1,17},{2,18},{3,19},{4,20},{5,21},{6,22},{7,23},{8,24},{9,... | collective-permute-start | bytes 245768 | tf_op jit(solution)/shard_map/ppermute | solution.py:27
  54.2 11.0 %collective-permute-start.11 = (f32[160,128]{1,0:T(8,128)S(1)}, f32[160,128]{1,0:T(8,128)S(1)}, u32[]{:S(2)}, u32[]{:S(2)}) collective-permute-start(f32[160,128]{1,0:T(8,128)S(1)} %get-tuple-element.62.refs_2_), channel_id=1, source_target_pairs={{0,1},{1,0},{2,3},{3,2},{4,5},{5,4},{6,7},{7,6},{8,9},{9,8},{10,11... | collective-permute-start | bytes 245768 | tf_op jit(solution)/shard_map/ppermute | solution.py:27
  58.7 10.7 %collective-permute-start.13 = (f32[96,128]{1,0:T(8,128)S(1)}, f32[96,128]{1,0:T(8,128)S(1)}, u32[]{:S(2)}, u32[]{:S(2)}) collective-permute-start(f32[96,128]{1,0:T(8,128)S(1)} %get-tuple-element.67), channel_id=1, source_target_pairs={{0,32},{1,33},{2,34},{3,35},{4,36},{5,37},{6,38},{7,39},{8,40},{9,... | collective-permute-start | bytes 147464 | tf_op jit(solution)/shard_map/ppermute | solution.py:27
  65.9 12.5 %collective-permute-start.12 = (f32[64,256]{1,0:T(8,128)S(1)}, f32[64,256]{1,0:T(8,128)S(1)}, u32[]{:S(2)}, u32[]{:S(2)}) collective-permute-start(f32[64,256]{1,0:T(8,128)S(1)} %get-tuple-element.65.refs_2_.refs_0_), channel_id=1, source_target_pairs={{0,32},{1,33},{2,34},{3,35},{4,36},{5,37},{6,38},{7,39},{8,40},{9,... | collective-permute-start | bytes 196616 | tf_op jit(solution)/shard_map/ppermute | solution.py:27
  69.6 8.8 %collective-permute-start.14 = (f32[64,256]{1,0:T(8,128)S(1)}, f32[64,256]{1,0:T(8,128)S(1)}, u32[]{:S(2)}, u32[]{:S(2)}) collective-permute-start(f32[64,256]{1,0:T(8,128)S(1)} %shard_map.61.refs_4_), channel_id=1, source_target_pairs={{0,1},{1,0},{2,3},{3,2},{4,5},{5,4},{6,7},{7,6},{8,9},{9,8},{10,11... | collective-permute-start | bytes 196616 | tf_op jit(solution)/shard_map/ppermute | solution.py:27
  72.1 6.3 %collective-permute-start.15 = (f32[32,128]{1,0:T(8,128)S(1)}, f32[32,128]{1,0:T(8,128)S(1)}, u32[]{:S(2)}, u32[]{:S(2)}) collective-permute-start(f32[32,128]{1,0:T(8,128)S(1)} %get-tuple-element.69), channel_id=1, source_target_pairs={{0,6},{1,7},{2,4},{3,5},{4,2},{5,3},{6,0},{7,1},{8,14},{9,15},{10,... | collective-permute-start | bytes 49160 | tf_op jit(solution)/shard_map/ppermute | solution.py:27
  78.9 14.7 %collective-permute-start.16 = (f32[64,384]{1,0:T(8,128)S(1)}, f32[64,384]{1,0:T(8,128)S(1)}, u32[]{:S(2)}, u32[]{:S(2)}) collective-permute-start(f32[64,384]{1,0:T(8,128)S(1)} %get-tuple-element.70.refs_0_), channel_id=1, source_target_pairs={{0,96},{1,97},{2,98},{3,99},{4,100},{5,101},{6,102},{7,103},{8,104... | collective-permute-start | bytes 294920 | tf_op jit(solution)/shard_map/ppermute | solution.py:27
  86.0 5.0 %collective-permute-start.17 = (f32[128,128]{1,0:T(8,128)S(1)}, f32[128,128]{1,0:T(8,128)S(1)}, u32[]{:S(2)}, u32[]{:S(2)}) collective-permute-start(f32[128,128]{1,0:T(8,128)S(1)} %get-tuple-element.71.refs_3_), channel_id=1, source_target_pairs={{0,2},{1,3},{2,0},{3,1},{4,6},{5,7},{6,4},{7,5},{8,10},{9,11},{10,... | collective-permute-start | bytes 196616 | tf_op jit(solution)/shard_map/ppermute | solution.py:27
  94.2 5.0 %collective-permute-start.19 = (f32[64,256]{1,0:T(8,128)S(1)}, f32[64,256]{1,0:T(8,128)S(1)}, u32[]{:S(2)}, u32[]{:S(2)}) collective-permute-start(f32[64,256]{1,0:T(8,128)S(1)} %get-tuple-element.75.refs_0_), channel_id=1, source_target_pairs={{0,128},{1,129},{2,130},{3,131},{4,132},{5,133},{6,134},{7,135},{8... | collective-permute-start | bytes 196616 | tf_op jit(solution)/shard_map/ppermute | solution.py:27
  99.7 8.2 %collective-permute-start.20 = (f32[64,128]{1,0:T(8,128)S(1)}, f32[64,128]{1,0:T(8,128)S(1)}, u32[]{:S(2)}, u32[]{:S(2)}) collective-permute-start(f32[64,128]{1,0:T(8,128)S(1)} %get-tuple-element.76.refs_0_), channel_id=1, source_target_pairs={{0,384},{1,385},{2,386},{3,387},{4,388},{5,389},{6,390},{7,391},{8... | collective-permute-start | bytes 98312 | tf_op jit(solution)/shard_map/ppermute | solution.py:27
  104.1 17.8 %collective-permute-start.18 = (f32[256,256]{1,0:T(8,128)S(1)}, f32[256,256]{1,0:T(8,128)S(1)}, u32[]{:S(2)}, u32[]{:S(2)}) collective-permute-start(f32[256,256]{1,0:T(8,128)S(1)} %get-tuple-element.73), channel_id=1, source_target_pairs={{0,1},{1,0},{2,3},{3,2},{4,5},{5,4},{6,7},{7,6},{8,9},{9,8},{10,11... | collective-permute-start | bytes 786440 | tf_op jit(solution)/shard_map/ppermute | solution.py:27

commit v2 on v1

--- a/solution.py
+++ b/solution.py
@@ -7,7 +7,6 @@
 from jax.experimental.pallas import tpu as pltpu
 from jax.sharding import PartitionSpec as P
 
-HIGHEST = lax.Precision.HIGHEST
 F32 = jnp.float32
 BF16 = jnp.bfloat16
 RANK = 64
@@ -61,7 +60,7 @@
 
 
 def small(a, b, dims):
-    return lax.dot_general(a, b, (dims, ((), ())), precision=HIGHEST, preferred_element_type=F32)
+    return mm3(split(a), split(b), dims)
 
 
 def side(*parts):

time: 125 us -> 125 us (level)
  waiting for transfers between devices: 18.8 us -> 21.9 us
  starting transfers between devices: 75.8 us -> 73.7 us
  Pallas kernels: 14.3 us -> 12.8 us
    ppermute x21, waiting for transfers between devices: 18.8 us -> 21.9 us  [sent(): return lax.ppermute(array, 'leaf', [(i, i ^ mask) for i in range(count)])]
    ppermute x21, starting transfers between devices: 75.8 us -> 73.7 us  [sent(): return lax.ppermute(array, 'leaf', [(i, i ^ mask) for i in range(count)])]
    pallas_call x21, Pallas kernels: 14.3 us -> 12.8 us  [call(): pl.pallas_call(kernel, out_shape=shapes, in_specs=[vmem] * after, out_spe...]
  transfers between devices with their start and end apart: 21 -> 21, of which waited for: 8 -> 8; matrix products, arithmetic and copies ran while one was open for 0% -> 0% of each run, Pallas kernels for 8% -> 7%
where the time goes in v2:
time: 125 us; the launch traced here: 124 us
  starting transfers between devices  73.7 us (59%)
  waiting for transfers between devices  21.9 us (18%)
  blocking collectives  13.6 us (11%)
  Pallas kernels  12.8 us (10%)
  local copies, waits for them, and re-layouts  1.43 us (1%)
    ppermute x21, starting transfers between devices, sent(): return lax.ppermute(array, 'leaf', [(i, i ^ mask) for i in range(count)])  73.7 us
    ppermute x21, waiting for transfers between devices, sent(): return lax.ppermute(array, 'leaf', [(i, i ^ mask) for i in range(count)])  21.9 us
    all_gather x1, blocking collectives, local(): gathered = lax.all_gather(last, 'leaf', axis_index_groups=octets)  13.6 us
    pallas_call x21, Pallas kernels, call(): pl.pallas_call(kernel, out_shape=shapes, in_specs=[vmem] * after, out_spe...  12.8 us
  transfers between devices with their start and end apart: 21, of which 8 were waited for; matrix products, arithmetic and copies ran while one was open for 0% of the time, Pallas kernels for 7%

profile of v2, /device:TPU:1, one launch (start us, length us, event | category | flops | bytes accessed | tf_op | source)
XLA Modules:
  0.0 123.9 jit_solution(17252084263635653293)
XLA Ops:
  0.0 1.4 %copy-done.2 = f32[512,576]{0,1:T(8,128)S(1)} copy-done((f32[512,576]{0,1:T(8,128)S(1)}, f32[512,576]{0,1:T(8,128)}, u32[]{:S(2)}) %copy-start.2) | copy-done | bytes 1179672
  1.4 0.9 shard_map.46
  2.3 8.8 %collective-permute-start = (f32[256,512]{1,0:T(8,128)S(1)}, f32[256,512]{1,0:T(8,128)S(1)}, u32[]{:S(2)}, u32[]{:S(2)}) collective-permute-start(f32[256,512]{1,0:T(8,128)S(1)} %get-tuple-element.48), channel_id=1, source_target_pairs={{0,1},{1,0},{2,3},{3,2},{4,5},{5,4},{6,7},{7,6},{8,9},{9,8},{10,11... | collective-permute-start | bytes 1572872 | tf_op jit(solution)/shard_map/ppermute | solution.py:26
  11.1 2.1 %shard_map.47 = (f32[512,256]{1,0:T(8,128)S(1)}, f32[256,640]{1,0:T(8,128)S(1)}) custom-call(f32[512,512]{1,0:T(8,128)S(1)} %copy-done, f32[512,512]{1,0:T(8,128)S(1)} %copy-done.1, bf16[576,512]{1,0:T(8,128)(2,1)S(1)} %get-tuple-element.44.refs_2_, bf16[576,512]{1,0:T(8,128)(2,1)S(1)} %get-tuple-element.45.refs_3_), custom_call_target="tpu_custom_call" | custom-call | flops 852000000 | bytes 3276800 | tf_op jit(solution)/shard_map/pallas_call | solution.py:39
  13.3 0.0 copy-start.3
  13.3 2.1 %collective-permute-start.1 = (f32[256,640]{1,0:T(8,128)S(1)}, f32[256,640]{1,0:T(8,128)S(1)}, u32[]{:S(2)}, u32[]{:S(2)}) collective-permute-start(f32[256,640]{1,0:T(8,128)S(1)} %get-tuple-element.49.refs_2_), channel_id=1, source_target_pairs={{0,1},{1,0},{2,3},{3,2},{4,5},{5,4},{6,7},{7,6},{8,9},{9,8},{10,11... | collective-permute-start | bytes 1966088 | tf_op jit(solution)/shard_map/ppermute | solution.py:26
  15.4 0.0 collective-permute-done.refs_1_.refs_3_
  15.4 1.9 %collective-permute-start.3 = (f32[64,1408]{1,0:T(8,128)S(1)}, f32[64,1408]{1,0:T(8,128)S(1)}, u32[]{:S(2)}, u32[]{:S(2)}) collective-permute-start(f32[64,1408]{1,0:T(8,128)S(1)} %shard_map.48.refs_4_.refs_2_.refs_0_), channel_id=1, source_target_pairs={{0,2},{1,3},{2,0},{3,1},{4,6},{5,7},{6,4},{7,5},{8,10},{9,11},{10,... | collective-permute-start | bytes 1081352 | tf_op jit(solution)/shard_map/ppermute | solution.py:26
  17.3 0.0 copy-done.3
  17.4 0.2 shard_map.50.refs_4_.refs_6_.refs_2_.refs_7_
  17.6 2.2 %shard_map.49 = (f32[512,256]{1,0:T(8,128)S(1)}, f32[256,640]{1,0:T(8,128)S(1)}) custom-call(f32[512,512]{1,0:T(8,128)S(1)} %copy-done, f32[512,512]{1,0:T(8,128)S(1)} %copy-done.1, bf16[576,512]{1,0:T(8,128)(2,1)S(1)} %get-tuple-element.44.refs_2_, bf16[576,512]{1,0:T(8,128)(2,1)S(1)} %get-tuple-element.45.refs_3_, ...), custom_call_target="tpu_custom_call" | custom-call | flops 852000000 | bytes 3276800 | tf_op jit(solution)/shard_map/pallas_call | solution.py:39
  19.7 0.0 collective-permute-done.1.refs_1_
  19.8 0.7 shard_map.51
  20.4 3.4 %collective-permute-start.2 = (f32[128,512]{1,0:T(8,128)S(1)}, f32[128,512]{1,0:T(8,128)S(1)}, u32[]{:S(2)}, u32[]{:S(2)}) collective-permute-start(f32[128,512]{1,0:T(8,128)S(1)} %get-tuple-element.53.refs_2_), channel_id=1, source_target_pairs={{0,2},{1,3},{2,0},{3,1},{4,6},{5,7},{6,4},{7,5},{8,10},{9,11},{10,... | collective-permute-start | bytes 786440 | tf_op jit(solution)/shard_map/ppermute | solution.py:26
  23.8 3.0 %collective-permute-done.3.refs_3_.refs_1_ = f32[64,1408]{1,0:T(8,128)S(1)} collective-permute-done((f32[64,1408]{1,0:T(8,128)S(1)}, f32[64,1408]{1,0:T(8,128)S(1)}, u32[]{:S(2)}, u32[]{:S(2)}) %collective-permute-start.3) | collective-permute-done | bytes 360480 | tf_op jit(solution)/shard_map/ppermute | solution.py:26
  26.8 1.9 %collective-permute-start.5 = (f32[64,896]{1,0:T(8,128)S(1)}, f32[64,896]{1,0:T(8,128)S(1)}, u32[]{:S(2)}, u32[]{:S(2)}) collective-permute-start(f32[64,896]{1,0:T(8,128)S(1)} %shard_map.53.refs_2_.refs_0_), channel_id=1, source_target_pairs={{0,6},{1,7},{2,4},{3,5},{4,2},{5,3},{6,0},{7,1},{8,14},{9,15},{10,... | collective-permute-start | bytes 688136 | tf_op jit(solution)/shard_map/ppermute | solution.py:26
  28.8 3.7 %collective-permute-done.2.refs_1_ = f32[128,512]{1,0:T(8,128)S(1)} collective-permute-done((f32[128,512]{1,0:T(8,128)S(1)}, f32[128,512]{1,0:T(8,128)S(1)}, u32[]{:S(2)}, u32[]{:S(2)}) %collective-permute-start.2) | collective-permute-done | bytes 262176 | tf_op jit(solution)/shard_map/ppermute | solution.py:26
  32.4 0.6 shard_map.52
  33.0 1.9 %collective-permute-start.4 = (f32[64,512]{1,0:T(8,128)S(1)}, f32[64,512]{1,0:T(8,128)S(1)}, u32[]{:S(2)}, u32[]{:S(2)}) collective-permute-start(f32[64,512]{1,0:T(8,128)S(1)} %get-tuple-element.55.refs_2_), channel_id=1, source_target_pairs={{0,6},{1,7},{2,4},{3,5},{4,2},{5,3},{6,0},{7,1},{8,14},{9,15},{10,... | collective-permute-start | bytes 393224 | tf_op jit(solution)/shard_map/ppermute | solution.py:26
  34.9 0.0 collective-permute-done.5.refs_3_.refs_1_
  35.0 1.9 %collective-permute-start.7 = (f32[64,512]{1,0:T(8,128)S(1)}, f32[64,512]{1,0:T(8,128)S(1)}, u32[]{:S(2)}, u32[]{:S(2)}) collective-permute-start(f32[64,512]{1,0:T(8,128)S(1)} %shard_map.55.refs_0_), channel_id=1, source_target_pairs={{0,8},{1,9},{2,10},{3,11},{4,12},{5,13},{6,14},{7,15},{8,0},{9,1},... | collective-permute-start | bytes 393224 | tf_op jit(solution)/shard_map/ppermute | solution.py:26
  36.9 3.0 %collective-permute-done.4.refs_1_ = f32[64,512]{1,0:T(8,128)S(1)} collective-permute-done((f32[64,512]{1,0:T(8,128)S(1)}, f32[64,512]{1,0:T(8,128)S(1)}, u32[]{:S(2)}, u32[]{:S(2)}) %collective-permute-start.4) | collective-permute-done | bytes 131104 | tf_op jit(solution)/shard_map/ppermute | solution.py:26
  39.9 0.5 shard_map.54
  40.4 1.9 %collective-permute-start.6 = (f32[64,384]{1,0:T(8,128)S(1)}, f32[64,384]{1,0:T(8,128)S(1)}, u32[]{:S(2)}, u32[]{:S(2)}) collective-permute-start(f32[64,384]{1,0:T(8,128)S(1)} %get-tuple-element.56.refs_2_.refs_0_.refs_1_), channel_id=1, source_target_pairs={{0,8},{1,9},{2,10},{3,11},{4,12},{5,13},{6,14},{7,15},{8,0},{9,1},... | collective-permute-start | bytes 294920 | tf_op jit(solution)/shard_map/ppermute | solution.py:26
  42.3 0.0 collective-permute-done.7.refs_1_
  42.3 0.1 shard_map.56
  42.4 4.7 %collective-permute-start.8 = (f32[64,384]{1,0:T(8,128)S(1)}, f32[64,384]{1,0:T(8,128)S(1)}, u32[]{:S(2)}, u32[]{:S(2)}) collective-permute-start(f32[64,384]{1,0:T(8,128)S(1)} %get-tuple-element.57.refs_2_), channel_id=1, source_target_pairs={{0,1},{1,0},{2,3},{3,2},{4,5},{5,4},{6,7},{7,6},{8,9},{9,8},{10,11... | collective-permute-start | bytes 294920 | tf_op jit(solution)/shard_map/ppermute | solution.py:26
  47.1 1.9 %collective-permute-start.10 = (f32[160,128]{1,0:T(8,128)S(1)}, f32[160,128]{1,0:T(8,128)S(1)}, u32[]{:S(2)}, u32[]{:S(2)}) collective-permute-start(f32[160,128]{1,0:T(8,128)S(1)} %get-tuple-element.61), channel_id=1, source_target_pairs={{0,16},{1,17},{2,18},{3,19},{4,20},{5,21},{6,22},{7,23},{8,24},{9,... | collective-permute-start | bytes 245768 | tf_op jit(solution)/shard_map/ppermute | solution.py:26
  49.0 0.0 collective-permute-done.6.refs_1_
  49.0 0.0 collective-permute-done.8.refs_3_
  49.1 0.5 shard_map.57
  49.6 4.3 %collective-permute-start.9 = (f32[160,128]{1,0:T(8,128)S(1)}, f32[160,128]{1,0:T(8,128)S(1)}, u32[]{:S(2)}, u32[]{:S(2)}) collective-permute-start(f32[160,128]{1,0:T(8,128)S(1)} %get-tuple-element.59), channel_id=1, source_target_pairs={{0,16},{1,17},{2,18},{3,19},{4,20},{5,21},{6,22},{7,23},{8,24},{9,... | collective-permute-start | bytes 245768 | tf_op jit(solution)/shard_map/ppermute | solution.py:26
  53.9 1.9 %collective-permute-done.10.refs_1_ = f32[160,128]{1,0:T(8,128)S(1)} collective-permute-done((f32[160,128]{1,0:T(8,128)S(1)}, f32[160,128]{1,0:T(8,128)S(1)}, u32[]{:S(2)}, u32[]{:S(2)}) %collective-permute-start.10) | collective-permute-done | bytes 81952 | tf_op jit(solution)/shard_map/ppermute | solution.py:26
  55.7 0.1 shard_map.58
  55.9 4.8 %collective-permute-start.11 = (f32[160,128]{1,0:T(8,128)S(1)}, f32[160,128]{1,0:T(8,128)S(1)}, u32[]{:S(2)}, u32[]{:S(2)}) collective-permute-start(f32[160,128]{1,0:T(8,128)S(1)} %get-tuple-element.62.refs_2_), channel_id=1, source_target_pairs={{0,1},{1,0},{2,3},{3,2},{4,5},{5,4},{6,7},{7,6},{8,9},{9,8},{10,11... | collective-permute-start | bytes 245768 | tf_op jit(solution)/shard_map/ppermute | solution.py:26
  60.7 3.8 %collective-permute-start.13 = (f32[96,128]{1,0:T(8,128)S(1)}, f32[96,128]{1,0:T(8,128)S(1)}, u32[]{:S(2)}, u32[]{:S(2)}) collective-permute-start(f32[96,128]{1,0:T(8,128)S(1)} %get-tuple-element.67), channel_id=1, source_target_pairs={{0,32},{1,33},{2,34},{3,35},{4,36},{5,37},{6,38},{7,39},{8,40},{9,... | collective-permute-start | bytes 147464 | tf_op jit(solution)/shard_map/ppermute | solution.py:26
  64.5 0.4 shard_map.59
  65.0 0.0 collective-permute-done.9.refs_1_
  65.0 0.0 collective-permute-done.11.refs_3_
  65.0 0.4 shard_map.60
  65.4 5.4 %collective-permute-start.12 = (f32[64,256]{1,0:T(8,128)S(1)}, f32[64,256]{1,0:T(8,128)S(1)}, u32[]{:S(2)}, u32[]{:S(2)}) collective-permute-start(f32[64,256]{1,0:T(8,128)S(1)} %get-tuple-element.65.refs_2_.refs_0_), channel_id=1, source_target_pairs={{0,32},{1,33},{2,34},{3,35},{4,36},{5,37},{6,38},{7,39},{8,40},{9,... | collective-permute-start | bytes 196616 | tf_op jit(solution)/shard_map/ppermute | solution.py:26
  70.8 0.0 collective-permute-done.13.refs_1_
  70.8 0.1 shard_map.61.refs_4_
  70.9 2.5 %collective-permute-start.14 = (f32[64,256]{1,0:T(8,128)S(1)}, f32[64,256]{1,0:T(8,128)S(1)}, u32[]{:S(2)}, u32[]{:S(2)}) collective-permute-start(f32[64,256]{1,0:T(8,128)S(1)} %shard_map.61.refs_4_), channel_id=1, source_target_pairs={{0,1},{1,0},{2,3},{3,2},{4,5},{5,4},{6,7},{7,6},{8,9},{9,8},{10,11... | collective-permute-start | bytes 196616 | tf_op jit(solution)/shard_map/ppermute | solution.py:26
  73.4 3.0 %collective-permute-start.15 = (f32[32,128]{1,0:T(8,128)S(1)}, f32[32,128]{1,0:T(8,128)S(1)}, u32[]{:S(2)}, u32[]{:S(2)}) collective-permute-start(f32[32,128]{1,0:T(8,128)S(1)} %get-tuple-element.69), channel_id=1, source_target_pairs={{0,6},{1,7},{2,4},{3,5},{4,2},{5,3},{6,0},{7,1},{8,14},{9,15},{10,... | collective-permute-start | bytes 49160 | tf_op jit(solution)/shard_map/ppermute | solution.py:26
  76.4 2.7 %collective-permute-done.15.refs_9_ = f32[32,128]{1,0:T(8,128)S(1)} collective-permute-done((f32[32,128]{1,0:T(8,128)S(1)}, f32[32,128]{1,0:T(8,128)S(1)}, u32[]{:S(2)}, u32[]{:S(2)}) %collective-permute-start.15) | collective-permute-done | bytes 16416 | tf_op jit(solution)/shard_map/ppermute | solution.py:26
  79.1 0.0 collective-permute-done.12.refs_1_
  79.1 0.0 collective-permute-done.14.refs_5_
  79.1 0.4 shard_map.62
  79.5 6.3 %collective-permute-start.16 = (f32[64,384]{1,0:T(8,128)S(1)}, f32[64,384]{1,0:T(8,128)S(1)}, u32[]{:S(2)}, u32[]{:S(2)}) collective-permute-start(f32[64,384]{1,0:T(8,128)S(1)} %get-tuple-element.70.refs_0_), channel_id=1, source_target_pairs={{0,96},{1,97},{2,98},{3,99},{4,100},{5,101},{6,102},{7,103},{8,104... | collective-permute-start | bytes 294920 | tf_op jit(solution)/shard_map/ppermute | solution.py:26
  85.8 1.9 %collective-permute-start.17 = (f32[128,128]{1,0:T(8,128)S(1)}, f32[128,128]{1,0:T(8,128)S(1)}, u32[]{:S(2)}, u32[]{:S(2)}) collective-permute-start(f32[128,128]{1,0:T(8,128)S(1)} %get-tuple-element.71.refs_3_), channel_id=1, source_target_pairs={{0,2},{1,3},{2,0},{3,1},{4,6},{5,7},{6,4},{7,5},{8,10},{9,11},{10,... | collective-permute-start | bytes 196616 | tf_op jit(solution)/shard_map/ppermute | solution.py:26
  87.8 3.1 %collective-permute-done.17.refs_4_ = f32[128,128]{1,0:T(8,128)S(1)} collective-permute-done((f32[128,128]{1,0:T(8,128)S(1)}, f32[128,128]{1,0:T(8,128)S(1)}, u32[]{:S(2)}, u32[]{:S(2)}) %collective-permute-start.17) | collective-permute-done | bytes 65568 | tf_op jit(solution)/shard_map/ppermute | solution.py:26
  90.8 2.6 %collective-permute-done.16.refs_1_ = f32[64,384]{1,0:T(8,128)S(1)} collective-permute-done((f32[64,384]{1,0:T(8,128)S(1)}, f32[64,384]{1,0:T(8,128)S(1)}, u32[]{:S(2)}, u32[]{:S(2)}) %collective-permute-start.16) | collective-permute-done | bytes 98336 | tf_op jit(solution)/shard_map/ppermute | solution.py:26
  93.4 0.4 shard_map.63
  93.8 3.1 %collective-permute-start.19 = (f32[64,256]{1,0:T(8,128)S(1)}, f32[64,256]{1,0:T(8,128)S(1)}, u32[]{:S(2)}, u32[]{:S(2)}) collective-permute-start(f32[64,256]{1,0:T(8,128)S(1)} %get-tuple-element.75.refs_0_), channel_id=1, source_target_pairs={{0,128},{1,129},{2,130},{3,131},{4,132},{5,133},{6,134},{7,135},{8... | collective-permute-start | bytes 196616 | tf_op jit(solution)/shard_map/ppermute | solution.py:26
  96.9 1.9 %collective-permute-done.19.refs_1_ = f32[64,256]{1,0:T(8,128)S(1)} collective-permute-done((f32[64,256]{1,0:T(8,128)S(1)}, f32[64,256]{1,0:T(8,128)S(1)}, u32[]{:S(2)}, u32[]{:S(2)}) %collective-permute-start.19) | collective-permute-done | bytes 65568 | tf_op jit(solution)/shard_map/ppermute | solution.py:26
  98.8 0.4 shard_map.64
  99.2 4.4 %collective-permute-start.20 = (f32[64,128]{1,0:T(8,128)S(1)}, f32[64,128]{1,0:T(8,128)S(1)}, u32[]{:S(2)}, u32[]{:S(2)}) collective-permute-start(f32[64,128]{1,0:T(8,128)S(1)} %get-tuple-element.76.refs_0_), channel_id=1, source_target_pairs={{0,384},{1,385},{2,386},{3,387},{4,388},{5,389},{6,390},{7,391},{8... | collective-permute-start | bytes 98312 | tf_op jit(solution)/shard_map/ppermute | solution.py:26
  103.6 3.8 %collective-permute-start.18 = (f32[256,256]{1,0:T(8,128)S(1)}, f32[256,256]{1,0:T(8,128)S(1)}, u32[]{:S(2)}, u32[]{:S(2)}) collective-permute-start(f32[256,256]{1,0:T(8,128)S(1)} %get-tuple-element.73), channel_id=1, source_target_pairs={{0,1},{1,0},{2,3},{3,2},{4,5},{5,4},{6,7},{7,6},{8,9},{9,8},{10,11... | collective-permute-start | bytes 786440 | tf_op jit(solution)/shard_map/ppermute | solution.py:26
  107.4 0.0 collective-permute-done.20.refs_1_
  107.5 0.3 shard_map.65
  107.8 13.6 %all-gather = f32[512,384]{1,0:T(8,128)S(1)} all-gather(f32[64,384]{1,0:T(8,128)S(1)} %shard_map.65), channel_id=2, replica_groups={{0,1,2,3,4,5,6,7},{8,9,10,11,12,13,14,15},{16,17,18,19,20,21,22,23},{24..., dimensions={0}, use_global_device_ids=true | all-gather | bytes 884736 | tf_op jit(solution)/shard_map/all_gather | solution.py:399
  121.4 0.0 collective-permute-done.18.refs_2_
  121.4 2.5 %shard_map.66 = f32[512,512]{1,0:T(8,128)} custom-call(f32[512,256]{1,0:T(8,128)S(1)} %get-tuple-element.46.refs_0_, f32[512,256]{1,0:T(8,128)S(1)} %get-tuple-element.50.refs_1_, f32[256,256]{1,0:T(8,128)S(1)} %collective-permute-done.18.refs_2_, f32[256,256]{1,0:T(8,128)S(1)} %get-tuple-element.74.refs_3_, f32[8,64,384]{2,1,0:T(8,128)S(1)} %bitcast.3, ...), custom_call_target="tpu_custom_call" | custom-call | flops 900000000 | bytes 3538944 | tf_op jit(solution)/shard_map/pallas_call | solution.py:39
  (8 shorter events, 0.1 us)
Async XLA Ops:
  0.0 11.1 %copy-start = (f32[512,512]{1,0:T(8,128)S(1)}, f32[512,512]{1,0:T(8,128)}, u32[]{:S(2)}) copy-start(f32[512,512]{1,0:T(8,128)} %refs_0_.3) | copy-start | bytes 3145732
  0.0 11.1 %copy-start.1 = (f32[512,512]{1,0:T(8,128)S(1)}, f32[512,512]{1,0:T(8,128)}, u32[]{:S(2)}) copy-start(f32[512,512]{1,0:T(8,128)} %refs_1_.3) | copy-start | bytes 3145732
  0.0 1.4 %copy-start.2 = (f32[512,576]{0,1:T(8,128)S(1)}, f32[512,576]{0,1:T(8,128)}, u32[]{:S(2)}) copy-start(f32[512,576]{0,1:T(8,128)} %param.6) | copy-start | bytes 3538948
  2.3 13.1 %collective-permute-start = (f32[256,512]{1,0:T(8,128)S(1)}, f32[256,512]{1,0:T(8,128)S(1)}, u32[]{:S(2)}, u32[]{:S(2)}) collective-permute-start(f32[256,512]{1,0:T(8,128)S(1)} %get-tuple-element.48), channel_id=1, source_target_pairs={{0,1},{1,0},{2,3},{3,2},{4,5},{5,4},{6,7},{7,6},{8,9},{9,8},{10,11... | collective-permute-start | bytes 1572872 | tf_op jit(solution)/shard_map/ppermute | solution.py:26
  13.3 4.1 %copy-start.3 = (f32[1,9,128,128]{3,2,1,0:T(8,128)S(1)}, f32[1,9,128,128]{3,2,1,0:T(8,128)}, u32[]{:S(2)}) copy-start(f32[1,9,128,128]{3,2,1,0:T(8,128)} %param.7) | copy-start | bytes 1769476
  13.3 6.5 %collective-permute-start.1 = (f32[256,640]{1,0:T(8,128)S(1)}, f32[256,640]{1,0:T(8,128)S(1)}, u32[]{:S(2)}, u32[]{:S(2)}) collective-permute-start(f32[256,640]{1,0:T(8,128)S(1)} %get-tuple-element.49.refs_2_), channel_id=1, source_target_pairs={{0,1},{1,0},{2,3},{3,2},{4,5},{5,4},{6,7},{7,6},{8,9},{9,8},{10,11... | collective-permute-start | bytes 1966088 | tf_op jit(solution)/shard_map/ppermute | solution.py:26
  15.4 11.4 %collective-permute-start.3 = (f32[64,1408]{1,0:T(8,128)S(1)}, f32[64,1408]{1,0:T(8,128)S(1)}, u32[]{:S(2)}, u32[]{:S(2)}) collective-permute-start(f32[64,1408]{1,0:T(8,128)S(1)} %shard_map.48.refs_4_.refs_2_.refs_0_), channel_id=1, source_target_pairs={{0,2},{1,3},{2,0},{3,1},{4,6},{5,7},{6,4},{7,5},{8,10},{9,11},{10,... | collective-permute-start | bytes 1081352 | tf_op jit(solution)/shard_map/ppermute | solution.py:26
  20.4 12.0 %collective-permute-start.2 = (f32[128,512]{1,0:T(8,128)S(1)}, f32[128,512]{1,0:T(8,128)S(1)}, u32[]{:S(2)}, u32[]{:S(2)}) collective-permute-start(f32[128,512]{1,0:T(8,128)S(1)} %get-tuple-element.53.refs_2_), channel_id=1, source_target_pairs={{0,2},{1,3},{2,0},{3,1},{4,6},{5,7},{6,4},{7,5},{8,10},{9,11},{10,... | collective-permute-start | bytes 786440 | tf_op jit(solution)/shard_map/ppermute | solution.py:26
  26.8 8.1 %collective-permute-start.5 = (f32[64,896]{1,0:T(8,128)S(1)}, f32[64,896]{1,0:T(8,128)S(1)}, u32[]{:S(2)}, u32[]{:S(2)}) collective-permute-start(f32[64,896]{1,0:T(8,128)S(1)} %shard_map.53.refs_2_.refs_0_), channel_id=1, source_target_pairs={{0,6},{1,7},{2,4},{3,5},{4,2},{5,3},{6,0},{7,1},{8,14},{9,15},{10,... | collective-permute-start | bytes 688136 | tf_op jit(solution)/shard_map/ppermute | solution.py:26
  33.0 6.9 %collective-permute-start.4 = (f32[64,512]{1,0:T(8,128)S(1)}, f32[64,512]{1,0:T(8,128)S(1)}, u32[]{:S(2)}, u32[]{:S(2)}) collective-permute-start(f32[64,512]{1,0:T(8,128)S(1)} %get-tuple-element.55.refs_2_), channel_id=1, source_target_pairs={{0,6},{1,7},{2,4},{3,5},{4,2},{5,3},{6,0},{7,1},{8,14},{9,15},{10,... | collective-permute-start | bytes 393224 | tf_op jit(solution)/shard_map/ppermute | solution.py:26
  35.0 7.4 %collective-permute-start.7 = (f32[64,512]{1,0:T(8,128)S(1)}, f32[64,512]{1,0:T(8,128)S(1)}, u32[]{:S(2)}, u32[]{:S(2)}) collective-permute-start(f32[64,512]{1,0:T(8,128)S(1)} %shard_map.55.refs_0_), channel_id=1, source_target_pairs={{0,8},{1,9},{2,10},{3,11},{4,12},{5,13},{6,14},{7,15},{8,0},{9,1},... | collective-permute-start | bytes 393224 | tf_op jit(solution)/shard_map/ppermute | solution.py:26
  40.4 8.7 %collective-permute-start.6 = (f32[64,384]{1,0:T(8,128)S(1)}, f32[64,384]{1,0:T(8,128)S(1)}, u32[]{:S(2)}, u32[]{:S(2)}) collective-permute-start(f32[64,384]{1,0:T(8,128)S(1)} %get-tuple-element.56.refs_2_.refs_0_.refs_1_), channel_id=1, source_target_pairs={{0,8},{1,9},{2,10},{3,11},{4,12},{5,13},{6,14},{7,15},{8,0},{9,1},... | collective-permute-start | bytes 294920 | tf_op jit(solution)/shard_map/ppermute | solution.py:26
  42.4 6.6 %collective-permute-start.8 = (f32[64,384]{1,0:T(8,128)S(1)}, f32[64,384]{1,0:T(8,128)S(1)}, u32[]{:S(2)}, u32[]{:S(2)}) collective-permute-start(f32[64,384]{1,0:T(8,128)S(1)} %get-tuple-element.57.refs_2_), channel_id=1, source_target_pairs={{0,1},{1,0},{2,3},{3,2},{4,5},{5,4},{6,7},{7,6},{8,9},{9,8},{10,11... | collective-permute-start | bytes 294920 | tf_op jit(solution)/shard_map/ppermute | solution.py:26
  47.1 8.6 %collective-permute-start.10 = (f32[160,128]{1,0:T(8,128)S(1)}, f32[160,128]{1,0:T(8,128)S(1)}, u32[]{:S(2)}, u32[]{:S(2)}) collective-permute-start(f32[160,128]{1,0:T(8,128)S(1)} %get-tuple-element.61), channel_id=1, source_target_pairs={{0,16},{1,17},{2,18},{3,19},{4,20},{5,21},{6,22},{7,23},{8,24},{9,... | collective-permute-start | bytes 245768 | tf_op jit(solution)/shard_map/ppermute | solution.py:26
  49.6 15.4 %collective-permute-start.9 = (f32[160,128]{1,0:T(8,128)S(1)}, f32[160,128]{1,0:T(8,128)S(1)}, u32[]{:S(2)}, u32[]{:S(2)}) collective-permute-start(f32[160,128]{1,0:T(8,128)S(1)} %get-tuple-element.59), channel_id=1, source_target_pairs={{0,16},{1,17},{2,18},{3,19},{4,20},{5,21},{6,22},{7,23},{8,24},{9,... | collective-permute-start | bytes 245768 | tf_op jit(solution)/shard_map/ppermute | solution.py:26
  55.9 9.1 %collective-permute-start.11 = (f32[160,128]{1,0:T(8,128)S(1)}, f32[160,128]{1,0:T(8,128)S(1)}, u32[]{:S(2)}, u32[]{:S(2)}) collective-permute-start(f32[160,128]{1,0:T(8,128)S(1)} %get-tuple-element.62.refs_2_), channel_id=1, source_target_pairs={{0,1},{1,0},{2,3},{3,2},{4,5},{5,4},{6,7},{7,6},{8,9},{9,8},{10,11... | collective-permute-start | bytes 245768 | tf_op jit(solution)/shard_map/ppermute | solution.py:26
  60.7 10.1 %collective-permute-start.13 = (f32[96,128]{1,0:T(8,128)S(1)}, f32[96,128]{1,0:T(8,128)S(1)}, u32[]{:S(2)}, u32[]{:S(2)}) collective-permute-start(f32[96,128]{1,0:T(8,128)S(1)} %get-tuple-element.67), channel_id=1, source_target_pairs={{0,32},{1,33},{2,34},{3,35},{4,36},{5,37},{6,38},{7,39},{8,40},{9,... | collective-permute-start | bytes 147464 | tf_op jit(solution)/shard_map/ppermute | solution.py:26
  65.4 13.7 %collective-permute-start.12 = (f32[64,256]{1,0:T(8,128)S(1)}, f32[64,256]{1,0:T(8,128)S(1)}, u32[]{:S(2)}, u32[]{:S(2)}) collective-permute-start(f32[64,256]{1,0:T(8,128)S(1)} %get-tuple-element.65.refs_2_.refs_0_), channel_id=1, source_target_pairs={{0,32},{1,33},{2,34},{3,35},{4,36},{5,37},{6,38},{7,39},{8,40},{9,... | collective-permute-start | bytes 196616 | tf_op jit(solution)/shard_map/ppermute | solution.py:26
  70.9 8.2 %collective-permute-start.14 = (f32[64,256]{1,0:T(8,128)S(1)}, f32[64,256]{1,0:T(8,128)S(1)}, u32[]{:S(2)}, u32[]{:S(2)}) collective-permute-start(f32[64,256]{1,0:T(8,128)S(1)} %shard_map.61.refs_4_), channel_id=1, source_target_pairs={{0,1},{1,0},{2,3},{3,2},{4,5},{5,4},{6,7},{7,6},{8,9},{9,8},{10,11... | collective-permute-start | bytes 196616 | tf_op jit(solution)/shard_map/ppermute | solution.py:26
  73.4 5.7 %collective-permute-start.15 = (f32[32,128]{1,0:T(8,128)S(1)}, f32[32,128]{1,0:T(8,128)S(1)}, u32[]{:S(2)}, u32[]{:S(2)}) collective-permute-start(f32[32,128]{1,0:T(8,128)S(1)} %get-tuple-element.69), channel_id=1, source_target_pairs={{0,6},{1,7},{2,4},{3,5},{4,2},{5,3},{6,0},{7,1},{8,14},{9,15},{10,... | collective-permute-start | bytes 49160 | tf_op jit(solution)/shard_map/ppermute | solution.py:26
  79.5 13.9 %collective-permute-start.16 = (f32[64,384]{1,0:T(8,128)S(1)}, f32[64,384]{1,0:T(8,128)S(1)}, u32[]{:S(2)}, u32[]{:S(2)}) collective-permute-start(f32[64,384]{1,0:T(8,128)S(1)} %get-tuple-element.70.refs_0_), channel_id=1, source_target_pairs={{0,96},{1,97},{2,98},{3,99},{4,100},{5,101},{6,102},{7,103},{8,104... | collective-permute-start | bytes 294920 | tf_op jit(solution)/shard_map/ppermute | solution.py:26
  85.8 5.0 %collective-permute-start.17 = (f32[128,128]{1,0:T(8,128)S(1)}, f32[128,128]{1,0:T(8,128)S(1)}, u32[]{:S(2)}, u32[]{:S(2)}) collective-permute-start(f32[128,128]{1,0:T(8,128)S(1)} %get-tuple-element.71.refs_3_), channel_id=1, source_target_pairs={{0,2},{1,3},{2,0},{3,1},{4,6},{5,7},{6,4},{7,5},{8,10},{9,11},{10,... | collective-permute-start | bytes 196616 | tf_op jit(solution)/shard_map/ppermute | solution.py:26
  93.8 5.0 %collective-permute-start.19 = (f32[64,256]{1,0:T(8,128)S(1)}, f32[64,256]{1,0:T(8,128)S(1)}, u32[]{:S(2)}, u32[]{:S(2)}) collective-permute-start(f32[64,256]{1,0:T(8,128)S(1)} %get-tuple-element.75.refs_0_), channel_id=1, source_target_pairs={{0,128},{1,129},{2,130},{3,131},{4,132},{5,133},{6,134},{7,135},{8... | collective-permute-start | bytes 196616 | tf_op jit(solution)/shard_map/ppermute | solution.py:26
  99.2 8.2 %collective-permute-start.20 = (f32[64,128]{1,0:T(8,128)S(1)}, f32[64,128]{1,0:T(8,128)S(1)}, u32[]{:S(2)}, u32[]{:S(2)}) collective-permute-start(f32[64,128]{1,0:T(8,128)S(1)} %get-tuple-element.76.refs_0_), channel_id=1, source_target_pairs={{0,384},{1,385},{2,386},{3,387},{4,388},{5,389},{6,390},{7,391},{8... | collective-permute-start | bytes 98312 | tf_op jit(solution)/shard_map/ppermute | solution.py:26
  103.6 17.8 %collective-permute-start.18 = (f32[256,256]{1,0:T(8,128)S(1)}, f32[256,256]{1,0:T(8,128)S(1)}, u32[]{:S(2)}, u32[]{:S(2)}) collective-permute-start(f32[256,256]{1,0:T(8,128)S(1)} %get-tuple-element.73), channel_id=1, source_target_pairs={{0,1},{1,0},{2,3},{3,2},{4,5},{5,4},{6,7},{7,6},{8,9},{9,8},{10,11... | collective-permute-start | bytes 786440 | tf_op jit(solution)/shard_map/ppermute | solution.py:26

commit v3 on v2

--- a/solution.py
+++ b/solution.py
@@ -117,9 +117,15 @@
 
 
 def gram_core_kernel(keep_ref, got_ref, out_ref):
-    out_ref[:, :512] = keep_ref[192:, :] + got_ref[192:, :]
-    out_ref[:, 512:896] = keep_ref[:64, :384] + got_ref[:64, :384]
-    out_ref[:, 896:] = keep_ref[64:128, :] + got_ref[64:128, :]
+    out_ref[...] = folded(side(
+        keep_ref[192:, :] + got_ref[192:, :],
+        keep_ref[:64, :384] + got_ref[:64, :384],
+        keep_ref[64:128, :448] + got_ref[64:128, :448],
+    ))
+
+
+def gram_y_kernel(own_ref, got_ref, out_ref):
+    out_ref[...] = unfolded(own_ref[...] + got_ref[...])[:, :896]
 
 
 def gram_add_kernel(own_ref, got_ref, out_ref):
@@ -203,7 +209,7 @@
     own, other = own_ref[...], got_ref[...]
     both = solved(own, other, caps_ref[1])
     both_ref[...] = both
-    rest = rest_of(own, other, both, low_ref[:, 896:1344], low_got_ref[:, 896:1344])
+    rest = rest_of(own, other, both, unfolded(low_ref[...])[:, 896:], unfolded(low_got_ref[...])[:, 896:])
     send_ref[:, :448] = either(y_high, rest[64:], rest[:64])
     next_ref[:, :448] = either(y_high, rest[:64], rest[64:])
     send_ref[:, 448:] = jnp.zeros((64, 64), F32)
@@ -278,22 +284,21 @@
     own, other = own_ref[:, :192], got_ref[:, :192]
     both = solved(own, other, caps_ref[6])
     both_ref[...] = both
-    next_ref[:, :128] = rest_of(own, other, both, own_ref[:, 192:320], got_ref[:, 192:320])
-    gram7 = own_ref[:, 320:] + got_ref[:, 320:]
-    next_ref[:, 128:] = side(gram7, gram7)
+    rest = rest_of(own, other, both, own_ref[:, 192:320], got_ref[:, 192:320])
+    next_ref[...] = folded(side(rest, own_ref[:, 320:] + got_ref[:, 320:]))
 
 
 def level7_kernel(own_ref, got_ref, caps_ref, both_ref, next_ref):
-    own, other = own_ref[:, :128], got_ref[:, :128]
+    mine, theirs = unfolded(own_ref[...]), unfolded(got_ref[...])
+    own, other = mine[:, :128], theirs[:, :128]
     both = solved(own, other, caps_ref[7])
     both_ref[...] = both
-    rest = rest_of(own, other, both, own_ref[:, 128:192], got_ref[:, 128:192])
-    next_ref[...] = side(rest, jnp.zeros((64, RANK), F32))
+    next_ref[...] = folded(rest_of(own, other, both, mine[:, 128:], theirs[:, 128:]))
 
 
 def level8_kernel(own_ref, got_ref, both3_ref, both4_ref, both5_ref, both6_ref, both7_ref,
                   caps_ref, out_ref):
-    both = solved(own_ref[:, :RANK], got_ref[:, :RANK], caps_ref[8])
+    both = solved(unfolded(own_ref[...]), unfolded(got_ref[...]), caps_ref[8])
     out_ref[:, :128] = side(both3_ref[:, :RANK], both4_ref[:, :RANK])
     out_ref[:, 128:256] = side(both5_ref[:, :RANK], both6_ref[:, :RANK])
     out_ref[:, 256:] = side(both7_ref[:, :RANK], both[:, :RANK])
@@ -304,17 +309,41 @@
     return y_high << 2 | (part ^ y_high) << 1 | core
 
 
-def final_kernel(theirs_ref, mine_ref, got_ref, own_ref, all_ref, high_ref, low_ref, out_ref):
-    _, core, _, _ = bits()
-    factors = (high_ref[...], low_ref[...])
+def final_kernel(theirs_ref, mine_ref, got_ref, own_ref, all_ref, high_ref, low_ref, out_ref,
+                 block_ref, sems):
+    _, core, _, _ = bits()
     last = [all_ref[place(shard)] for shard in range(8)]
     first, second = stack(*last[:4]), stack(*last[4:])
-    own = side(own_ref[:, :192], either(core, first, second))
-    other = side(got_ref[:, :192], either(core, second, first))
-    own_out = mine_ref[...] - mm3(factors, split(own), NT)
-    other_out = theirs_ref[...] - mm3(factors, split(other), NT)
-    out_ref[:, :256] = either(core, own_out, other_out)
-    out_ref[:, 256:] = either(core, other_out, own_out)
+    own = split(side(own_ref[:, :192], either(core, first, second)))
+    other = split(side(got_ref[:, :192], either(core, second, first)))
+    copies = []
+    for n in range(2):
+        rows = slice(256 * n, 256 * (n + 1))
+        factors = (high_ref[rows, :], low_ref[rows, :])
+        own_out = mine_ref[rows, :] - mm3(factors, own, NT)
+        other_out = theirs_ref[rows, :] - mm3(factors, other, NT)
+        block_ref[n, :, :256] = either(core, own_out, other_out)
+        block_ref[n, :, 256:] = either(core, other_out, own_out)
+        copies.append(
+            pltpu.make_async_copy(block_ref.at[n], out_ref.at[pl.ds(256 * n, 256)], sems.at[n])
+        )
+        copies[n].start()
+    for copy in copies:
+        copy.wait()
+
+
+def final(*args):
+    return pl.pallas_call(
+        final_kernel,
+        out_shape=jax.ShapeDtypeStruct((512, 512), F32),
+        in_specs=[pl.BlockSpec(memory_space=pltpu.VMEM)] * len(args),
+        out_specs=pl.BlockSpec(memory_space=pl.ANY),
+        scratch_shapes=[pltpu.VMEM((2, 256, 512), F32), pltpu.SemaphoreType.DMA((2,))],
+        compiler_params=pltpu.CompilerParams(vmem_limit_bytes=16 * 2**20),
+        cost_estimate=pl.CostEstimate(
+            flops=12 * 75_000_000, bytes_accessed=2**20, transcendentals=0
+        ),
+    )(*args)
 
 
 def local(rhs, leaf_inverse, basis, caps):
@@ -329,7 +358,7 @@
         rhs, leaf_inverse, high, low, flops=6 * 142_000_000, grant=12,
     )
     terms_got = sent(terms_theirs, PARTNER[0])
-    gram1, = call(gram_core_kernel, [(64, 1408)], gram_keep, gram_got, tokens=(terms_theirs,))
+    gram1, = call(gram_core_kernel, [(672, 128)], gram_keep, gram_got, tokens=(terms_theirs,))
     gram1_got = sent(gram1, PARTNER[1])
     iterate_own, terms = call(
         partial(solve_kernel, False), [(512, 256), (256, 640)],
@@ -341,7 +370,7 @@
         terms, terms_got, gram_keep, gram_got, caps,
     )
     got = sent(send1, PARTNER[1])
-    gram2, = call(gram_add_kernel, [(64, 896)], gram1, gram1_got, tokens=(send1,))
+    gram2, = call(gram_y_kernel, [(64, 896)], gram1, gram1_got, tokens=(send1,))
     gram2_got = sent(gram2, PARTNER[2])
     both1, send2, state = call(
         level1_kernel, [(128, 128), (64, 512), (64, 512)], state, got, gram1, gram1_got, caps
@@ -385,23 +414,21 @@
     got = sent(state, PARTNER[6])
     down_got = sent(down, PARTNER[1])
     both6, state, down_send, down_own = call(
-        level6_kernel, [(64, 128), (64, 256), (256, 256), (256, 256)],
+        level6_kernel, [(64, 128), (96, 128), (256, 256), (256, 256)],
         state, got, caps, down, down_got, both1, both0,
     )
     got = sent(state, PARTNER[7])
     down_got = sent(down_send, PARTNER[0])
-    both7, state = call(level7_kernel, [(64, 128), (64, 128)], state, got, caps)
+    both7, state = call(level7_kernel, [(64, 128), (32, 128)], state, got, caps)
     got = sent(state, PARTNER[8])
     last, = call(
         level8_kernel, [(64, 384)], state, got, both3, both4, both5, both6, both7, caps
     )
     octets = [list(range(n, n + 8)) for n in range(0, 512, 8)]
     gathered = lax.all_gather(last, "leaf", axis_index_groups=octets)
-    out, = call(
-        final_kernel, [(512, 512)], iterate_theirs, iterate_own, down_got, down_own, gathered,
-        basis_high, basis_low, flops=12 * 75_000_000, grant=16,
-    )
-    return out
+    return final(
+        iterate_theirs, iterate_own, down_got, down_own, gathered, basis_high, basis_low
+    )
 
 
 def solution(mesh):

time: 125 us -> 124 us (level)
    pallas_call x0 -> x1, Pallas kernels: none -> 2.39 us  [final(): pl.pallas_call(final_kernel, out_shape=jax.ShapeDtypeStruct((512, 512), F...]
    pallas_call x21 -> x20, Pallas kernels: 12.8 us -> 10.4 us  [call(): pl.pallas_call(kernel, out_shape=shapes, in_specs=[vmem] * after, out_spe...]
where the time goes in v3:
time: 124 us; the launch traced here: 123 us
  starting transfers between devices  73.7 us (59%)
  waiting for transfers between devices  21.4 us (17%)
  blocking collectives  13.4 us (11%)
  Pallas kernels  12.8 us (10%)
  local copies, waits for them, and re-layouts  1.43 us (1%)
    ppermute x21, starting transfers between devices, sent(): return lax.ppermute(array, 'leaf', [(i, i ^ mask) for i in range(count)])  73.7 us
    ppermute x21, waiting for transfers between devices, sent(): return lax.ppermute(array, 'leaf', [(i, i ^ mask) for i in range(count)])  21.4 us
    all_gather x1, blocking collectives, local(): gathered = lax.all_gather(last, 'leaf', axis_index_groups=octets)  13.4 us
    pallas_call x20, Pallas kernels, call(): pl.pallas_call(kernel, out_shape=shapes, in_specs=[vmem] * after, out_spe...  10.4 us
  transfers between devices with their start and end apart: 21, of which 8 were waited for; matrix products, arithmetic and copies ran while one was open for 0% of the time, Pallas kernels for 7%

profile of v3, /device:TPU:1, one launch (start us, length us, event | category | flops | bytes accessed | tf_op | source)
XLA Modules:
  0.0 123.2 jit_solution(3970191336452127292)
XLA Ops:
  0.0 1.4 %copy-done.2 = f32[512,576]{0,1:T(8,128)S(1)} copy-done((f32[512,576]{0,1:T(8,128)S(1)}, f32[512,576]{0,1:T(8,128)}, u32[]{:S(2)}) %copy-start.2) | copy-done | bytes 1179672
  1.4 0.9 shard_map.46
  2.3 8.8 %collective-permute-start = (f32[256,512]{1,0:T(8,128)S(1)}, f32[256,512]{1,0:T(8,128)S(1)}, u32[]{:S(2)}, u32[]{:S(2)}) collective-permute-start(f32[256,512]{1,0:T(8,128)S(1)} %get-tuple-element.48), channel_id=1, source_target_pairs={{0,1},{1,0},{2,3},{3,2},{4,5},{5,4},{6,7},{7,6},{8,9},{9,8},{10,11... | collective-permute-start | bytes 1572872 | tf_op jit(solution)/shard_map/ppermute | solution.py:26
  11.1 2.1 %shard_map.47 = (f32[512,256]{1,0:T(8,128)S(1)}, f32[256,640]{1,0:T(8,128)S(1)}) custom-call(f32[512,512]{1,0:T(8,128)S(1)} %copy-done, f32[512,512]{1,0:T(8,128)S(1)} %copy-done.1, bf16[576,512]{1,0:T(8,128)(2,1)S(1)} %get-tuple-element.44.refs_2_, bf16[576,512]{1,0:T(8,128)(2,1)S(1)} %get-tuple-element.45.refs_3_), custom_call_target="tpu_custom_call" | custom-call | flops 852000000 | bytes 3276800 | tf_op jit(solution)/shard_map/pallas_call | solution.py:39
  13.3 0.0 copy-start.3
  13.3 2.1 %collective-permute-start.1 = (f32[256,640]{1,0:T(8,128)S(1)}, f32[256,640]{1,0:T(8,128)S(1)}, u32[]{:S(2)}, u32[]{:S(2)}) collective-permute-start(f32[256,640]{1,0:T(8,128)S(1)} %get-tuple-element.49.refs_2_), channel_id=1, source_target_pairs={{0,1},{1,0},{2,3},{3,2},{4,5},{5,4},{6,7},{7,6},{8,9},{9,8},{10,11... | collective-permute-start | bytes 1966088 | tf_op jit(solution)/shard_map/ppermute | solution.py:26
  15.4 0.0 collective-permute-done.refs_1_.refs_3_
  15.4 0.1 shard_map.48.refs_4_.refs_2_.refs_0_
  15.4 1.9 %collective-permute-start.3 = (f32[672,128]{1,0:T(8,128)S(1)}, f32[672,128]{1,0:T(8,128)S(1)}, u32[]{:S(2)}, u32[]{:S(2)}) collective-permute-start(f32[672,128]{1,0:T(8,128)S(1)} %shard_map.48.refs_4_.refs_2_.refs_0_), channel_id=1, source_target_pairs={{0,2},{1,3},{2,0},{3,1},{4,6},{5,7},{6,4},{7,5},{8,10},{9,11},{10,... | collective-permute-start | bytes 1032200 | tf_op jit(solution)/shard_map/ppermute | solution.py:26
  17.4 0.2 shard_map.50.refs_4_.refs_6_.refs_2_.refs_7_
  17.6 2.2 %shard_map.49 = (f32[512,256]{1,0:T(8,128)S(1)}, f32[256,640]{1,0:T(8,128)S(1)}) custom-call(f32[512,512]{1,0:T(8,128)S(1)} %copy-done, f32[512,512]{1,0:T(8,128)S(1)} %copy-done.1, bf16[576,512]{1,0:T(8,128)(2,1)S(1)} %get-tuple-element.44.refs_2_, bf16[576,512]{1,0:T(8,128)(2,1)S(1)} %get-tuple-element.45.refs_3_, ...), custom_call_target="tpu_custom_call" | custom-call | flops 852000000 | bytes 3276800 | tf_op jit(solution)/shard_map/pallas_call | solution.py:39
  19.8 0.0 collective-permute-done.1.refs_1_
  19.8 0.7 shard_map.51
  20.4 3.4 %collective-permute-start.2 = (f32[128,512]{1,0:T(8,128)S(1)}, f32[128,512]{1,0:T(8,128)S(1)}, u32[]{:S(2)}, u32[]{:S(2)}) collective-permute-start(f32[128,512]{1,0:T(8,128)S(1)} %get-tuple-element.53.refs_2_), channel_id=1, source_target_pairs={{0,2},{1,3},{2,0},{3,1},{4,6},{5,7},{6,4},{7,5},{8,10},{9,11},{10,... | collective-permute-start | bytes 786440 | tf_op jit(solution)/shard_map/ppermute | solution.py:26
  23.8 2.7 %collective-permute-done.3.refs_3_.refs_1_ = f32[672,128]{1,0:T(8,128)S(1)} collective-permute-done((f32[672,128]{1,0:T(8,128)S(1)}, f32[672,128]{1,0:T(8,128)S(1)}, u32[]{:S(2)}, u32[]{:S(2)}) %collective-permute-start.3) | collective-permute-done | bytes 344096 | tf_op jit(solution)/shard_map/ppermute | solution.py:26
  26.5 1.9 %collective-permute-start.5 = (f32[64,896]{1,0:T(8,128)S(1)}, f32[64,896]{1,0:T(8,128)S(1)}, u32[]{:S(2)}, u32[]{:S(2)}) collective-permute-start(f32[64,896]{1,0:T(8,128)S(1)} %shard_map.53.refs_2_.refs_0_), channel_id=1, source_target_pairs={{0,6},{1,7},{2,4},{3,5},{4,2},{5,3},{6,0},{7,1},{8,14},{9,15},{10,... | collective-permute-start | bytes 688136 | tf_op jit(solution)/shard_map/ppermute | solution.py:26
  28.4 3.7 %collective-permute-done.2.refs_1_ = f32[128,512]{1,0:T(8,128)S(1)} collective-permute-done((f32[128,512]{1,0:T(8,128)S(1)}, f32[128,512]{1,0:T(8,128)S(1)}, u32[]{:S(2)}, u32[]{:S(2)}) %collective-permute-start.2) | collective-permute-done | bytes 262176 | tf_op jit(solution)/shard_map/ppermute | solution.py:26
  32.1 0.6 shard_map.52
  32.7 1.9 %collective-permute-start.4 = (f32[64,512]{1,0:T(8,128)S(1)}, f32[64,512]{1,0:T(8,128)S(1)}, u32[]{:S(2)}, u32[]{:S(2)}) collective-permute-start(f32[64,512]{1,0:T(8,128)S(1)} %get-tuple-element.55.refs_2_), channel_id=1, source_target_pairs={{0,6},{1,7},{2,4},{3,5},{4,2},{5,3},{6,0},{7,1},{8,14},{9,15},{10,... | collective-permute-start | bytes 393224 | tf_op jit(solution)/shard_map/ppermute | solution.py:26
  34.6 0.0 collective-permute-done.5.refs_3_.refs_1_
  34.6 1.9 %collective-permute-start.7 = (f32[64,512]{1,0:T(8,128)S(1)}, f32[64,512]{1,0:T(8,128)S(1)}, u32[]{:S(2)}, u32[]{:S(2)}) collective-permute-start(f32[64,512]{1,0:T(8,128)S(1)} %shard_map.55.refs_0_), channel_id=1, source_target_pairs={{0,8},{1,9},{2,10},{3,11},{4,12},{5,13},{6,14},{7,15},{8,0},{9,1},... | collective-permute-start | bytes 393224 | tf_op jit(solution)/shard_map/ppermute | solution.py:26
  36.5 3.0 %collective-permute-done.4.refs_1_ = f32[64,512]{1,0:T(8,128)S(1)} collective-permute-done((f32[64,512]{1,0:T(8,128)S(1)}, f32[64,512]{1,0:T(8,128)S(1)}, u32[]{:S(2)}, u32[]{:S(2)}) %collective-permute-start.4) | collective-permute-done | bytes 131104 | tf_op jit(solution)/shard_map/ppermute | solution.py:26
  39.6 0.5 shard_map.54
  40.1 1.9 %collective-permute-start.6 = (f32[64,384]{1,0:T(8,128)S(1)}, f32[64,384]{1,0:T(8,128)S(1)}, u32[]{:S(2)}, u32[]{:S(2)}) collective-permute-start(f32[64,384]{1,0:T(8,128)S(1)} %get-tuple-element.56.refs_2_.refs_0_.refs_1_), channel_id=1, source_target_pairs={{0,8},{1,9},{2,10},{3,11},{4,12},{5,13},{6,14},{7,15},{8,0},{9,1},... | collective-permute-start | bytes 294920 | tf_op jit(solution)/shard_map/ppermute | solution.py:26
  42.0 0.0 collective-permute-done.7.refs_1_
  42.0 0.1 shard_map.56
  42.1 4.7 %collective-permute-start.8 = (f32[64,384]{1,0:T(8,128)S(1)}, f32[64,384]{1,0:T(8,128)S(1)}, u32[]{:S(2)}, u32[]{:S(2)}) collective-permute-start(f32[64,384]{1,0:T(8,128)S(1)} %get-tuple-element.57.refs_2_), channel_id=1, source_target_pairs={{0,1},{1,0},{2,3},{3,2},{4,5},{5,4},{6,7},{7,6},{8,9},{9,8},{10,11... | collective-permute-start | bytes 294920 | tf_op jit(solution)/shard_map/ppermute | solution.py:26
  46.8 1.9 %collective-permute-start.10 = (f32[160,128]{1,0:T(8,128)S(1)}, f32[160,128]{1,0:T(8,128)S(1)}, u32[]{:S(2)}, u32[]{:S(2)}) collective-permute-start(f32[160,128]{1,0:T(8,128)S(1)} %get-tuple-element.61), channel_id=1, source_target_pairs={{0,16},{1,17},{2,18},{3,19},{4,20},{5,21},{6,22},{7,23},{8,24},{9,... | collective-permute-start | bytes 245768 | tf_op jit(solution)/shard_map/ppermute | solution.py:26
  48.7 0.0 collective-permute-done.6.refs_1_
  48.7 0.0 collective-permute-done.8.refs_3_
  48.7 0.5 shard_map.57
  49.3 4.3 %collective-permute-start.9 = (f32[160,128]{1,0:T(8,128)S(1)}, f32[160,128]{1,0:T(8,128)S(1)}, u32[]{:S(2)}, u32[]{:S(2)}) collective-permute-start(f32[160,128]{1,0:T(8,128)S(1)} %get-tuple-element.59), channel_id=1, source_target_pairs={{0,16},{1,17},{2,18},{3,19},{4,20},{5,21},{6,22},{7,23},{8,24},{9,... | collective-permute-start | bytes 245768 | tf_op jit(solution)/shard_map/ppermute | solution.py:26
  53.5 1.9 %collective-permute-done.10.refs_1_ = f32[160,128]{1,0:T(8,128)S(1)} collective-permute-done((f32[160,128]{1,0:T(8,128)S(1)}, f32[160,128]{1,0:T(8,128)S(1)}, u32[]{:S(2)}, u32[]{:S(2)}) %collective-permute-start.10) | collective-permute-done | bytes 81952 | tf_op jit(solution)/shard_map/ppermute | solution.py:26
  55.4 0.1 shard_map.58
  55.5 4.8 %collective-permute-start.11 = (f32[160,128]{1,0:T(8,128)S(1)}, f32[160,128]{1,0:T(8,128)S(1)}, u32[]{:S(2)}, u32[]{:S(2)}) collective-permute-start(f32[160,128]{1,0:T(8,128)S(1)} %get-tuple-element.62.refs_2_), channel_id=1, source_target_pairs={{0,1},{1,0},{2,3},{3,2},{4,5},{5,4},{6,7},{7,6},{8,9},{9,8},{10,11... | collective-permute-start | bytes 245768 | tf_op jit(solution)/shard_map/ppermute | solution.py:26
  60.4 3.8 %collective-permute-start.13 = (f32[96,128]{1,0:T(8,128)S(1)}, f32[96,128]{1,0:T(8,128)S(1)}, u32[]{:S(2)}, u32[]{:S(2)}) collective-permute-start(f32[96,128]{1,0:T(8,128)S(1)} %get-tuple-element.67), channel_id=1, source_target_pairs={{0,32},{1,33},{2,34},{3,35},{4,36},{5,37},{6,38},{7,39},{8,40},{9,... | collective-permute-start | bytes 147464 | tf_op jit(solution)/shard_map/ppermute | solution.py:26
  64.2 0.4 shard_map.59
  64.6 0.0 collective-permute-done.9.refs_1_
  64.6 0.0 collective-permute-done.11.refs_3_
  64.7 0.4 shard_map.60
  65.1 5.4 %collective-permute-start.12 = (f32[64,256]{1,0:T(8,128)S(1)}, f32[64,256]{1,0:T(8,128)S(1)}, u32[]{:S(2)}, u32[]{:S(2)}) collective-permute-start(f32[64,256]{1,0:T(8,128)S(1)} %get-tuple-element.65.refs_2_.refs_0_), channel_id=1, source_target_pairs={{0,32},{1,33},{2,34},{3,35},{4,36},{5,37},{6,38},{7,39},{8,40},{9,... | collective-permute-start | bytes 196616 | tf_op jit(solution)/shard_map/ppermute | solution.py:26
  70.5 0.0 collective-permute-done.13.refs_1_
  70.5 0.1 shard_map.61.refs_4_
  70.6 2.5 %collective-permute-start.14 = (f32[64,256]{1,0:T(8,128)S(1)}, f32[64,256]{1,0:T(8,128)S(1)}, u32[]{:S(2)}, u32[]{:S(2)}) collective-permute-start(f32[64,256]{1,0:T(8,128)S(1)} %shard_map.61.refs_4_), channel_id=1, source_target_pairs={{0,1},{1,0},{2,3},{3,2},{4,5},{5,4},{6,7},{7,6},{8,9},{9,8},{10,11... | collective-permute-start | bytes 196616 | tf_op jit(solution)/shard_map/ppermute | solution.py:26
  73.1 3.0 %collective-permute-start.15 = (f32[32,128]{1,0:T(8,128)S(1)}, f32[32,128]{1,0:T(8,128)S(1)}, u32[]{:S(2)}, u32[]{:S(2)}) collective-permute-start(f32[32,128]{1,0:T(8,128)S(1)} %get-tuple-element.69), channel_id=1, source_target_pairs={{0,6},{1,7},{2,4},{3,5},{4,2},{5,3},{6,0},{7,1},{8,14},{9,15},{10,... | collective-permute-start | bytes 49160 | tf_op jit(solution)/shard_map/ppermute | solution.py:26
  76.0 2.7 %collective-permute-done.15.refs_9_ = f32[32,128]{1,0:T(8,128)S(1)} collective-permute-done((f32[32,128]{1,0:T(8,128)S(1)}, f32[32,128]{1,0:T(8,128)S(1)}, u32[]{:S(2)}, u32[]{:S(2)}) %collective-permute-start.15) | collective-permute-done | bytes 16416 | tf_op jit(solution)/shard_map/ppermute | solution.py:26
  78.8 0.0 collective-permute-done.12.refs_1_
  78.8 0.0 collective-permute-done.14.refs_5_
  78.8 0.4 shard_map.62
  79.2 6.3 %collective-permute-start.16 = (f32[64,384]{1,0:T(8,128)S(1)}, f32[64,384]{1,0:T(8,128)S(1)}, u32[]{:S(2)}, u32[]{:S(2)}) collective-permute-start(f32[64,384]{1,0:T(8,128)S(1)} %get-tuple-element.70.refs_0_), channel_id=1, source_target_pairs={{0,96},{1,97},{2,98},{3,99},{4,100},{5,101},{6,102},{7,103},{8,104... | collective-permute-start | bytes 294920 | tf_op jit(solution)/shard_map/ppermute | solution.py:26
  85.5 1.9 %collective-permute-start.17 = (f32[128,128]{1,0:T(8,128)S(1)}, f32[128,128]{1,0:T(8,128)S(1)}, u32[]{:S(2)}, u32[]{:S(2)}) collective-permute-start(f32[128,128]{1,0:T(8,128)S(1)} %get-tuple-element.71.refs_3_), channel_id=1, source_target_pairs={{0,2},{1,3},{2,0},{3,1},{4,6},{5,7},{6,4},{7,5},{8,10},{9,11},{10,... | collective-permute-start | bytes 196616 | tf_op jit(solution)/shard_map/ppermute | solution.py:26
  87.4 3.1 %collective-permute-done.17.refs_4_ = f32[128,128]{1,0:T(8,128)S(1)} collective-permute-done((f32[128,128]{1,0:T(8,128)S(1)}, f32[128,128]{1,0:T(8,128)S(1)}, u32[]{:S(2)}, u32[]{:S(2)}) %collective-permute-start.17) | collective-permute-done | bytes 65568 | tf_op jit(solution)/shard_map/ppermute | solution.py:26
  90.5 2.6 %collective-permute-done.16.refs_1_ = f32[64,384]{1,0:T(8,128)S(1)} collective-permute-done((f32[64,384]{1,0:T(8,128)S(1)}, f32[64,384]{1,0:T(8,128)S(1)}, u32[]{:S(2)}, u32[]{:S(2)}) %collective-permute-start.16) | collective-permute-done | bytes 98336 | tf_op jit(solution)/shard_map/ppermute | solution.py:26
  93.1 0.4 shard_map.63
  93.5 3.1 %collective-permute-start.19 = (f32[96,128]{1,0:T(8,128)S(1)}, f32[96,128]{1,0:T(8,128)S(1)}, u32[]{:S(2)}, u32[]{:S(2)}) collective-permute-start(f32[96,128]{1,0:T(8,128)S(1)} %get-tuple-element.75.refs_0_), channel_id=1, source_target_pairs={{0,128},{1,129},{2,130},{3,131},{4,132},{5,133},{6,134},{7,135},{8... | collective-permute-start | bytes 147464 | tf_op jit(solution)/shard_map/ppermute | solution.py:26
  96.6 1.7 %collective-permute-done.19.refs_1_ = f32[96,128]{1,0:T(8,128)S(1)} collective-permute-done((f32[96,128]{1,0:T(8,128)S(1)}, f32[96,128]{1,0:T(8,128)S(1)}, u32[]{:S(2)}, u32[]{:S(2)}) %collective-permute-start.19) | collective-permute-done | bytes 49184 | tf_op jit(solution)/shard_map/ppermute | solution.py:26
  98.3 0.4 shard_map.64
  98.7 4.4 %collective-permute-start.20 = (f32[32,128]{1,0:T(8,128)S(1)}, f32[32,128]{1,0:T(8,128)S(1)}, u32[]{:S(2)}, u32[]{:S(2)}) collective-permute-start(f32[32,128]{1,0:T(8,128)S(1)} %get-tuple-element.76.refs_0_), channel_id=1, source_target_pairs={{0,384},{1,385},{2,386},{3,387},{4,388},{5,389},{6,390},{7,391},{8... | collective-permute-start | bytes 49160 | tf_op jit(solution)/shard_map/ppermute | solution.py:26
  103.2 3.8 %collective-permute-start.18 = (f32[256,256]{1,0:T(8,128)S(1)}, f32[256,256]{1,0:T(8,128)S(1)}, u32[]{:S(2)}, u32[]{:S(2)}) collective-permute-start(f32[256,256]{1,0:T(8,128)S(1)} %get-tuple-element.73), channel_id=1, source_target_pairs={{0,1},{1,0},{2,3},{3,2},{4,5},{5,4},{6,7},{7,6},{8,9},{9,8},{10,11... | collective-permute-start | bytes 786440 | tf_op jit(solution)/shard_map/ppermute | solution.py:26
  107.0 0.0 collective-permute-done.20.refs_1_
  107.0 0.3 shard_map.65
  107.3 13.4 %all-gather = f32[512,384]{1,0:T(8,128)S(1)} all-gather(f32[64,384]{1,0:T(8,128)S(1)} %shard_map.65), channel_id=2, replica_groups={{0,1,2,3,4,5,6,7},{8,9,10,11,12,13,14,15},{16,17,18,19,20,21,22,23},{24..., dimensions={0}, use_global_device_ids=true | all-gather | bytes 884736 | tf_op jit(solution)/shard_map/all_gather | solution.py:428
  120.8 0.0 collective-permute-done.18.got_ref
  120.8 2.4 %shard_map.66 = f32[512,512]{1,0:T(8,128)} custom-call(f32[512,256]{1,0:T(8,128)S(1)} %get-tuple-element.46.theirs_ref, f32[512,256]{1,0:T(8,128)S(1)} %get-tuple-element.50.mine_ref, f32[256,256]{1,0:T(8,128)S(1)} %collective-permute-done.18.got_ref, f32[256,256]{1,0:T(8,128)S(1)} %get-tuple-element.74.own_ref, f32[8,64,384]{2,1,0:T(8,128)S(1)} %bitcast.3, ...), custom_call_target="tpu_custom_call" | custom-call | flops 900000000 | bytes 1048576 | tf_op jit(solution)/shard_map/pallas_call | solution.py:336
  (8 shorter events, 0.1 us)
Async XLA Ops:
  0.0 11.1 %copy-start = (f32[512,512]{1,0:T(8,128)S(1)}, f32[512,512]{1,0:T(8,128)}, u32[]{:S(2)}) copy-start(f32[512,512]{1,0:T(8,128)} %refs_0_.3) | copy-start | bytes 3145732
  0.0 11.1 %copy-start.1 = (f32[512,512]{1,0:T(8,128)S(1)}, f32[512,512]{1,0:T(8,128)}, u32[]{:S(2)}) copy-start(f32[512,512]{1,0:T(8,128)} %refs_1_.3) | copy-start | bytes 3145732
  0.0 1.4 %copy-start.2 = (f32[512,576]{0,1:T(8,128)S(1)}, f32[512,576]{0,1:T(8,128)}, u32[]{:S(2)}) copy-start(f32[512,576]{0,1:T(8,128)} %param.6) | copy-start | bytes 3538948
  2.3 13.1 %collective-permute-start = (f32[256,512]{1,0:T(8,128)S(1)}, f32[256,512]{1,0:T(8,128)S(1)}, u32[]{:S(2)}, u32[]{:S(2)}) collective-permute-start(f32[256,512]{1,0:T(8,128)S(1)} %get-tuple-element.48), channel_id=1, source_target_pairs={{0,1},{1,0},{2,3},{3,2},{4,5},{5,4},{6,7},{7,6},{8,9},{9,8},{10,11... | collective-permute-start | bytes 1572872 | tf_op jit(solution)/shard_map/ppermute | solution.py:26
  13.3 4.1 %copy-start.3 = (f32[1,9,128,128]{3,2,1,0:T(8,128)S(1)}, f32[1,9,128,128]{3,2,1,0:T(8,128)}, u32[]{:S(2)}) copy-start(f32[1,9,128,128]{3,2,1,0:T(8,128)} %param.7) | copy-start | bytes 1769476
  13.3 6.5 %collective-permute-start.1 = (f32[256,640]{1,0:T(8,128)S(1)}, f32[256,640]{1,0:T(8,128)S(1)}, u32[]{:S(2)}, u32[]{:S(2)}) collective-permute-start(f32[256,640]{1,0:T(8,128)S(1)} %get-tuple-element.49.refs_2_), channel_id=1, source_target_pairs={{0,1},{1,0},{2,3},{3,2},{4,5},{5,4},{6,7},{7,6},{8,9},{9,8},{10,11... | collective-permute-start | bytes 1966088 | tf_op jit(solution)/shard_map/ppermute | solution.py:26
  15.4 11.0 %collective-permute-start.3 = (f32[672,128]{1,0:T(8,128)S(1)}, f32[672,128]{1,0:T(8,128)S(1)}, u32[]{:S(2)}, u32[]{:S(2)}) collective-permute-start(f32[672,128]{1,0:T(8,128)S(1)} %shard_map.48.refs_4_.refs_2_.refs_0_), channel_id=1, source_target_pairs={{0,2},{1,3},{2,0},{3,1},{4,6},{5,7},{6,4},{7,5},{8,10},{9,11},{10,... | collective-permute-start | bytes 1032200 | tf_op jit(solution)/shard_map/ppermute | solution.py:26
  20.4 11.7 %collective-permute-start.2 = (f32[128,512]{1,0:T(8,128)S(1)}, f32[128,512]{1,0:T(8,128)S(1)}, u32[]{:S(2)}, u32[]{:S(2)}) collective-permute-start(f32[128,512]{1,0:T(8,128)S(1)} %get-tuple-element.53.refs_2_), channel_id=1, source_target_pairs={{0,2},{1,3},{2,0},{3,1},{4,6},{5,7},{6,4},{7,5},{8,10},{9,11},{10,... | collective-permute-start | bytes 786440 | tf_op jit(solution)/shard_map/ppermute | solution.py:26
  26.5 8.1 %collective-permute-start.5 = (f32[64,896]{1,0:T(8,128)S(1)}, f32[64,896]{1,0:T(8,128)S(1)}, u32[]{:S(2)}, u32[]{:S(2)}) collective-permute-start(f32[64,896]{1,0:T(8,128)S(1)} %shard_map.53.refs_2_.refs_0_), channel_id=1, source_target_pairs={{0,6},{1,7},{2,4},{3,5},{4,2},{5,3},{6,0},{7,1},{8,14},{9,15},{10,... | collective-permute-start | bytes 688136 | tf_op jit(solution)/shard_map/ppermute | solution.py:26
  32.7 6.9 %collective-permute-start.4 = (f32[64,512]{1,0:T(8,128)S(1)}, f32[64,512]{1,0:T(8,128)S(1)}, u32[]{:S(2)}, u32[]{:S(2)}) collective-permute-start(f32[64,512]{1,0:T(8,128)S(1)} %get-tuple-element.55.refs_2_), channel_id=1, source_target_pairs={{0,6},{1,7},{2,4},{3,5},{4,2},{5,3},{6,0},{7,1},{8,14},{9,15},{10,... | collective-permute-start | bytes 393224 | tf_op jit(solution)/shard_map/ppermute | solution.py:26
  34.6 7.4 %collective-permute-start.7 = (f32[64,512]{1,0:T(8,128)S(1)}, f32[64,512]{1,0:T(8,128)S(1)}, u32[]{:S(2)}, u32[]{:S(2)}) collective-permute-start(f32[64,512]{1,0:T(8,128)S(1)} %shard_map.55.refs_0_), channel_id=1, source_target_pairs={{0,8},{1,9},{2,10},{3,11},{4,12},{5,13},{6,14},{7,15},{8,0},{9,1},... | collective-permute-start | bytes 393224 | tf_op jit(solution)/shard_map/ppermute | solution.py:26
  40.1 8.7 %collective-permute-start.6 = (f32[64,384]{1,0:T(8,128)S(1)}, f32[64,384]{1,0:T(8,128)S(1)}, u32[]{:S(2)}, u32[]{:S(2)}) collective-permute-start(f32[64,384]{1,0:T(8,128)S(1)} %get-tuple-element.56.refs_2_.refs_0_.refs_1_), channel_id=1, source_target_pairs={{0,8},{1,9},{2,10},{3,11},{4,12},{5,13},{6,14},{7,15},{8,0},{9,1},... | collective-permute-start | bytes 294920 | tf_op jit(solution)/shard_map/ppermute | solution.py:26
  42.1 6.6 %collective-permute-start.8 = (f32[64,384]{1,0:T(8,128)S(1)}, f32[64,384]{1,0:T(8,128)S(1)}, u32[]{:S(2)}, u32[]{:S(2)}) collective-permute-start(f32[64,384]{1,0:T(8,128)S(1)} %get-tuple-element.57.refs_2_), channel_id=1, source_target_pairs={{0,1},{1,0},{2,3},{3,2},{4,5},{5,4},{6,7},{7,6},{8,9},{9,8},{10,11... | collective-permute-start | bytes 294920 | tf_op jit(solution)/shard_map/ppermute | solution.py:26
  46.8 8.6 %collective-permute-start.10 = (f32[160,128]{1,0:T(8,128)S(1)}, f32[160,128]{1,0:T(8,128)S(1)}, u32[]{:S(2)}, u32[]{:S(2)}) collective-permute-start(f32[160,128]{1,0:T(8,128)S(1)} %get-tuple-element.61), channel_id=1, source_target_pairs={{0,16},{1,17},{2,18},{3,19},{4,20},{5,21},{6,22},{7,23},{8,24},{9,... | collective-permute-start | bytes 245768 | tf_op jit(solution)/shard_map/ppermute | solution.py:26
  49.3 15.4 %collective-permute-start.9 = (f32[160,128]{1,0:T(8,128)S(1)}, f32[160,128]{1,0:T(8,128)S(1)}, u32[]{:S(2)}, u32[]{:S(2)}) collective-permute-start(f32[160,128]{1,0:T(8,128)S(1)} %get-tuple-element.59), channel_id=1, source_target_pairs={{0,16},{1,17},{2,18},{3,19},{4,20},{5,21},{6,22},{7,23},{8,24},{9,... | collective-permute-start | bytes 245768 | tf_op jit(solution)/shard_map/ppermute | solution.py:26
  55.5 9.1 %collective-permute-start.11 = (f32[160,128]{1,0:T(8,128)S(1)}, f32[160,128]{1,0:T(8,128)S(1)}, u32[]{:S(2)}, u32[]{:S(2)}) collective-permute-start(f32[160,128]{1,0:T(8,128)S(1)} %get-tuple-element.62.refs_2_), channel_id=1, source_target_pairs={{0,1},{1,0},{2,3},{3,2},{4,5},{5,4},{6,7},{7,6},{8,9},{9,8},{10,11... | collective-permute-start | bytes 245768 | tf_op jit(solution)/shard_map/ppermute | solution.py:26
  60.4 10.1 %collective-permute-start.13 = (f32[96,128]{1,0:T(8,128)S(1)}, f32[96,128]{1,0:T(8,128)S(1)}, u32[]{:S(2)}, u32[]{:S(2)}) collective-permute-start(f32[96,128]{1,0:T(8,128)S(1)} %get-tuple-element.67), channel_id=1, source_target_pairs={{0,32},{1,33},{2,34},{3,35},{4,36},{5,37},{6,38},{7,39},{8,40},{9,... | collective-permute-start | bytes 147464 | tf_op jit(solution)/shard_map/ppermute | solution.py:26
  65.1 13.7 %collective-permute-start.12 = (f32[64,256]{1,0:T(8,128)S(1)}, f32[64,256]{1,0:T(8,128)S(1)}, u32[]{:S(2)}, u32[]{:S(2)}) collective-permute-start(f32[64,256]{1,0:T(8,128)S(1)} %get-tuple-element.65.refs_2_.refs_0_), channel_id=1, source_target_pairs={{0,32},{1,33},{2,34},{3,35},{4,36},{5,37},{6,38},{7,39},{8,40},{9,... | collective-permute-start | bytes 196616 | tf_op jit(solution)/shard_map/ppermute | solution.py:26
  70.6 8.2 %collective-permute-start.14 = (f32[64,256]{1,0:T(8,128)S(1)}, f32[64,256]{1,0:T(8,128)S(1)}, u32[]{:S(2)}, u32[]{:S(2)}) collective-permute-start(f32[64,256]{1,0:T(8,128)S(1)} %shard_map.61.refs_4_), channel_id=1, source_target_pairs={{0,1},{1,0},{2,3},{3,2},{4,5},{5,4},{6,7},{7,6},{8,9},{9,8},{10,11... | collective-permute-start | bytes 196616 | tf_op jit(solution)/shard_map/ppermute | solution.py:26
  73.1 5.7 %collective-permute-start.15 = (f32[32,128]{1,0:T(8,128)S(1)}, f32[32,128]{1,0:T(8,128)S(1)}, u32[]{:S(2)}, u32[]{:S(2)}) collective-permute-start(f32[32,128]{1,0:T(8,128)S(1)} %get-tuple-element.69), channel_id=1, source_target_pairs={{0,6},{1,7},{2,4},{3,5},{4,2},{5,3},{6,0},{7,1},{8,14},{9,15},{10,... | collective-permute-start | bytes 49160 | tf_op jit(solution)/shard_map/ppermute | solution.py:26
  79.2 13.9 %collective-permute-start.16 = (f32[64,384]{1,0:T(8,128)S(1)}, f32[64,384]{1,0:T(8,128)S(1)}, u32[]{:S(2)}, u32[]{:S(2)}) collective-permute-start(f32[64,384]{1,0:T(8,128)S(1)} %get-tuple-element.70.refs_0_), channel_id=1, source_target_pairs={{0,96},{1,97},{2,98},{3,99},{4,100},{5,101},{6,102},{7,103},{8,104... | collective-permute-start | bytes 294920 | tf_op jit(solution)/shard_map/ppermute | solution.py:26
  85.5 5.0 %collective-permute-start.17 = (f32[128,128]{1,0:T(8,128)S(1)}, f32[128,128]{1,0:T(8,128)S(1)}, u32[]{:S(2)}, u32[]{:S(2)}) collective-permute-start(f32[128,128]{1,0:T(8,128)S(1)} %get-tuple-element.71.refs_3_), channel_id=1, source_target_pairs={{0,2},{1,3},{2,0},{3,1},{4,6},{5,7},{6,4},{7,5},{8,10},{9,11},{10,... | collective-permute-start | bytes 196616 | tf_op jit(solution)/shard_map/ppermute | solution.py:26
  93.5 4.8 %collective-permute-start.19 = (f32[96,128]{1,0:T(8,128)S(1)}, f32[96,128]{1,0:T(8,128)S(1)}, u32[]{:S(2)}, u32[]{:S(2)}) collective-permute-start(f32[96,128]{1,0:T(8,128)S(1)} %get-tuple-element.75.refs_0_), channel_id=1, source_target_pairs={{0,128},{1,129},{2,130},{3,131},{4,132},{5,133},{6,134},{7,135},{8... | collective-permute-start | bytes 147464 | tf_op jit(solution)/shard_map/ppermute | solution.py:26
  98.7 8.3 %collective-permute-start.20 = (f32[32,128]{1,0:T(8,128)S(1)}, f32[32,128]{1,0:T(8,128)S(1)}, u32[]{:S(2)}, u32[]{:S(2)}) collective-permute-start(f32[32,128]{1,0:T(8,128)S(1)} %get-tuple-element.76.refs_0_), channel_id=1, source_target_pairs={{0,384},{1,385},{2,386},{3,387},{4,388},{5,389},{6,390},{7,391},{8... | collective-permute-start | bytes 49160 | tf_op jit(solution)/shard_map/ppermute | solution.py:26
  103.2 17.6 %collective-permute-start.18 = (f32[256,256]{1,0:T(8,128)S(1)}, f32[256,256]{1,0:T(8,128)S(1)}, u32[]{:S(2)}, u32[]{:S(2)}) collective-permute-start(f32[256,256]{1,0:T(8,128)S(1)} %get-tuple-element.73), channel_id=1, source_target_pairs={{0,1},{1,0},{2,3},{3,2},{4,5},{5,4},{6,7},{7,6},{8,9},{9,8},{10,11... | collective-permute-start | bytes 786440 | tf_op jit(solution)/shard_map/ppermute | solution.py:26

commit v4 on v3

--- a/solution.py
+++ b/solution.py
@@ -76,16 +76,16 @@
 
 
 def folded(x):
-    full = x.shape[1] // 128
+    rows, full = x.shape[0], x.shape[1] // 128
     parts = [x[:, 128 * i : 128 * (i + 1)] for i in range(full)]
     last = x[:, 128 * full :]
-    return stack(*parts, side(last[:32], last[32:]))
-
-
-def unfolded(x):
-    full = x.shape[0] // 64
-    parts = [x[64 * i : 64 * (i + 1)] for i in range(full)]
-    last = x[64 * full :]
+    return stack(*parts, side(last[: rows // 2], last[rows // 2 :]))
+
+
+def unfolded(x, rows=64):
+    full = x.shape[0] // rows
+    parts = [x[rows * i : rows * (i + 1)] for i in range(full)]
+    last = x[rows * full :]
     return side(*parts, stack(last[:, :64], last[:, 64:]))
 
 
@@ -238,10 +238,8 @@
     send_ref[...] = folded(rest)
 
 
-def level4_kernel(own_ref, got_ref, swap_ref, swap_got_ref, caps_ref, both2_ref, both_ref,
-                  next_ref, down_ref):
-    _, core, _, _ = bits()
-    down_ref[...] = folded(both2_ref[:, RANK:])
+def level4_kernel(own_ref, got_ref, swap_ref, swap_got_ref, caps_ref, both_ref, next_ref):
+    _, core, _, _ = bits()
     own, other = own_ref[...], unfolded(got_ref[...])
     both = solved(own, other, caps_ref[4])
     both_ref[...] = both
@@ -253,12 +251,9 @@
 
 
 def level5_kernel(own_ref, got_ref, swap4_ref, swap4_got_ref, swap_ref, swap_got_ref, caps_ref,
-                  both2_ref, both1_ref, down_got_ref, both_ref, next_ref, down_ref):
-    _, core, _, y_high = bits()
-    mine, got = both2_ref[:, :RANK], unfolded(down_got_ref[...])
-    down_ref[...] = side(
-        both1_ref[:, RANK:], either(y_high, stack(mine, got), stack(got, mine))
-    )
+                  both0_ref, both_ref, next_ref, down_ref):
+    _, core, _, _ = bits()
+    down_ref[...] = folded(both0_ref[:, RANK:])
     own, other = own_ref[...], got_ref[...]
     both = solved(own, other, caps_ref[5])
     both_ref[...] = both
@@ -272,15 +267,7 @@
     next_ref[...] = side(rest, a[:, 128:192], b[:, 128:192], a[:, 64:128])
 
 
-def level6_kernel(own_ref, got_ref, caps_ref, down_mine_ref, down_got_ref, both1_ref, both0_ref,
-                  both_ref, next_ref, down_send_ref, down_own_ref):
-    _, _, part, _ = bits()
-    mine = side(both1_ref[:, :RANK], down_mine_ref[:, RANK:])
-    theirs = down_got_ref[...]
-    rows = either(part, stack(mine, theirs), stack(theirs, mine))
-    fill = jnp.zeros((256, RANK), F32)
-    down_send_ref[...] = side(both0_ref[:, RANK:], rows, fill)
-    down_own_ref[...] = side(both0_ref[:, :RANK], rows, fill)
+def level6_kernel(own_ref, got_ref, caps_ref, both_ref, next_ref):
     own, other = own_ref[:, :192], got_ref[:, :192]
     both = solved(own, other, caps_ref[6])
     both_ref[...] = both
@@ -296,12 +283,15 @@
     next_ref[...] = folded(rest_of(own, other, both, mine[:, 128:], theirs[:, 128:]))
 
 
-def level8_kernel(own_ref, got_ref, both3_ref, both4_ref, both5_ref, both6_ref, both7_ref,
-                  caps_ref, out_ref):
+def level8_kernel(own_ref, got_ref, both1_ref, both2_ref, both3_ref, both4_ref, both5_ref,
+                  both6_ref, both7_ref, caps_ref, out_ref):
     both = solved(unfolded(own_ref[...]), unfolded(got_ref[...]), caps_ref[8])
     out_ref[:, :128] = side(both3_ref[:, :RANK], both4_ref[:, :RANK])
     out_ref[:, 128:256] = side(both5_ref[:, :RANK], both6_ref[:, :RANK])
-    out_ref[:, 256:] = side(both7_ref[:, :RANK], both[:, :RANK])
+    out_ref[:, 256:384] = side(both7_ref[:, :RANK], both[:, :RANK])
+    out_ref[:, 384:512] = both2_ref[...]
+    out_ref[:, 512:640] = both1_ref[:64, :]
+    out_ref[:, 640:] = both1_ref[64:, :]
 
 
 def place(shard):
@@ -309,13 +299,24 @@
     return y_high << 2 | (part ^ y_high) << 1 | core
 
 
-def final_kernel(theirs_ref, mine_ref, got_ref, own_ref, all_ref, high_ref, low_ref, out_ref,
+def final_kernel(theirs_ref, mine_ref, got_ref, both0_ref, all_ref, high_ref, low_ref, out_ref,
                  block_ref, sems):
-    _, core, _, _ = bits()
-    last = [all_ref[place(shard)] for shard in range(8)]
-    first, second = stack(*last[:4]), stack(*last[4:])
-    own = split(side(own_ref[:, :192], either(core, first, second)))
-    other = split(side(got_ref[:, :192], either(core, second, first)))
+    _, core, part, y_high = bits()
+    halves = []
+    for c in range(2):
+        rows = []
+        for b1 in range(2):
+            quad = all_ref[y_high << 2 | (b1 ^ y_high) << 1 | c]
+            for b2 in range(2):
+                level1 = quad[:, 512 + 128 * b2 : 640 + 128 * b2]
+                level1 = either(part ^ b1, level1[:, :RANK], level1[:, RANK:])
+                block = all_ref[place(4 * c + 2 * b1 + b2)]
+                level2 = either(y_high ^ b2, block[:, 384:448], block[:, 448:512])
+                rows.append(side(level1, level2, block[:, :384]))
+        halves.append(stack(*rows))
+    first, second = halves
+    own = split(side(both0_ref[:, :RANK], either(core, first, second)))
+    other = split(side(unfolded(got_ref[...], 256), either(core, second, first)))
     copies = []
     for n in range(2):
         rows = slice(256 * n, 256 * (n + 1))
@@ -399,35 +400,33 @@
     )
     swap4_got = sent(swap4, PARTNER[0])
     grams = gram, sent(going, PARTNER[5])
-    both4, state, down = call(
-        level4_kernel, [(64, 128), (64, 256), (32, 128)],
-        state, got, swap4, swap4_got, caps, both2, tokens=(basis_low,),
-    )
-    down_got = sent(down, PARTNER[2])
+    both4, state = call(
+        level4_kernel, [(64, 128), (64, 256)],
+        state, got, swap4, swap4_got, caps, tokens=(basis_low,),
+    )
     got = sent(state, PARTNER[5])
     swap, = call(partial(gram_level_kernel, 5), GRAM_OUTS[5], *grams, tokens=(state,))
     swap_got = sent(swap, PARTNER[0])
     both5, state, down = call(
         level5_kernel, [(64, 128), (64, 384), (128, 128)],
-        state, got, swap4, swap4_got, swap, swap_got, caps, both2, both1, down_got,
+        state, got, swap4, swap4_got, swap, swap_got, caps, both0,
     )
     got = sent(state, PARTNER[6])
-    down_got = sent(down, PARTNER[1])
-    both6, state, down_send, down_own = call(
-        level6_kernel, [(64, 128), (96, 128), (256, 256), (256, 256)],
-        state, got, caps, down, down_got, both1, both0,
+    down_got = sent(down, PARTNER[0])
+    both6, state = call(
+        level6_kernel, [(64, 128), (96, 128)], state, got, caps, tokens=(down_got,)
     )
     got = sent(state, PARTNER[7])
-    down_got = sent(down_send, PARTNER[0])
     both7, state = call(level7_kernel, [(64, 128), (32, 128)], state, got, caps)
     got = sent(state, PARTNER[8])
     last, = call(
-        level8_kernel, [(64, 384)], state, got, both3, both4, both5, both6, both7, caps
+        level8_kernel, [(64, 768)],
+        state, got, both1, both2, both3, both4, both5, both6, both7, caps,
     )
     octets = [list(range(n, n + 8)) for n in range(0, 512, 8)]
     gathered = lax.all_gather(last, "leaf", axis_index_groups=octets)
     return final(
-        iterate_theirs, iterate_own, down_got, down_own, gathered, basis_high, basis_low
+        iterate_theirs, iterate_own, down_got, both0, gathered, basis_high, basis_low
     )
 
 

time: 124 us -> 163 us (1.31)
  waiting for transfers between devices: 21.4 us -> 62 us
  between operations: 0.38 us -> 13.8 us
  blocking collectives: 13.4 us -> 0 us
  starting transfers between devices: 73.7 us -> 70.5 us
    all_gather x0 -> x1, waiting for transfers between devices: none -> 38.4 us  [local(): gathered = lax.all_gather(last, 'leaf', axis_index_groups=octets)]
    all_gather x1 -> x0, blocking collectives: 13.4 us -> none  [local(): gathered = lax.all_gather(last, 'leaf', axis_index_groups=octets)]
    ppermute x21 -> x19, starting transfers between devices: 73.7 us -> 70.5 us  [sent(): return lax.ppermute(array, 'leaf', [(i, i ^ mask) for i in range(count)])]
    ppermute x21 -> x19, waiting for transfers between devices: 21.4 us -> 23.5 us  [sent(): return lax.ppermute(array, 'leaf', [(i, i ^ mask) for i in range(count)])]
  transfers between devices with their start and end apart: 21 -> 20, of which waited for: 8 -> 10; matrix products, arithmetic and copies ran while one was open for 0% -> 0% of each run, Pallas kernels for 7% -> 5%
where the time goes in v4:
time: 163 us
  starting transfers between devices  70.5 us (43%)
  waiting for transfers between devices  62 us (38%)
  Pallas kernels  13.8 us (8%)
  between operations  13.8 us (8%)
  local copies, waits for them, and re-layouts  2.84 us (2%)
    ppermute x19, starting transfers between devices, sent(): return lax.ppermute(array, 'leaf', [(i, i ^ mask) for i in range(count)])  70.5 us
    all_gather x1, waiting for transfers between devices, local(): gathered = lax.all_gather(last, 'leaf', axis_index_groups=octets)  38.4 us
    ppermute x19, waiting for transfers between devices, sent(): return lax.ppermute(array, 'leaf', [(i, i ^ mask) for i in range(count)])  23.5 us
    pallas_call x20, Pallas kernels, call(): pl.pallas_call(kernel, out_shape=shapes, in_specs=[vmem] * after, out_spe...  11.1 us
  transfers between devices with their start and end apart: 20, of which 10 were waited for; matrix products, arithmetic and copies ran while one was open for 0% of the time, Pallas kernels for 5%

profile of v4, /device:TPU:1, one launch (start us, length us, event | category | flops | bytes accessed | tf_op | source)
XLA Modules:
  0.0 162.9 jit_solution(16133353026251837071)
XLA Ops:
  6.5 1.4 copy-done.3
  8.0 0.9 shard_map.46
  8.8 8.8 %collective-permute-start = (f32[256,512]{1,0:T(8,128)S(1)}, f32[256,512]{1,0:T(8,128)S(1)}, u32[]{:S(2)}, u32[]{:S(2)}) collective-permute-start(f32[256,512]{1,0:T(8,128)S(1)} %get-tuple-element.45), channel_id=1, source_target_pairs={{0,1},{1,0},{2,3},{3,2},{4,5},{5,4},{6,7},{7,6},{8,9},{9,8},{10,11... | collective-permute-start | bytes 1572872 | tf_op jit(solution)/shard_map/ppermute | solution.py:26
  17.6 0.0 copy-done
  17.7 0.0 copy-done.1
  17.7 2.1 %shard_map.47 = (f32[512,256]{1,0:T(8,128)S(1)}, f32[256,640]{1,0:T(8,128)S(1)}) custom-call(f32[512,512]{1,0:T(8,128)S(1)} %copy-done, f32[512,512]{1,0:T(8,128)S(1)} %copy-done.1, bf16[576,512]{1,0:T(8,128)(2,1)S(1)} %get-tuple-element.41.refs_2_, bf16[576,512]{1,0:T(8,128)(2,1)S(1)} %get-tuple-element.42.refs_3_), custom_call_target="tpu_custom_call" | custom-call | flops 852000000 | bytes 3276800 | tf_op jit(solution)/shard_map/pallas_call | solution.py:39
  19.8 0.0 copy-start.4
  19.8 2.1 %collective-permute-start.1 = (f32[256,640]{1,0:T(8,128)S(1)}, f32[256,640]{1,0:T(8,128)S(1)}, u32[]{:S(2)}, u32[]{:S(2)}) collective-permute-start(f32[256,640]{1,0:T(8,128)S(1)} %get-tuple-element.46.refs_2_), channel_id=1, source_target_pairs={{0,1},{1,0},{2,3},{3,2},{4,5},{5,4},{6,7},{7,6},{8,9},{9,8},{10,11... | collective-permute-start | bytes 1966088 | tf_op jit(solution)/shard_map/ppermute | solution.py:26
  21.9 0.0 collective-permute-done.refs_1_.refs_3_
  21.9 0.1 shard_map.48.refs_4_.refs_2_.refs_0_
  22.0 1.9 %collective-permute-start.3 = (f32[672,128]{1,0:T(8,128)S(1)}, f32[672,128]{1,0:T(8,128)S(1)}, u32[]{:S(2)}, u32[]{:S(2)}) collective-permute-start(f32[672,128]{1,0:T(8,128)S(1)} %shard_map.48.refs_4_.refs_2_.refs_0_), channel_id=1, source_target_pairs={{0,2},{1,3},{2,0},{3,1},{4,6},{5,7},{6,4},{7,5},{8,10},{9,11},{10,... | collective-permute-start | bytes 1032200 | tf_op jit(solution)/shard_map/ppermute | solution.py:26
  23.9 0.2 shard_map.50.refs_4_.refs_6_.refs_2_.refs_9_
  24.1 2.2 %shard_map.49 = (f32[512,256]{1,0:T(8,128)S(1)}, f32[256,640]{1,0:T(8,128)S(1)}) custom-call(f32[512,512]{1,0:T(8,128)S(1)} %copy-done, f32[512,512]{1,0:T(8,128)S(1)} %copy-done.1, bf16[576,512]{1,0:T(8,128)(2,1)S(1)} %get-tuple-element.41.refs_2_, bf16[576,512]{1,0:T(8,128)(2,1)S(1)} %get-tuple-element.42.refs_3_, ...), custom_call_target="tpu_custom_call" | custom-call | flops 852000000 | bytes 3276800 | tf_op jit(solution)/shard_map/pallas_call | solution.py:39
  26.3 0.0 collective-permute-done.1.refs_1_
  26.3 0.7 shard_map.51
  27.0 3.4 %collective-permute-start.2 = (f32[128,512]{1,0:T(8,128)S(1)}, f32[128,512]{1,0:T(8,128)S(1)}, u32[]{:S(2)}, u32[]{:S(2)}) collective-permute-start(f32[128,512]{1,0:T(8,128)S(1)} %get-tuple-element.50.refs_2_), channel_id=1, source_target_pairs={{0,2},{1,3},{2,0},{3,1},{4,6},{5,7},{6,4},{7,5},{8,10},{9,11},{10,... | collective-permute-start | bytes 786440 | tf_op jit(solution)/shard_map/ppermute | solution.py:26
  30.3 2.7 %collective-permute-done.3.refs_3_.refs_1_ = f32[672,128]{1,0:T(8,128)S(1)} collective-permute-done((f32[672,128]{1,0:T(8,128)S(1)}, f32[672,128]{1,0:T(8,128)S(1)}, u32[]{:S(2)}, u32[]{:S(2)}) %collective-permute-start.3) | collective-permute-done | bytes 344096 | tf_op jit(solution)/shard_map/ppermute | solution.py:26
  33.0 1.9 %collective-permute-start.5 = (f32[64,896]{1,0:T(8,128)S(1)}, f32[64,896]{1,0:T(8,128)S(1)}, u32[]{:S(2)}, u32[]{:S(2)}) collective-permute-start(f32[64,896]{1,0:T(8,128)S(1)} %shard_map.53.refs_2_.refs_0_), channel_id=1, source_target_pairs={{0,6},{1,7},{2,4},{3,5},{4,2},{5,3},{6,0},{7,1},{8,14},{9,15},{10,... | collective-permute-start | bytes 688136 | tf_op jit(solution)/shard_map/ppermute | solution.py:26
  35.0 3.7 %collective-permute-done.2.refs_1_ = f32[128,512]{1,0:T(8,128)S(1)} collective-permute-done((f32[128,512]{1,0:T(8,128)S(1)}, f32[128,512]{1,0:T(8,128)S(1)}, u32[]{:S(2)}, u32[]{:S(2)}) %collective-permute-start.2) | collective-permute-done | bytes 262176 | tf_op jit(solution)/shard_map/ppermute | solution.py:26
  38.6 0.6 shard_map.52
  39.2 1.9 %collective-permute-start.4 = (f32[64,512]{1,0:T(8,128)S(1)}, f32[64,512]{1,0:T(8,128)S(1)}, u32[]{:S(2)}, u32[]{:S(2)}) collective-permute-start(f32[64,512]{1,0:T(8,128)S(1)} %get-tuple-element.52.refs_2_), channel_id=1, source_target_pairs={{0,6},{1,7},{2,4},{3,5},{4,2},{5,3},{6,0},{7,1},{8,14},{9,15},{10,... | collective-permute-start | bytes 393224 | tf_op jit(solution)/shard_map/ppermute | solution.py:26
  41.1 0.0 collective-permute-done.5.refs_3_.refs_1_
  41.2 1.9 %collective-permute-start.7 = (f32[64,512]{1,0:T(8,128)S(1)}, f32[64,512]{1,0:T(8,128)S(1)}, u32[]{:S(2)}, u32[]{:S(2)}) collective-permute-start(f32[64,512]{1,0:T(8,128)S(1)} %shard_map.55.refs_0_), channel_id=1, source_target_pairs={{0,8},{1,9},{2,10},{3,11},{4,12},{5,13},{6,14},{7,15},{8,0},{9,1},... | collective-permute-start | bytes 393224 | tf_op jit(solution)/shard_map/ppermute | solution.py:26
  43.1 3.0 %collective-permute-done.4.refs_1_ = f32[64,512]{1,0:T(8,128)S(1)} collective-permute-done((f32[64,512]{1,0:T(8,128)S(1)}, f32[64,512]{1,0:T(8,128)S(1)}, u32[]{:S(2)}, u32[]{:S(2)}) %collective-permute-start.4) | collective-permute-done | bytes 131104 | tf_op jit(solution)/shard_map/ppermute | solution.py:26
  46.1 0.5 shard_map.54
  46.6 1.9 %collective-permute-start.6 = (f32[64,384]{1,0:T(8,128)S(1)}, f32[64,384]{1,0:T(8,128)S(1)}, u32[]{:S(2)}, u32[]{:S(2)}) collective-permute-start(f32[64,384]{1,0:T(8,128)S(1)} %get-tuple-element.53.refs_2_.refs_0_.refs_1_), channel_id=1, source_target_pairs={{0,8},{1,9},{2,10},{3,11},{4,12},{5,13},{6,14},{7,15},{8,0},{9,1},... | collective-permute-start | bytes 294920 | tf_op jit(solution)/shard_map/ppermute | solution.py:26
  48.5 0.0 collective-permute-done.7.refs_1_
  48.5 0.1 shard_map.56
  48.6 4.7 %collective-permute-start.8 = (f32[64,384]{1,0:T(8,128)S(1)}, f32[64,384]{1,0:T(8,128)S(1)}, u32[]{:S(2)}, u32[]{:S(2)}) collective-permute-start(f32[64,384]{1,0:T(8,128)S(1)} %get-tuple-element.54.refs_2_), channel_id=1, source_target_pairs={{0,1},{1,0},{2,3},{3,2},{4,5},{5,4},{6,7},{7,6},{8,9},{9,8},{10,11... | collective-permute-start | bytes 294920 | tf_op jit(solution)/shard_map/ppermute | solution.py:26
  53.3 1.9 %collective-permute-start.10 = (f32[160,128]{1,0:T(8,128)S(1)}, f32[160,128]{1,0:T(8,128)S(1)}, u32[]{:S(2)}, u32[]{:S(2)}) collective-permute-start(f32[160,128]{1,0:T(8,128)S(1)} %get-tuple-element.58), channel_id=1, source_target_pairs={{0,16},{1,17},{2,18},{3,19},{4,20},{5,21},{6,22},{7,23},{8,24},{9,... | collective-permute-start | bytes 245768 | tf_op jit(solution)/shard_map/ppermute | solution.py:26
  55.2 0.0 collective-permute-done.6.refs_1_
  55.3 0.0 collective-permute-done.8.refs_3_
  55.3 0.5 shard_map.57
  55.8 6.1 %collective-permute-done.10.refs_1_ = f32[160,128]{1,0:T(8,128)S(1)} collective-permute-done((f32[160,128]{1,0:T(8,128)S(1)}, f32[160,128]{1,0:T(8,128)S(1)}, u32[]{:S(2)}, u32[]{:S(2)}) %collective-permute-start.10) | collective-permute-done | bytes 81952 | tf_op jit(solution)/shard_map/ppermute | solution.py:26
  61.9 0.1 shard_map.58
  62.1 2.7 %collective-permute-start.11 = (f32[160,128]{1,0:T(8,128)S(1)}, f32[160,128]{1,0:T(8,128)S(1)}, u32[]{:S(2)}, u32[]{:S(2)}) collective-permute-start(f32[160,128]{1,0:T(8,128)S(1)} %get-tuple-element.59.refs_2_), channel_id=1, source_target_pairs={{0,1},{1,0},{2,3},{3,2},{4,5},{5,4},{6,7},{7,6},{8,9},{9,8},{10,11... | collective-permute-start | bytes 245768 | tf_op jit(solution)/shard_map/ppermute | solution.py:26
  64.8 1.9 %collective-permute-start.9 = (f32[160,128]{1,0:T(8,128)S(1)}, f32[160,128]{1,0:T(8,128)S(1)}, u32[]{:S(2)}, u32[]{:S(2)}) collective-permute-start(f32[160,128]{1,0:T(8,128)S(1)} %get-tuple-element.56), channel_id=1, source_target_pairs={{0,16},{1,17},{2,18},{3,19},{4,20},{5,21},{6,22},{7,23},{8,24},{9,... | collective-permute-start | bytes 245768 | tf_op jit(solution)/shard_map/ppermute | solution.py:26
  66.7 6.7 %collective-permute-start.13 = (f32[96,128]{1,0:T(8,128)S(1)}, f32[96,128]{1,0:T(8,128)S(1)}, u32[]{:S(2)}, u32[]{:S(2)}) collective-permute-start(f32[96,128]{1,0:T(8,128)S(1)} %get-tuple-element.63), channel_id=1, source_target_pairs={{0,32},{1,33},{2,34},{3,35},{4,36},{5,37},{6,38},{7,39},{8,40},{9,... | collective-permute-start | bytes 147464 | tf_op jit(solution)/shard_map/ppermute | solution.py:26
  73.4 0.4 shard_map.59
  73.8 0.0 collective-permute-done.11.refs_3_
  73.8 0.0 collective-permute-done.9.refs_1_
  73.8 0.4 shard_map.60
  74.2 1.6 %collective-permute-done.13.refs_1_ = f32[96,128]{1,0:T(8,128)S(1)} collective-permute-done((f32[96,128]{1,0:T(8,128)S(1)}, f32[96,128]{1,0:T(8,128)S(1)}, u32[]{:S(2)}, u32[]{:S(2)}) %collective-permute-start.13) | collective-permute-done | bytes 49184 | tf_op jit(solution)/shard_map/ppermute | solution.py:26
  75.9 0.1 shard_map.61.refs_4_
  76.0 2.7 %collective-permute-start.14 = (f32[64,256]{1,0:T(8,128)S(1)}, f32[64,256]{1,0:T(8,128)S(1)}, u32[]{:S(2)}, u32[]{:S(2)}) collective-permute-start(f32[64,256]{1,0:T(8,128)S(1)} %shard_map.61.refs_4_), channel_id=1, source_target_pairs={{0,1},{1,0},{2,3},{3,2},{4,5},{5,4},{6,7},{7,6},{8,9},{9,8},{10,11... | collective-permute-start | bytes 196616 | tf_op jit(solution)/shard_map/ppermute | solution.py:26
  78.7 7.0 %collective-permute-start.12 = (f32[64,256]{1,0:T(8,128)S(1)}, f32[64,256]{1,0:T(8,128)S(1)}, u32[]{:S(2)}, u32[]{:S(2)}) collective-permute-start(f32[64,256]{1,0:T(8,128)S(1)} %get-tuple-element.61.refs_2_.refs_0_), channel_id=1, source_target_pairs={{0,32},{1,33},{2,34},{3,35},{4,36},{5,37},{6,38},{7,39},{8,40},{9,... | collective-permute-start | bytes 196616 | tf_op jit(solution)/shard_map/ppermute | solution.py:26
  85.7 0.0 collective-permute-done.14.refs_5_
  85.7 2.5 %collective-permute-done.12.refs_1_ = f32[64,256]{1,0:T(8,128)S(1)} collective-permute-done((f32[64,256]{1,0:T(8,128)S(1)}, f32[64,256]{1,0:T(8,128)S(1)}, u32[]{:S(2)}, u32[]{:S(2)}) %collective-permute-start.12) | collective-permute-done | bytes 65568 | tf_op jit(solution)/shard_map/ppermute | solution.py:26
  88.2 0.4 shard_map.62
  88.6 8.6 %collective-permute-start.16 = (f32[64,384]{1,0:T(8,128)S(1)}, f32[64,384]{1,0:T(8,128)S(1)}, u32[]{:S(2)}, u32[]{:S(2)}) collective-permute-start(f32[64,384]{1,0:T(8,128)S(1)} %get-tuple-element.66.refs_0_), channel_id=1, source_target_pairs={{0,96},{1,97},{2,98},{3,99},{4,100},{5,101},{6,102},{7,103},{8,104... | collective-permute-start | bytes 294920 | tf_op jit(solution)/shard_map/ppermute | solution.py:26
  97.2 3.0 %collective-permute-start.15 = (f32[128,128]{1,0:T(8,128)S(1)}, f32[128,128]{1,0:T(8,128)S(1)}, u32[]{:S(2)}, u32[]{:S(2)}) collective-permute-start(f32[128,128]{1,0:T(8,128)S(1)} %get-tuple-element.65), channel_id=1, source_target_pairs={{0,1},{1,0},{2,3},{3,2},{4,5},{5,4},{6,7},{7,6},{8,9},{9,8},{10,11... | collective-permute-start | bytes 196616 | tf_op jit(solution)/shard_map/ppermute | solution.py:26
  100.2 0.9 collective-permute-done.15.refs_3_.got_ref
  101.1 0.0 collective-permute-done.16.refs_1_
  101.1 0.4 shard_map.63
  101.5 3.1 %collective-permute-start.17 = (f32[96,128]{1,0:T(8,128)S(1)}, f32[96,128]{1,0:T(8,128)S(1)}, u32[]{:S(2)}, u32[]{:S(2)}) collective-permute-start(f32[96,128]{1,0:T(8,128)S(1)} %get-tuple-element.67.refs_0_), channel_id=1, source_target_pairs={{0,128},{1,129},{2,130},{3,131},{4,132},{5,133},{6,134},{7,135},{8... | collective-permute-start | bytes 147464 | tf_op jit(solution)/shard_map/ppermute | solution.py:26
  104.6 1.7 %collective-permute-done.17.refs_1_ = f32[96,128]{1,0:T(8,128)S(1)} collective-permute-done((f32[96,128]{1,0:T(8,128)S(1)}, f32[96,128]{1,0:T(8,128)S(1)}, u32[]{:S(2)}, u32[]{:S(2)}) %collective-permute-start.17) | collective-permute-done | bytes 49184 | tf_op jit(solution)/shard_map/ppermute | solution.py:26
  106.3 0.4 shard_map.64
  106.7 4.4 %collective-permute-start.18 = (f32[32,128]{1,0:T(8,128)S(1)}, f32[32,128]{1,0:T(8,128)S(1)}, u32[]{:S(2)}, u32[]{:S(2)}) collective-permute-start(f32[32,128]{1,0:T(8,128)S(1)} %get-tuple-element.68.refs_0_), channel_id=1, source_target_pairs={{0,384},{1,385},{2,386},{3,387},{4,388},{5,389},{6,390},{7,391},{8... | collective-permute-start | bytes 49160 | tf_op jit(solution)/shard_map/ppermute | solution.py:26
  111.2 1.3 collective-permute-done.18.refs_1_
  112.4 1.0 shard_map.65
  113.5 0.0 all-gather.3.cloned.1.call-update
  113.5 38.4 %all-gather.3.cloned.1.call-done = f32[512,768]{1,0:T(8,128)} async-done(((f32[64,768]{1,0:T(8,128)}), f32[512,768]{1,0:T(8,128)}) %all-gather.3.cloned.1.call-update) | async-done | bytes 1572880 | tf_op jit(solution)/shard_map/all_gather | solution.py:427
  151.9 1.4 copy-done.2
  153.3 2.7 %shard_map.66 = f32[512,512]{1,0:T(8,128)} custom-call(f32[512,256]{1,0:T(8,128)S(1)} %get-tuple-element.43.theirs_ref, f32[512,256]{1,0:T(8,128)S(1)} %get-tuple-element.47.mine_ref, f32[128,128]{1,0:T(8,128)S(1)} %collective-permute-done.15.refs_3_.got_ref, f32[256,128]{1,0:T(8,128)S(1)} %get-tuple-element.64.refs_7_.both0_ref, f32[8,64,768]{2,1,0:T(8,128)S(1)} %bitcast.3, ...), custom_call_target="tpu_custom_call" | custom-call | flops 900000000 | bytes 1048576 | tf_op jit(solution)/shard_map/pallas_call | solution.py:337
  (8 shorter events, 0.1 us)
Async XLA Ops:
  6.5 11.1 %copy-start = (f32[512,512]{1,0:T(8,128)S(1)}, f32[512,512]{1,0:T(8,128)}, u32[]{:S(2)}) copy-start(f32[512,512]{1,0:T(8,128)} %refs_0_.3) | copy-start | bytes 3145732
  6.5 11.1 %copy-start.1 = (f32[512,512]{1,0:T(8,128)S(1)}, f32[512,512]{1,0:T(8,128)}, u32[]{:S(2)}) copy-start(f32[512,512]{1,0:T(8,128)} %refs_1_.3) | copy-start | bytes 3145732
  6.5 145.4 %all-gather.3.cloned.1.call-start = ((), (), s32[]{:S(2)}) async-start(), calls=%async_computation | async-start | bytes 1769472 | tf_op jit(solution)/shard_map/all_gather | solution.py:427
  6.5 1.4 copy-start.3
  8.8 13.1 %collective-permute-start = (f32[256,512]{1,0:T(8,128)S(1)}, f32[256,512]{1,0:T(8,128)S(1)}, u32[]{:S(2)}, u32[]{:S(2)}) collective-permute-start(f32[256,512]{1,0:T(8,128)S(1)} %get-tuple-element.45), channel_id=1, source_target_pairs={{0,1},{1,0},{2,3},{3,2},{4,5},{5,4},{6,7},{7,6},{8,9},{9,8},{10,11... | collective-permute-start | bytes 1572872 | tf_op jit(solution)/shard_map/ppermute | solution.py:26
  19.8 4.1 %copy-start.4 = (f32[1,9,128,128]{3,2,1,0:T(8,128)S(1)}, f32[1,9,128,128]{3,2,1,0:T(8,128)}, u32[]{:S(2)}) copy-start(f32[1,9,128,128]{3,2,1,0:T(8,128)} %param.7) | copy-start | bytes 1769476
  19.8 6.5 %collective-permute-start.1 = (f32[256,640]{1,0:T(8,128)S(1)}, f32[256,640]{1,0:T(8,128)S(1)}, u32[]{:S(2)}, u32[]{:S(2)}) collective-permute-start(f32[256,640]{1,0:T(8,128)S(1)} %get-tuple-element.46.refs_2_), channel_id=1, source_target_pairs={{0,1},{1,0},{2,3},{3,2},{4,5},{5,4},{6,7},{7,6},{8,9},{9,8},{10,11... | collective-permute-start | bytes 1966088 | tf_op jit(solution)/shard_map/ppermute | solution.py:26
  22.0 11.0 %collective-permute-start.3 = (f32[672,128]{1,0:T(8,128)S(1)}, f32[672,128]{1,0:T(8,128)S(1)}, u32[]{:S(2)}, u32[]{:S(2)}) collective-permute-start(f32[672,128]{1,0:T(8,128)S(1)} %shard_map.48.refs_4_.refs_2_.refs_0_), channel_id=1, source_target_pairs={{0,2},{1,3},{2,0},{3,1},{4,6},{5,7},{6,4},{7,5},{8,10},{9,11},{10,... | collective-permute-start | bytes 1032200 | tf_op jit(solution)/shard_map/ppermute | solution.py:26
  27.0 11.7 %collective-permute-start.2 = (f32[128,512]{1,0:T(8,128)S(1)}, f32[128,512]{1,0:T(8,128)S(1)}, u32[]{:S(2)}, u32[]{:S(2)}) collective-permute-start(f32[128,512]{1,0:T(8,128)S(1)} %get-tuple-element.50.refs_2_), channel_id=1, source_target_pairs={{0,2},{1,3},{2,0},{3,1},{4,6},{5,7},{6,4},{7,5},{8,10},{9,11},{10,... | collective-permute-start | bytes 786440 | tf_op jit(solution)/shard_map/ppermute | solution.py:26
  33.0 8.1 %collective-permute-start.5 = (f32[64,896]{1,0:T(8,128)S(1)}, f32[64,896]{1,0:T(8,128)S(1)}, u32[]{:S(2)}, u32[]{:S(2)}) collective-permute-start(f32[64,896]{1,0:T(8,128)S(1)} %shard_map.53.refs_2_.refs_0_), channel_id=1, source_target_pairs={{0,6},{1,7},{2,4},{3,5},{4,2},{5,3},{6,0},{7,1},{8,14},{9,15},{10,... | collective-permute-start | bytes 688136 | tf_op jit(solution)/shard_map/ppermute | solution.py:26
  39.2 6.9 %collective-permute-start.4 = (f32[64,512]{1,0:T(8,128)S(1)}, f32[64,512]{1,0:T(8,128)S(1)}, u32[]{:S(2)}, u32[]{:S(2)}) collective-permute-start(f32[64,512]{1,0:T(8,128)S(1)} %get-tuple-element.52.refs_2_), channel_id=1, source_target_pairs={{0,6},{1,7},{2,4},{3,5},{4,2},{5,3},{6,0},{7,1},{8,14},{9,15},{10,... | collective-permute-start | bytes 393224 | tf_op jit(solution)/shard_map/ppermute | solution.py:26
  41.2 7.4 %collective-permute-start.7 = (f32[64,512]{1,0:T(8,128)S(1)}, f32[64,512]{1,0:T(8,128)S(1)}, u32[]{:S(2)}, u32[]{:S(2)}) collective-permute-start(f32[64,512]{1,0:T(8,128)S(1)} %shard_map.55.refs_0_), channel_id=1, source_target_pairs={{0,8},{1,9},{2,10},{3,11},{4,12},{5,13},{6,14},{7,15},{8,0},{9,1},... | collective-permute-start | bytes 393224 | tf_op jit(solution)/shard_map/ppermute | solution.py:26
  46.6 8.7 %collective-permute-start.6 = (f32[64,384]{1,0:T(8,128)S(1)}, f32[64,384]{1,0:T(8,128)S(1)}, u32[]{:S(2)}, u32[]{:S(2)}) collective-permute-start(f32[64,384]{1,0:T(8,128)S(1)} %get-tuple-element.53.refs_2_.refs_0_.refs_1_), channel_id=1, source_target_pairs={{0,8},{1,9},{2,10},{3,11},{4,12},{5,13},{6,14},{7,15},{8,0},{9,1},... | collective-permute-start | bytes 294920 | tf_op jit(solution)/shard_map/ppermute | solution.py:26
  48.6 6.6 %collective-permute-start.8 = (f32[64,384]{1,0:T(8,128)S(1)}, f32[64,384]{1,0:T(8,128)S(1)}, u32[]{:S(2)}, u32[]{:S(2)}) collective-permute-start(f32[64,384]{1,0:T(8,128)S(1)} %get-tuple-element.54.refs_2_), channel_id=1, source_target_pairs={{0,1},{1,0},{2,3},{3,2},{4,5},{5,4},{6,7},{7,6},{8,9},{9,8},{10,11... | collective-permute-start | bytes 294920 | tf_op jit(solution)/shard_map/ppermute | solution.py:26
  53.3 8.6 %collective-permute-start.10 = (f32[160,128]{1,0:T(8,128)S(1)}, f32[160,128]{1,0:T(8,128)S(1)}, u32[]{:S(2)}, u32[]{:S(2)}) collective-permute-start(f32[160,128]{1,0:T(8,128)S(1)} %get-tuple-element.58), channel_id=1, source_target_pairs={{0,16},{1,17},{2,18},{3,19},{4,20},{5,21},{6,22},{7,23},{8,24},{9,... | collective-permute-start | bytes 245768 | tf_op jit(solution)/shard_map/ppermute | solution.py:26
  62.1 11.7 %collective-permute-start.11 = (f32[160,128]{1,0:T(8,128)S(1)}, f32[160,128]{1,0:T(8,128)S(1)}, u32[]{:S(2)}, u32[]{:S(2)}) collective-permute-start(f32[160,128]{1,0:T(8,128)S(1)} %get-tuple-element.59.refs_2_), channel_id=1, source_target_pairs={{0,1},{1,0},{2,3},{3,2},{4,5},{5,4},{6,7},{7,6},{8,9},{9,8},{10,11... | collective-permute-start | bytes 245768 | tf_op jit(solution)/shard_map/ppermute | solution.py:26
  64.8 9.0 %collective-permute-start.9 = (f32[160,128]{1,0:T(8,128)S(1)}, f32[160,128]{1,0:T(8,128)S(1)}, u32[]{:S(2)}, u32[]{:S(2)}) collective-permute-start(f32[160,128]{1,0:T(8,128)S(1)} %get-tuple-element.56), channel_id=1, source_target_pairs={{0,16},{1,17},{2,18},{3,19},{4,20},{5,21},{6,22},{7,23},{8,24},{9,... | collective-permute-start | bytes 245768 | tf_op jit(solution)/shard_map/ppermute | solution.py:26
  66.7 9.2 %collective-permute-start.13 = (f32[96,128]{1,0:T(8,128)S(1)}, f32[96,128]{1,0:T(8,128)S(1)}, u32[]{:S(2)}, u32[]{:S(2)}) collective-permute-start(f32[96,128]{1,0:T(8,128)S(1)} %get-tuple-element.63), channel_id=1, source_target_pairs={{0,32},{1,33},{2,34},{3,35},{4,36},{5,37},{6,38},{7,39},{8,40},{9,... | collective-permute-start | bytes 147464 | tf_op jit(solution)/shard_map/ppermute | solution.py:26
  76.0 9.7 %collective-permute-start.14 = (f32[64,256]{1,0:T(8,128)S(1)}, f32[64,256]{1,0:T(8,128)S(1)}, u32[]{:S(2)}, u32[]{:S(2)}) collective-permute-start(f32[64,256]{1,0:T(8,128)S(1)} %shard_map.61.refs_4_), channel_id=1, source_target_pairs={{0,1},{1,0},{2,3},{3,2},{4,5},{5,4},{6,7},{7,6},{8,9},{9,8},{10,11... | collective-permute-start | bytes 196616 | tf_op jit(solution)/shard_map/ppermute | solution.py:26
  78.7 9.5 %collective-permute-start.12 = (f32[64,256]{1,0:T(8,128)S(1)}, f32[64,256]{1,0:T(8,128)S(1)}, u32[]{:S(2)}, u32[]{:S(2)}) collective-permute-start(f32[64,256]{1,0:T(8,128)S(1)} %get-tuple-element.61.refs_2_.refs_0_), channel_id=1, source_target_pairs={{0,32},{1,33},{2,34},{3,35},{4,36},{5,37},{6,38},{7,39},{8,40},{9,... | collective-permute-start | bytes 196616 | tf_op jit(solution)/shard_map/ppermute | solution.py:26
  88.6 12.5 %collective-permute-start.16 = (f32[64,384]{1,0:T(8,128)S(1)}, f32[64,384]{1,0:T(8,128)S(1)}, u32[]{:S(2)}, u32[]{:S(2)}) collective-permute-start(f32[64,384]{1,0:T(8,128)S(1)} %get-tuple-element.66.refs_0_), channel_id=1, source_target_pairs={{0,96},{1,97},{2,98},{3,99},{4,100},{5,101},{6,102},{7,103},{8,104... | collective-permute-start | bytes 294920 | tf_op jit(solution)/shard_map/ppermute | solution.py:26
  97.2 3.9 %collective-permute-start.15 = (f32[128,128]{1,0:T(8,128)S(1)}, f32[128,128]{1,0:T(8,128)S(1)}, u32[]{:S(2)}, u32[]{:S(2)}) collective-permute-start(f32[128,128]{1,0:T(8,128)S(1)} %get-tuple-element.65), channel_id=1, source_target_pairs={{0,1},{1,0},{2,3},{3,2},{4,5},{5,4},{6,7},{7,6},{8,9},{9,8},{10,11... | collective-permute-start | bytes 196616 | tf_op jit(solution)/shard_map/ppermute | solution.py:26
  101.5 4.9 %collective-permute-start.17 = (f32[96,128]{1,0:T(8,128)S(1)}, f32[96,128]{1,0:T(8,128)S(1)}, u32[]{:S(2)}, u32[]{:S(2)}) collective-permute-start(f32[96,128]{1,0:T(8,128)S(1)} %get-tuple-element.67.refs_0_), channel_id=1, source_target_pairs={{0,128},{1,129},{2,130},{3,131},{4,132},{5,133},{6,134},{7,135},{8... | collective-permute-start | bytes 147464 | tf_op jit(solution)/shard_map/ppermute | solution.py:26
  106.7 5.7 %collective-permute-start.18 = (f32[32,128]{1,0:T(8,128)S(1)}, f32[32,128]{1,0:T(8,128)S(1)}, u32[]{:S(2)}, u32[]{:S(2)}) collective-permute-start(f32[32,128]{1,0:T(8,128)S(1)} %get-tuple-element.68.refs_0_), channel_id=1, source_target_pairs={{0,384},{1,385},{2,386},{3,387},{4,388},{5,389},{6,390},{7,391},{8... | collective-permute-start | bytes 49160 | tf_op jit(solution)/shard_map/ppermute | solution.py:26
  151.9 1.4 copy-start.2
Sparse Core Ops, SparseCore 0:
  113.6 38.2 all-gather.2
